TPU v7x, 512 devices: a whole 4x8x8 slice. The times are simulated.
512 devices in a mesh: blk: 32 (over z_hi, x, core), lane: 16 (over z_lo, y).
Axes of the slice: x: 4, y: 8, z: 8 (z_hi: 4, z_lo: 2; z = z_hi * 2 + z_lo), core: 2. Of those that a mesh axis runs over, the one named last changes fastest.
Arguments:
- image_feat: bfloat16 [196608, 768], P(('blk', 'lane')), may hold values from -1 to 1
- text_emb: bfloat16 [196608, 768], P(('blk', 'lane')), may hold values from -1 to 1
- head_weight: bfloat16 [768, 768], replicated, may hold values from -0.21875 to 0.21875
- lang_ids: int32 [196608], P(('blk', 'lane')), may hold values from 0 to 108, never falling along the last dimension, each value on 1 to 7214 neighbouring positions
- pair_mask: int32 [109, 109], replicated, may hold values 0 or 1
- weight_codes: int32 [109], replicated, may hold values from 1 to 4
- log_scale: float32 [], replicated, may hold values from 0.693 to 2.079
- logit_bias: float32 [], replicated, may hold values from -3 to -1
Outputs:
- image_back: bfloat16 [196608, 768], P(('blk', 'lane'))
- text_back: bfloat16 [196608, 768], P(('blk', 'lane'))
- head_grad: float32 [768, 768], P('lane', 'blk')
Inputs may be any that keep to these rules, and one draw needn't show every extreme that they name: lang_ids never decreases along the rows.
All inputs are finite; a program needn't handle non-finite values.
Results may differ from a plain program's by a relative error of at most 0.022.
Values may be sent and summed in bfloat16 or wider, within the bound.
No kernel may reach another device: no remote copies, remote signals or barrier semaphores. Data moves between devices by JAX's collectives and lax.ppermute only.
A program may use at most 64 MiB of HBM per device.

v0:
```python
import jax
import jax.numpy as jnp
from jax import lax
from jax.sharding import PartitionSpec as P

STEPS = 4


EPSILON = 1e-06


def from_behind(value, axis, steps):
    count = lax.axis_size(axis)
    pairs = [(source, (source + steps) % count) for source in range(count)]
    return lax.ppermute(value, axis, pairs)


def unit_rows(vectors):
    inverse = lax.rsqrt(jnp.sum(vectors * vectors, axis=-1, keepdims=True) + EPSILON)
    return (vectors * inverse, inverse)


def language_table(lang_values, lang_count):
    labels = jnp.arange(lang_count, dtype=jnp.float32)
    return (lang_values.astype(jnp.float32)[:, None] == labels[None, :]).astype(jnp.float32)


def image_side(lang_values, allowed, code_vals):
    image_hot = language_table(lang_values, code_vals.shape[0])
    row_codes = jnp.sum(image_hot * code_vals[None, :], axis=1)
    allow_rows = jnp.dot(
        image_hot.astype(jnp.bfloat16), allowed, preferred_element_type=jnp.float32
    ).astype(jnp.bfloat16)
    return (allow_rows, row_codes)


def pair_terms(
    image_low,
    allow_rows,
    row_codes,
    text_low,
    text_langs,
    code_vals,
    logit_scale,
    logit_bias,
    positive,
):
    lang_count = code_vals.shape[0]
    row_count = image_low.shape[0]
    text_hot = language_table(text_langs, lang_count)
    text_codes = jnp.sum(text_hot * code_vals[None, :], axis=1)
    keep_mask = jnp.einsum(
        "il,jl->ij", allow_rows, text_hot.astype(jnp.bfloat16), preferred_element_type=jnp.float32
    )
    pair_weight = keep_mask * (0.25 * (row_codes[:, None] + text_codes[None, :]))
    cosine = jnp.einsum("id,jd->ij", image_low, text_low, preferred_element_type=jnp.float32)
    excess = jax.nn.sigmoid(logit_scale * cosine + logit_bias)
    if positive:
        excess = excess - jnp.eye(row_count, dtype=jnp.float32)
    pair_grad = (pair_weight * excess).astype(jnp.bfloat16)
    image_term = logit_scale * jnp.dot(pair_grad, text_low, preferred_element_type=jnp.float32)
    text_term = logit_scale * jnp.einsum(
        "ij,id->jd", pair_grad, image_low, preferred_element_type=jnp.float32
    )
    return (image_term, text_term)


def on_device(
    image_feat, text_emb, head_weight, lang_ids, pair_mask, weight_codes, log_scale, logit_bias
):
    lang_count = pair_mask.shape[0]
    logit_scale = jnp.exp(log_scale)
    allowed = jnp.maximum(pair_mask, jnp.eye(lang_count, dtype=jnp.int32)).astype(jnp.bfloat16)
    code_vals = weight_codes.astype(jnp.float32)
    projected = jnp.dot(image_feat, head_weight, preferred_element_type=jnp.float32)
    image_unit, image_inv = unit_rows(projected)
    text_unit, text_inv = unit_rows(text_emb.astype(jnp.float32))
    image_low = image_unit.astype(jnp.bfloat16)
    text_low = text_unit.astype(jnp.bfloat16)
    own_langs = lang_ids.astype(jnp.bfloat16)
    allow_rows, row_codes = image_side(lang_ids, allowed, code_vals)
    image_grad = jnp.zeros(projected.shape, jnp.float32)
    visitor = (text_low, own_langs)
    carried = jnp.zeros(projected.shape, jnp.float32)
    for offset in range(STEPS):
        if offset > 0:
            visitor = from_behind((visitor[0], visitor[1]), "blk", 1)
            carried = from_behind(carried.astype(jnp.bfloat16), "blk", 1).astype(carried.dtype)
        image_term, text_term = pair_terms(
            image_low,
            allow_rows,
            row_codes,
            visitor[0],
            visitor[1],
            code_vals,
            logit_scale,
            logit_bias,
            offset == 0,
        )
        image_grad = image_grad + image_term
        carried = text_term if offset == 0 else carried + text_term
    text_grad = from_behind(carried.astype(jnp.bfloat16), "blk", -(STEPS - 1)).astype(carried.dtype)
    radial = jnp.sum(image_unit * image_grad, axis=-1, keepdims=True)
    image_dir = ((image_grad - image_unit * radial) * image_inv).astype(jnp.bfloat16)
    image_back = jnp.einsum(
        "re,de->rd", image_dir, head_weight, preferred_element_type=jnp.float32
    ).astype(jnp.bfloat16)
    text_radial = jnp.sum(text_unit * text_grad, axis=-1, keepdims=True)
    text_back = ((text_grad - text_unit * text_radial) * text_inv).astype(jnp.bfloat16)
    head_term = jnp.einsum("rd,re->de", image_feat, image_dir, preferred_element_type=jnp.float32)
    block_sums = lax.psum_scatter(
        head_term.astype(jnp.bfloat16), "blk", scatter_dimension=1, tiled=True
    )
    head_grad = lax.psum_scatter(block_sums, "lane", scatter_dimension=0, tiled=True).astype(
        jnp.float32
    )
    return (image_back, text_back, head_grad)


def solution(mesh):
    in_specs = (
        P(("blk", "lane"), None),
        P(("blk", "lane"), None),
        P(),
        P(("blk", "lane")),
        P(),
        P(),
        P(),
        P(),
    )
    out_specs = (P(("blk", "lane"), None), P(("blk", "lane"), None), P("lane", "blk"))
    return jax.shard_map(
        on_device, mesh=mesh, in_specs=in_specs, out_specs=out_specs, check_vma=False
    )
```

profile of v0, /device:TPU:6, one launch (start us, length us, event | category | flops | bytes accessed | tf_op | source)
XLA Modules:
  0.0 288.8 jit_solution(16521871866539902279)
XLA Ops:
  7.2 1.4 fusion.43
  8.6 1.9 collective-permute-start
  10.5 1.3 fusion.34
  11.8 1.2 fusion.1
  13.0 6.1 %collective-permute-start.1 = (bf16[384,768]{1,0:T(8,128)(2,1)S(1)}, bf16[384,768]{1,0:T(8,128)(2,1)}, u32[]{:S(2)}, u32[]{:S(2)}) collective-permute-start(bf16[384,768]{1,0:T(8,128)(2,1)S(1)} %fusion.1), channel_id=1, source_target_pairs={{0,16},{16,32},{32,48},{48,64},{64,80},{80,96},{96,112},{112,128},... | collective-permute-start | bytes 1769480 | tf_op jit(solution)/shard_map/ppermute | solution.py:15
  21.4 1.9 collective-permute-start.2
  23.9 2.6 collective-permute-done.2
  26.5 2.2 collective-permute-start.4
  29.7 1.7 collective-permute-done.4
  32.4 5.8 %collective-permute-start.6 = (bf16[384,768]{1,0:T(8,128)(2,1)S(1)}, bf16[384,768]{1,0:T(8,128)(2,1)S(1)}, u32[]{:S(2)}, u32[]{:S(2)}) collective-permute-start(bf16[384,768]{1,0:T(8,128)(2,1)S(1)} %fusion.4), channel_id=1, source_target_pairs={{0,16},{16,32},{32,48},{48,64},{64,80},{80,96},{96,112},{112,128},... | collective-permute-start | bytes 1769480 | tf_op jit(solution)/shard_map/ppermute | solution.py:15
  38.7 1.6 fusion.17
  40.3 7.1 %collective-permute-start.3 = (bf16[384,768]{1,0:T(8,128)(2,1)}, bf16[384,768]{1,0:T(8,128)(2,1)S(1)}, u32[]{:S(2)}, u32[]{:S(2)}) collective-permute-start(bf16[384,768]{1,0:T(8,128)(2,1)} %collective-permute-done.1), channel_id=1, source_target_pairs={{0,16},{16,32},{32,48},{48,64},{64,80},{80,96},{96,112},{112,128},... | collective-permute-start | bytes 1769480 | tf_op jit(solution)/shard_map/ppermute | solution.py:15
  47.6 1.5 convolution_add_fusion.2
  49.2 1.3 add_convert_fusion.2
  50.5 2.9 collective-permute-start.7
  53.9 7.5 %collective-permute-start.5 = (bf16[384,768]{1,0:T(8,128)(2,1)S(1)}, bf16[384,768]{1,0:T(8,128)(2,1)S(1)}, u32[]{:S(2)}, u32[]{:S(2)}) collective-permute-start(bf16[384,768]{1,0:T(8,128)(2,1)S(1)} %collective-permute-done.3), channel_id=1, source_target_pairs={{0,16},{16,32},{32,48},{48,64},{64,80},{80,96},{96,112},{112,128},... | collective-permute-start | bytes 1769480 | tf_op jit(solution)/shard_map/ppermute | solution.py:15
  61.7 1.6 convolution_multiply_fusion.1
  63.7 4.5 %collective-permute-done.5 = bf16[384,768]{1,0:T(8,128)(2,1)S(1)} collective-permute-done((bf16[384,768]{1,0:T(8,128)(2,1)S(1)}, bf16[384,768]{1,0:T(8,128)(2,1)S(1)}, u32[]{:S(2)}, u32[]{:S(2)}) %collective-permute-start.5) | collective-permute-done | bytes 589856 | tf_op jit(solution)/shard_map/ppermute | solution.py:15
  69.9 0.8 copy-done.5
  70.7 1.8 fusion.3
  72.6 1.2 copy-done.2
  73.8 1.2 add_convert_fusion.1
  75.0 20.2 %collective-permute-start.8 = (bf16[384,768]{1,0:T(8,128)(2,1)S(1)}, bf16[384,768]{1,0:T(8,128)(2,1)S(1)}, u32[]{:S(2)}, u32[]{:S(2)}) collective-permute-start(bf16[384,768]{1,0:T(8,128)(2,1)S(1)} %add_convert_fusion.1), channel_id=1, source_target_pairs={{0,16},{16,32},{32,48},{48,64},{64,80},{80,96},{96,112},{112,128},... | collective-permute-start | bytes 1769480 | tf_op jit(solution)/shard_map/ppermute | solution.py:15
  95.8 1.1 collective-permute-done.8
  97.0 2.1 collective-permute-start.9
  99.1 1.5 convolution_convert_fusion.1
  100.6 11.4 %collective-permute-done.9 = bf16[384,768]{1,0:T(8,128)(2,1)S(1)} collective-permute-done((bf16[384,768]{1,0:T(8,128)(2,1)S(1)}, bf16[384,768]{1,0:T(8,128)(2,1)S(1)}, u32[]{:S(2)}, u32[]{:S(2)}) %collective-permute-start.9) | collective-permute-done | bytes 589856 | tf_op jit(solution)/shard_map/ppermute | solution.py:15
  112.4 95.3 %reduce-scatter.5.cloned.1.call-done = bf16[768,24]{0,1:T(8,128)(2,1)} async-done(((bf16[768,768]{0,1:T(8,128)(2,1)}), bf16[768,24]{0,1:T(8,128)(2,1)}) %reduce-scatter.5.cloned.1.call-update) | async-done | bytes 36880 | tf_op jit(solution)/shard_map/reduce_scatter | solution.py:111
  207.7 1.6 copy.11
  209.3 1.1 fusion.37
  210.4 70.1 %reduce-scatter.7.cloned.1.call-done = bf16[48,24]{1,0:T(8,128)(2,1)} async-done(((bf16[768,24]{1,0:T(8,128)(2,1)}), bf16[48,24]{1,0:T(8,128)(2,1)}) %reduce-scatter.7.cloned.1.call-update) | async-done | bytes 2320
  280.5 0.8 copy.12
  (51 shorter events, 8.7 us)
Async XLA Ops:
  7.2 12.0 %copy-start = (bf16[768,768]{1,0:T(8,128)(2,1)S(1)}, bf16[768,768]{1,0:T(8,128)(2,1)}, u32[]{:S(2)}) copy-start(bf16[768,768]{1,0:T(8,128)(2,1)} %param.10) | copy-start | bytes 3538948
  7.2 12.0 %copy-start.3 = (bf16[384,768]{1,0:T(8,128)(2,1)S(1)}, bf16[384,768]{1,0:T(8,128)(2,1)}, u32[]{:S(2)}) copy-start(bf16[384,768]{1,0:T(8,128)(2,1)} %param.8) | copy-start | bytes 1769476
  7.2 200.5 %reduce-scatter.5.cloned.1.call-start = ((), (), s32[]{:S(2)}) async-start(), calls=%async_computation.2 | async-start | bytes 1216512 | tf_op jit(solution)/shard_map/reduce_scatter | solution.py:111
  8.6 12.8 %collective-permute-start = (bf16[384]{0:T(512)(128)(2,1)}, bf16[384]{0:T(512)(128)(2,1)}, u32[]{:S(2)}, u32[]{:S(2)}) collective-permute-start(bf16[384]{0:T(512)(128)(2,1)} %get-tuple-element.9), channel_id=1, source_target_pairs={{0,16},{16,32},{32,48},{48,64},{64,80},{80,96},{96,112},{112,128},... | collective-permute-start | bytes 2312 | tf_op jit(solution)/shard_map/ppermute | solution.py:15
  13.0 25.6 %collective-permute-start.1 = (bf16[384,768]{1,0:T(8,128)(2,1)S(1)}, bf16[384,768]{1,0:T(8,128)(2,1)}, u32[]{:S(2)}, u32[]{:S(2)}) collective-permute-start(bf16[384,768]{1,0:T(8,128)(2,1)S(1)} %fusion.1), channel_id=1, source_target_pairs={{0,16},{16,32},{32,48},{48,64},{64,80},{80,96},{96,112},{112,128},... | collective-permute-start | bytes 1769480 | tf_op jit(solution)/shard_map/ppermute | solution.py:15
  21.4 7.4 %copy-start.7 = (s32[109,109]{1,0:T(8,128)S(1)}, s32[109,109]{1,0:T(8,128)}, u32[]{:S(2)}) copy-start(s32[109,109]{1,0:T(8,128)} %param.12) | copy-start | bytes 142576
  21.4 7.6 %copy-start.8 = (s32[109]{0:T(128)S(1)}, s32[109]{0:T(128)}, u32[]{:S(2)}) copy-start(s32[109]{0:T(128)} %param.13) | copy-start | bytes 1312
  21.4 5.1 %collective-permute-start.2 = (bf16[384]{0:T(512)(128)(2,1)}, bf16[384]{0:T(512)(128)(2,1)S(1)}, u32[]{:S(2)}, u32[]{:S(2)}) collective-permute-start(bf16[384]{0:T(512)(128)(2,1)} %collective-permute-done), channel_id=1, source_target_pairs={{0,16},{16,32},{32,48},{48,64},{64,80},{80,96},{96,112},{112,128},... | collective-permute-start | bytes 2312 | tf_op jit(solution)/shard_map/ppermute | solution.py:15
  26.5 4.9 %collective-permute-start.4 = (bf16[384]{0:T(512)(128)(2,1)S(1)}, bf16[384]{0:T(512)(128)(2,1)S(1)}, u32[]{:S(2)}, u32[]{:S(2)}) collective-permute-start(bf16[384]{0:T(512)(128)(2,1)S(1)} %collective-permute-done.2), channel_id=1, source_target_pairs={{0,16},{16,32},{32,48},{48,64},{64,80},{80,96},{96,112},{112,128},... | collective-permute-start | bytes 2312 | tf_op jit(solution)/shard_map/ppermute | solution.py:15
  32.4 16.8 %collective-permute-start.6 = (bf16[384,768]{1,0:T(8,128)(2,1)S(1)}, bf16[384,768]{1,0:T(8,128)(2,1)S(1)}, u32[]{:S(2)}, u32[]{:S(2)}) collective-permute-start(bf16[384,768]{1,0:T(8,128)(2,1)S(1)} %fusion.4), channel_id=1, source_target_pairs={{0,16},{16,32},{32,48},{48,64},{64,80},{80,96},{96,112},{112,128},... | collective-permute-start | bytes 1769480 | tf_op jit(solution)/shard_map/ppermute | solution.py:15
  40.3 13.1 %collective-permute-start.3 = (bf16[384,768]{1,0:T(8,128)(2,1)}, bf16[384,768]{1,0:T(8,128)(2,1)S(1)}, u32[]{:S(2)}, u32[]{:S(2)}) collective-permute-start(bf16[384,768]{1,0:T(8,128)(2,1)} %collective-permute-done.1), channel_id=1, source_target_pairs={{0,16},{16,32},{32,48},{48,64},{64,80},{80,96},{96,112},{112,128},... | collective-permute-start | bytes 1769480 | tf_op jit(solution)/shard_map/ppermute | solution.py:15
  50.5 22.1 %collective-permute-start.7 = (bf16[384,768]{1,0:T(8,128)(2,1)}, bf16[384,768]{1,0:T(8,128)(2,1)}, u32[]{:S(2)}, u32[]{:S(2)}) collective-permute-start(bf16[384,768]{1,0:T(8,128)(2,1)} %add_convert_fusion.2), channel_id=1, source_target_pairs={{0,16},{16,32},{32,48},{48,64},{64,80},{80,96},{96,112},{112,128},... | collective-permute-start | bytes 1769480 | tf_op jit(solution)/shard_map/ppermute | solution.py:15
  53.9 14.3 %collective-permute-start.5 = (bf16[384,768]{1,0:T(8,128)(2,1)S(1)}, bf16[384,768]{1,0:T(8,128)(2,1)S(1)}, u32[]{:S(2)}, u32[]{:S(2)}) collective-permute-start(bf16[384,768]{1,0:T(8,128)(2,1)S(1)} %collective-permute-done.3), channel_id=1, source_target_pairs={{0,16},{16,32},{32,48},{48,64},{64,80},{80,96},{96,112},{112,128},... | collective-permute-start | bytes 1769480 | tf_op jit(solution)/shard_map/ppermute | solution.py:15
  69.7 1.1 copy-start.4
  69.9 0.8 copy-start.5
  72.6 1.3 copy-start.2
  72.6 208.0 %reduce-scatter.7.cloned.1.call-start = ((), (), s32[]{:S(2)}) async-start(), calls=%async_computation.3 | async-start | bytes 208896
  75.0 21.9 %collective-permute-start.8 = (bf16[384,768]{1,0:T(8,128)(2,1)S(1)}, bf16[384,768]{1,0:T(8,128)(2,1)S(1)}, u32[]{:S(2)}, u32[]{:S(2)}) collective-permute-start(bf16[384,768]{1,0:T(8,128)(2,1)S(1)} %add_convert_fusion.1), channel_id=1, source_target_pairs={{0,16},{16,32},{32,48},{48,64},{64,80},{80,96},{96,112},{112,128},... | collective-permute-start | bytes 1769480 | tf_op jit(solution)/shard_map/ppermute | solution.py:15
  95.8 3.3 %copy-start.6 = (bf16[384,768]{1,0:T(8,128)(2,1)S(1)}, bf16[384,768]{1,0:T(8,128)(2,1)}, u32[]{:S(2)}) copy-start(bf16[384,768]{1,0:T(8,128)(2,1)} %copy-done.5) | copy-start | bytes 1769476
  97.0 15.0 %copy-start.1 = (bf16[384,768]{1,0:T(8,128)(2,1)S(1)}, bf16[384,768]{1,0:T(8,128)(2,1)}, u32[]{:S(2)}) copy-start(bf16[384,768]{1,0:T(8,128)(2,1)} %param.9) | copy-start | bytes 1769476
  97.0 15.0 %collective-permute-start.9 = (bf16[384,768]{1,0:T(8,128)(2,1)S(1)}, bf16[384,768]{1,0:T(8,128)(2,1)S(1)}, u32[]{:S(2)}, u32[]{:S(2)}) collective-permute-start(bf16[384,768]{1,0:T(8,128)(2,1)S(1)} %add_convert_fusion), channel_id=1, source_target_pairs={{0,464},{16,480},{32,496},{48,0},{64,16},{80,32},{96,48},{112,64},... | collective-permute-start | bytes 1769480 | tf_op jit(solution)/shard_map/ppermute | solution.py:15
Sparse Core Ops, SparseCore 0:
  72.7 134.9 reduce-scatter.4
  210.5 70.0 reduce-scatter.6
where the time goes:
time: 290 us; the launch traced here: 289 us
  waiting for transfers between devices  187 us (64%)
  starting transfers between devices  57.8 us (20%)
  between operations  15.7 us (5%)
  matrix products  15.5 us (5%)
  other arithmetic  8.56 us (3%)
  local copies, waits for them, and re-layouts  4.39 us (2%)
    reduce_scatter x1, waiting for transfers between devices, on_device(): lax.psum_scatter(head_term.astype(jnp.bfloat16), 'blk', scatter_dimension...  95.3 us
    unnamed x3, waiting for transfers between devices  70.2 us
    ppermute x10, starting transfers between devices, from_behind(): return lax.ppermute(value, axis, pairs)  57.7 us
    ppermute x10, waiting for transfers between devices, from_behind(): return lax.ppermute(value, axis, pairs)  21.4 us
  transfers between devices with their start and end apart: 12, of which 7 were waited for; matrix products, arithmetic and copies ran while one was open for 8% of the time, Pallas kernels for 0%

commit v1 on v0

v1 whole, which is shorter than its diff:
```python
import jax
import jax.numpy as jnp
from jax import lax
from jax.sharding import PartitionSpec as P

D = 768
ROWS = 384
N_BLK = 32
EPSILON = 1e-06


def device_index(z_hi, x, core, z_lo, y):
    return ((z_hi * 4 + x) * 2 + core) * 16 + z_lo * 8 + y


CORE_GROUPS = [
    [device_index(z, x, c, l, y) for c in range(2)]
    for z in range(4)
    for x in range(4)
    for l in range(2)
    for y in range(8)
]
NEAR_GROUPS = [
    [device_index(z, x, c, l, 2 * y_hi + y_lo) for x in range(4) for y_lo in range(2)]
    for z in range(4)
    for c in range(2)
    for l in range(2)
    for y_hi in range(4)
]
FAR_GROUPS = [
    [
        device_index(z, x, c, l, 2 * y_hi + y_lo)
        for z in range(4)
        for l in range(2)
        for y_hi in range(4)
    ]
    for x in range(4)
    for c in range(2)
    for y_lo in range(2)
]


def permute(value, target):
    return lax.ppermute(value, "blk", [(i, target(i) % N_BLK) for i in range(N_BLK)])


def swap_cores(value):
    return permute(value, lambda i: i ^ 1)


def exchange(value, groups):
    return lax.all_to_all(value, ("blk", "lane"), 0, 0, axis_index_groups=groups, tiled=True)


def unit_rows(vectors):
    inverse = lax.rsqrt(jnp.sum(vectors * vectors, axis=-1, keepdims=True) + EPSILON)
    return (vectors * inverse, inverse)


def dot(left, right, dims):
    return lax.dot_general(left, right, (dims, ((), ())), preferred_element_type=jnp.float32)


def column_order():
    new = jnp.arange(D, dtype=jnp.int32)
    core, x, z_hi, rest = new // 384, new // 96 % 4, new // 24 % 4, new % 24
    return z_hi * 192 + x * 48 + core * 24 + rest


def row_order():
    new = jnp.arange(D, dtype=jnp.int32)
    y_lo, z_lo, y_hi, rest = new // 384, new // 192 % 2, new // 48 % 4, new % 48
    return z_lo * 384 + (y_hi * 2 + y_lo) * 48 + rest


def order_matrix(old):
    return (jnp.arange(D, dtype=jnp.int32)[:, None] == old[None, :]).astype(jnp.bfloat16)


def on_device(
    image_feat, text_emb, head_weight, lang_ids, pair_mask, weight_codes, log_scale, logit_bias
):
    lang_count = pair_mask.shape[0]
    labels = jnp.arange(lang_count, dtype=jnp.bfloat16)
    logit_scale = jnp.exp(log_scale)
    allowed = jnp.maximum(pair_mask, jnp.eye(lang_count, dtype=jnp.int32)).astype(jnp.float32)
    codes = weight_codes.astype(jnp.float32)
    table = (allowed * (0.25 * (codes[:, None] + codes[None, :]))).astype(jnp.bfloat16)

    langs = lang_ids.astype(jnp.bfloat16)
    tail = jnp.pad(langs[None, :], ((0, 15), (0, D - ROWS)))

    text_unit, text_inv = unit_rows(text_emb.astype(jnp.float32))
    text_low = text_unit.astype(jnp.bfloat16)
    text_out = jnp.concatenate([text_low, tail], axis=0)
    text_far = permute(text_out, lambda i: i + 2)
    text_mix = permute(text_out, lambda i: i + 1 if i % 2 == 0 else i + 3)

    projected = dot(image_feat, head_weight, ((1,), (0,)))
    image_unit, image_inv = unit_rows(projected)
    image_low = image_unit.astype(jnp.bfloat16)
    image_out = jnp.concatenate([image_low, tail], axis=0)
    image_far = permute(image_out, lambda i: i - 2)
    image_mix = permute(image_out, lambda i: i - 1 if i % 2 == 1 else i - 3)

    text_near = swap_cores(text_far)
    image_near = swap_cores(image_far)

    def hot(lang_row):
        return (lang_row[:, None] == labels[None, :]).astype(jnp.bfloat16)

    own_hot = hot(langs)
    own_rows = dot(own_hot, table, ((1,), (0,))).astype(jnp.bfloat16)

    def pair_grad(image, rows, text, text_hot, positive):
        weight = dot(rows, text_hot, ((1,), (1,)))
        logit = logit_scale * dot(image, text, ((1,), (1,))) + logit_bias
        excess = jax.nn.sigmoid(logit)
        if positive:
            excess = excess - jnp.eye(ROWS, dtype=jnp.float32)
        return (weight * excess).astype(jnp.bfloat16)

    grad = pair_grad(image_low, own_rows, text_low, own_hot, True)
    image_sum = dot(grad, text_low, ((1,), (0,)))
    text_sum = dot(grad, image_low, ((0,), (0,)))
    for block in (text_mix, text_far, text_near):
        text = block[:ROWS]
        grad = pair_grad(image_low, own_rows, text, hot(block[ROWS, :ROWS]), False)
        image_sum = image_sum + dot(grad, text, ((1,), (0,)))

    image_grad = logit_scale * image_sum
    radial = jnp.sum(image_unit * image_grad, axis=-1, keepdims=True)
    image_dir = ((image_grad - image_unit * radial) * image_inv).astype(jnp.bfloat16)

    feat_turned = dot(image_feat, order_matrix(row_order()), ((1,), (0,))).astype(jnp.bfloat16)
    dir_turned = dot(image_dir, order_matrix(column_order()), ((1,), (0,))).astype(jnp.bfloat16)
    head = dot(dir_turned, feat_turned, ((0,), (0,))).astype(jnp.bfloat16)
    head = exchange(head, CORE_GROUPS).reshape(2, 384, D)
    head = jnp.sum(head.astype(jnp.float32), axis=0).astype(jnp.bfloat16)
    head = jnp.swapaxes(head.reshape(4, 96, 2, 384), 1, 2).reshape(768, 384)
    head = exchange(head, NEAR_GROUPS).reshape(8, 96, 384)
    head = jnp.sum(head.astype(jnp.float32), axis=0).astype(jnp.bfloat16)
    head = jnp.swapaxes(head.reshape(4, 24, 8, 48), 1, 2).reshape(32, 24, 48)
    head = exchange(head, FAR_GROUPS)
    head_grad = jnp.sum(head.astype(jnp.float32), axis=0).T

    image_back = dot(image_dir, head_weight, ((1,), (1,))).astype(jnp.bfloat16)
    for block in (image_mix, image_far, image_near):
        image = block[:ROWS]
        rows = dot(hot(block[ROWS, :ROWS]), table, ((1,), (0,))).astype(jnp.bfloat16)
        grad = pair_grad(image, rows, text_low, own_hot, False)
        text_sum = text_sum + dot(grad, image, ((0,), (0,)))
    text_grad = logit_scale * text_sum
    text_radial = jnp.sum(text_unit * text_grad, axis=-1, keepdims=True)
    text_back = ((text_grad - text_unit * text_radial) * text_inv).astype(jnp.bfloat16)
    return (image_back, text_back, head_grad)


def solution(mesh):
    in_specs = (
        P(("blk", "lane"), None),
        P(("blk", "lane"), None),
        P(),
        P(("blk", "lane")),
        P(),
        P(),
        P(),
        P(),
    )
    out_specs = (P(("blk", "lane"), None), P(("blk", "lane"), None), P("lane", "blk"))
    return jax.shard_map(
        on_device, mesh=mesh, in_specs=in_specs, out_specs=out_specs, check_vma=False
    )
```

time: 290 us -> 164 us (0.57)
  waiting for transfers between devices: 187 us -> 42.2 us
  matrix products: 15.5 us -> 52.2 us
  starting transfers between devices: 57.8 us -> 37.1 us
  between operations: 15.7 us -> 2.23 us
  local copies, waits for them, and re-layouts: 4.39 us -> 10.7 us
  blocking collectives: 0 us -> 5.8 us
  other arithmetic: 8.56 us -> 11.6 us
    reduce_scatter x1 -> x0, waiting for transfers between devices: 95.3 us -> none  [on_device(): lax.psum_scatter(head_term.astype(jnp.bfloat16), 'blk', scatter_dimension...]
    unnamed x3 -> x0, waiting for transfers between devices: 70.2 us -> none
    ppermute x10 -> x6, starting transfers between devices: 57.7 us -> 18.4 us  [permute(): lax.ppermute(value, 'blk', [(i, target(i) % N_BLK) for i in range(N_BLK)])]
    dot_general x20 -> x24, matrix products: 15.5 us -> 52.2 us  [dot(): lax.dot_general(left, right, (dims, ((), ())), preferred_element_type=jnp...]
    all_to_all x0 -> x2, starting transfers between devices: none -> 18.7 us  [exchange(): lax.all_to_all(value, ('blk', 'lane'), 0, 0, axis_index_groups=groups, ti...]
    all_to_all x0 -> x2, waiting for transfers between devices: none -> 10.9 us  [exchange(): lax.all_to_all(value, ('blk', 'lane'), 0, 0, axis_index_groups=groups, ti...]
    ppermute x10 -> x6, waiting for transfers between devices: 21.4 us -> 31.3 us  [permute(): lax.ppermute(value, 'blk', [(i, target(i) % N_BLK) for i in range(N_BLK)])]
    all_to_all x0 -> x1, blocking collectives: none -> 5.8 us  [exchange(): lax.all_to_all(value, ('blk', 'lane'), 0, 0, axis_index_groups=groups, ti...]
  transfers between devices with their start and end apart: 12 -> 8, of which waited for: 7 -> 3; matrix products, arithmetic and copies ran while one was open for 8% -> 39% of each run, Pallas kernels for 0% -> 0%
where the time goes in v1:
time: 164 us; the launch traced here: 162 us
  matrix products  52.2 us (32%)
  waiting for transfers between devices  42.2 us (26%)
  starting transfers between devices  37.1 us (23%)
  other arithmetic  11.6 us (7%)
  local copies, waits for them, and re-layouts  10.7 us (7%)
  blocking collectives  5.8 us (4%)
  between operations  2.23 us (1%)
    dot_general x24, matrix products, dot(): lax.dot_general(left, right, (dims, ((), ())), preferred_element_type=jnp...  52.2 us
    ppermute x6, waiting for transfers between devices, permute(): lax.ppermute(value, 'blk', [(i, target(i) % N_BLK) for i in range(N_BLK)])  31.3 us
    all_to_all x2, starting transfers between devices, exchange(): lax.all_to_all(value, ('blk', 'lane'), 0, 0, axis_index_groups=groups, ti...  18.7 us
    ppermute x6, starting transfers between devices, permute(): lax.ppermute(value, 'blk', [(i, target(i) % N_BLK) for i in range(N_BLK)])  18.4 us
    all_to_all x2, waiting for transfers between devices, exchange(): lax.all_to_all(value, ('blk', 'lane'), 0, 0, axis_index_groups=groups, ti...  10.9 us
    all_to_all x1, blocking collectives, exchange(): lax.all_to_all(value, ('blk', 'lane'), 0, 0, axis_index_groups=groups, ti...  5.8 us
  transfers between devices with their start and end apart: 8, of which 3 were waited for; matrix products, arithmetic and copies ran while one was open for 39% of the time, Pallas kernels for 0%

profile of v1, /device:TPU:6, one launch (start us, length us, event | category | flops | bytes accessed | tf_op | source)
XLA Modules:
  0.0 161.9 jit_solution(14422245704654588925)
XLA Ops:
  1.9 1.8 %multiply_reduce_fusion.1 = (f32[384]{0:T(512)S(1)}, f32[384,768]{1,0:T(8,128)S(1)}) fusion(bf16[384,768]{1,0:T(8,128)(2,1)} %param.8, bf16[768,768]{1,0:T(8,128)(2,1)S(1)} %copy-done), kind=kOutput, calls=%fused_computation.89 | convolution fusion | flops 453574272 | bytes 2950656 | tf_op jit(solution)/shard_map/dot_general | solution.py:61
  5.4 1.9 %collective-permute-start = (bf16[400,768]{1,0:T(8,128)(2,1)}, bf16[400,768]{1,0:T(8,128)(2,1)}, u32[]{:S(2)}, u32[]{:S(2)}) collective-permute-start(bf16[400,768]{1,0:T(8,128)(2,1)} %get-tuple-element.4), channel_id=1, source_target_pairs={{0,16},{16,64},{32,48},{48,96},{64,80},{80,128},{96,112},{112,160}... | collective-permute-start | bytes 1843208 | tf_op jit(solution)/shard_map/ppermute | solution.py:44
  7.3 6.0 %collective-permute-start.1 = (bf16[400,768]{1,0:T(8,128)(2,1)}, bf16[400,768]{1,0:T(8,128)(2,1)}, u32[]{:S(2)}, u32[]{:S(2)}) collective-permute-start(bf16[400,768]{1,0:T(8,128)(2,1)} %get-tuple-element.4), channel_id=1, source_target_pairs={{0,32},{16,48},{32,64},{48,80},{64,96},{80,112},{96,128},{112,144}... | collective-permute-start | bytes 1843208 | tf_op jit(solution)/shard_map/ppermute | solution.py:44
  13.4 4.3 %collective-permute-start.3 = (bf16[400,768]{1,0:T(8,128)(2,1)}, bf16[400,768]{1,0:T(8,128)(2,1)}, u32[]{:S(2)}, u32[]{:S(2)}) collective-permute-start(bf16[400,768]{1,0:T(8,128)(2,1)} %get-tuple-element.3), channel_id=1, source_target_pairs={{0,464},{16,0},{32,496},{48,32},{64,16},{80,64},{96,48},{112,96},{... | collective-permute-start | bytes 1843208 | tf_op jit(solution)/shard_map/ppermute | solution.py:44
  17.6 1.9 %collective-permute-start.4 = (bf16[400,768]{1,0:T(8,128)(2,1)}, bf16[400,768]{1,0:T(8,128)(2,1)}, u32[]{:S(2)}, u32[]{:S(2)}) collective-permute-start(bf16[400,768]{1,0:T(8,128)(2,1)} %get-tuple-element.3), channel_id=1, source_target_pairs={{0,480},{16,496},{32,0},{48,16},{64,32},{80,48},{96,64},{112,80},{... | collective-permute-start | bytes 1843208 | tf_op jit(solution)/shard_map/ppermute | solution.py:44
  22.8 1.6 %fusion.13 = f32[384,384]{1,0:T(8,128)S(1)} fusion(bf16[384,768]{1,0:T(8,128)(2,1)} %copy-done.2, bf16[384,768]{1,0:T(8,128)(2,1)S(1)} %get-tuple-element.11, f32[]{:T(128)S(6)} %copy.14, f32[]{:T(128)S(6)} %exp.24), kind=kOutput, calls=%fused_computation.40 | convolution fusion | flops 227672064 | bytes 1769480 | tf_op jit(solution)/shard_map/dot_general | solution.py:61
  24.8 1.5 fusion.146
  27.8 1.7 %convolution_convert_fusion.1 = bf16[768,384]{1,0:T(8,128)(2,1)} fusion(bf16[384,768]{1,0:T(8,128)(2,1)S(1)} %copy-done.6, s32[768]{0:T(1024)S(1)} %fusion.132), kind=kOutput, calls=%fused_computation.19 | convolution fusion | flops 454459392 | bytes 1182720 | tf_op jit(solution)/shard_map/dot_general | solution.py:61
  30.1 5.4 %collective-permute-done.3 = bf16[400,768]{1,0:T(8,128)(2,1)} collective-permute-done((bf16[400,768]{1,0:T(8,128)(2,1)}, bf16[400,768]{1,0:T(8,128)(2,1)}, u32[]{:S(2)}, u32[]{:S(2)}) %collective-permute-start.3) | collective-permute-done | bytes 614432 | tf_op jit(solution)/shard_map/ppermute | solution.py:44
  37.9 25.9 %collective-permute-done.4 = bf16[400,768]{1,0:T(8,128)(2,1)} collective-permute-done((bf16[400,768]{1,0:T(8,128)(2,1)}, bf16[400,768]{1,0:T(8,128)(2,1)}, u32[]{:S(2)}, u32[]{:S(2)}) %collective-permute-start.4) | collective-permute-done | bytes 614432 | tf_op jit(solution)/shard_map/ppermute | solution.py:44
  65.4 2.4 %fusion.18 = f32[384,384]{1,0:T(8,128)} fusion(bf16[384,768]{1,0:T(8,128)(2,1)S(1)} %copy-done.3, bf16[400,768]{1,0:T(8,128)(2,1)} %collective-permute-done, f32[]{:T(128)S(6)} %copy.14, f32[]{:T(128)S(6)} %exp.24), kind=kOutput, calls=%fused_computation.45 | convolution fusion | flops 227229696 | bytes 1769480 | tf_op jit(solution)/shard_map/dot_general | solution.py:61
  67.8 2.5 %fusion.23 = f32[384,384]{1,0:T(8,128)} fusion(bf16[384,768]{1,0:T(8,128)(2,1)S(1)} %copy-done.3, bf16[400,768]{1,0:T(8,128)(2,1)} %collective-permute-done.1, f32[]{:T(128)S(6)} %copy.14, f32[]{:T(128)S(6)} %exp.24), kind=kOutput, calls=%fused_computation.50 | convolution fusion | flops 227229696 | bytes 1769480 | tf_op jit(solution)/shard_map/dot_general | solution.py:61
  71.5 1.9 %collective-permute-start.2 = (bf16[400,768]{1,0:T(8,128)(2,1)}, bf16[400,768]{1,0:T(8,128)(2,1)}, u32[]{:S(2)}, u32[]{:S(2)}) collective-permute-start(bf16[400,768]{1,0:T(8,128)(2,1)} %collective-permute-done.1), channel_id=1, source_target_pairs={{0,16},{16,0},{32,48},{48,32},{64,80},{80,64},{96,112},{112,96},{1... | collective-permute-start | bytes 1843208 | tf_op jit(solution)/shard_map/ppermute | solution.py:44
  73.4 2.4 %fusion.33 = f32[384,384]{1,0:T(8,128)} fusion(bf16[384,768]{1,0:T(8,128)(2,1)S(1)} %get-tuple-element.11, bf16[400,768]{1,0:T(8,128)(2,1)} %collective-permute-done.3, f32[]{:T(128)S(6)} %copy.14, f32[]{:T(128)S(6)} %exp.24), kind=kOutput, calls=%fused_computation.60 | convolution fusion | flops 227229696 | bytes 1769480 | tf_op jit(solution)/shard_map/dot_general | solution.py:61
  75.9 2.4 %fusion.38 = f32[384,384]{1,0:T(8,128)} fusion(bf16[384,768]{1,0:T(8,128)(2,1)S(1)} %get-tuple-element.11, bf16[400,768]{1,0:T(8,128)(2,1)} %collective-permute-done.4, f32[]{:T(128)S(6)} %copy.14, f32[]{:T(128)S(6)} %exp.24), kind=kOutput, calls=%fused_computation.65 | convolution fusion | flops 227229696 | bytes 1769480 | tf_op jit(solution)/shard_map/dot_general | solution.py:61
  78.3 2.4 %collective-permute-start.5 = (bf16[400,768]{1,0:T(8,128)(2,1)}, bf16[400,768]{1,0:T(8,128)(2,1)}, u32[]{:S(2)}, u32[]{:S(2)}) collective-permute-start(bf16[400,768]{1,0:T(8,128)(2,1)} %collective-permute-done.4), channel_id=1, source_target_pairs={{0,16},{16,0},{32,48},{48,32},{64,80},{80,64},{96,112},{112,96},{1... | collective-permute-start | bytes 1843208 | tf_op jit(solution)/shard_map/ppermute | solution.py:44
  80.7 3.5 %convolution_add_fusion.5 = f32[384,768]{1,0:T(8,128)} fusion(f32[384,768]{1,0:T(8,128)} %fusion.146, f32[384,384]{1,0:T(8,128)} %fusion.18, bf16[384,109]{0,1:T(8,128)(2,1)} %copy-done.5, bf16[400,768]{1,0:T(8,128)(2,1)} %collective-permute-done, bf16[384]{0:T(512)(128)(2,1)S(1)} %slice_reduce_fusion.5), kind=kOutput, calls=%fused_computation.15 | convolution fusion | flops 259353216 | bytes 3625728 | tf_op jit(solution)/shard_map/dot_general | solution.py:61
  84.2 3.5 %convolution_add_fusion.4 = f32[384,768]{1,0:T(8,128)} fusion(f32[384,768]{1,0:T(8,128)} %convolution_add_fusion.5, f32[384,384]{1,0:T(8,128)} %fusion.23, bf16[384,109]{0,1:T(8,128)(2,1)} %copy-done.5, bf16[400,768]{1,0:T(8,128)(2,1)} %collective-permute-done.1, bf16[384]{0:T(512)(128)(2,1)} %slice_reduce_fusion.4), kind=kOutput, calls=%fused_computation.14 | convolution fusion | flops 259353216 | bytes 3625984 | tf_op jit(solution)/shard_map/dot_general | solution.py:61
  87.6 3.5 %convolution_add_fusion.2 = f32[384,768]{1,0:T(8,128)} fusion(f32[384,768]{1,0:T(8,128)} %fusion.147, f32[384,384]{1,0:T(8,128)} %fusion.33, bf16[384,109]{0,1:T(8,128)(2,1)} %convolution_convert_fusion.5, bf16[400,768]{1,0:T(8,128)(2,1)} %collective-permute-done.3, bf16[384]{0:T(512)(128)(2,1)S(1)} %convert_element_type.97), kind=kOutput, calls=%fused_computation.12 | convolution fusion | flops 259353216 | bytes 3625728 | tf_op jit(solution)/shard_map/dot_general | solution.py:61
  91.1 3.5 %convolution_add_fusion.1 = f32[384,768]{1,0:T(8,128)} fusion(f32[384,768]{1,0:T(8,128)} %convolution_add_fusion.2, f32[384,384]{1,0:T(8,128)} %fusion.38, bf16[384,109]{0,1:T(8,128)(2,1)} %convolution_convert_fusion.4, bf16[400,768]{1,0:T(8,128)(2,1)} %collective-permute-done.4, bf16[384]{0:T(512)(128)(2,1)S(1)} %convert_element_type.97), kind=kOutput, calls=%fused_computation.11 | convolution fusion | flops 259353216 | bytes 3625728 | tf_op jit(solution)/shard_map/dot_general | solution.py:61
  94.6 2.6 %fusion.28 = f32[384,384]{1,0:T(8,128)} fusion(bf16[384,768]{1,0:T(8,128)(2,1)} %copy-done.2, bf16[400,768]{1,0:T(8,128)(2,1)} %collective-permute-done.2, f32[]{:T(128)S(6)} %copy.14, f32[]{:T(128)S(6)} %exp.24), kind=kOutput, calls=%fused_computation.55 | convolution fusion | flops 227229696 | bytes 1769480 | tf_op jit(solution)/shard_map/dot_general | solution.py:61
  98.4 3.5 %multiply_reduce_fusion = (f32[384]{0:T(512)S(1)}, f32[384,768]{1,0:T(8,128)}) fusion(f32[384,768]{1,0:T(8,128)S(1)} %get-tuple-element.6, f32[384]{0:T(512)S(1)} %add_rsqrt_fusion.1, f32[384,768]{1,0:T(8,128)} %convolution_add_fusion.4, bf16[400,768]{1,0:T(8,128)(2,1)} %collective-permute-done.2, f32[384,384]{1,0:T(8,128)} %fusion.28, ...), kind=kOutput, calls=%fused_computation.88 | convolution fusion | flops 260532480 | bytes 4808708 | tf_op jit(solution)/shard_map/dot_general | solution.py:61
  101.9 2.3 %multiply_convert_fusion = bf16[384,768]{1,0:T(8,128)(2,1)} fusion(f32[384,768]{1,0:T(8,128)} %get-tuple-element.8, f32[384,768]{1,0:T(8,128)S(1)} %get-tuple-element.6, f32[384]{0:T(512)S(1)} %get-tuple-element.7, f32[384]{0:T(512)S(1)} %add_rsqrt_fusion.1), kind=kLoop, calls=%fused_computation.87 | loop fusion | flops 1474560 | bytes 2952192 | tf_op jit(solution)/shard_map/convert_element_type | solution.py:133
  104.3 4.0 %convolution_convert_fusion = bf16[768,768]{1,0:T(8,128)(2,1)} fusion(bf16[768,384]{1,0:T(8,128)(2,1)} %convolution_convert_fusion.1, bf16[384,768]{1,0:T(8,128)(2,1)} %multiply_convert_fusion, s32[768]{0:T(1024)} %fusion.126), kind=kOutput, calls=%fused_computation.4 | convolution fusion | flops 907444224 | bytes 2362368 | tf_op jit(solution)/shard_map/dot_general | solution.py:61
  108.2 5.8 %all_to_all.23 = bf16[2,384,768]{2,1,0:T(8,128)(2,1)S(1)} all-to-all(bf16[2,384,768]{2,1,0:T(8,128)(2,1)} %bitcast.37), channel_id=1, replica_groups={{0,16},{1,17},{2,18},{3,19},{4,20},{5,21},{6,22},{7,23},{8,24},{9,25},{..., dimensions={0} | all-to-all | bytes 2359296 | tf_op jit(solution)/shard_map/all_to_all | solution.py:52
  115.2 1.8 %reshape.161 = bf16[4,96,2,384]{3,2,1,0:T(2,128)(2,1)S(1)} reshape(bf16[384,768]{1,0:T(8,128)(2,1)} %reduce_sum.73) | data formatting | bytes 1179648 | tf_op jit(solution)/shard_map/reshape | solution.py:140
  118.0 5.5 %all-to-all-start.1 = ((bf16[8,96,384]{2,1,0:T(8,128)(2,1)}), bf16[8,96,384]{2,1,0:T(8,128)(2,1)}, u32[]{:S(2)}, u32[]{:S(2)}) async-start(bf16[8,96,384]{2,1,0:T(8,128)(2,1)} %bitcast.2), calls=%async_computation.1 | async-start | bytes 1179648 | tf_op jit(solution)/shard_map/all_to_all | solution.py:52
  125.1 2.5 %fusion.43 = f32[384,384]{1,0:T(8,128)} fusion(bf16[384,768]{1,0:T(8,128)(2,1)S(1)} %get-tuple-element.11, bf16[400,768]{1,0:T(8,128)(2,1)} %collective-permute-done.5, f32[]{:T(128)S(6)} %copy.14, f32[]{:T(128)S(6)} %exp.24), kind=kOutput, calls=%fused_computation.70 | convolution fusion | flops 227229696 | bytes 1769480 | tf_op jit(solution)/shard_map/dot_general | solution.py:61
  127.6 3.1 %fusion.52 = (f32[384]{0:T(512)S(1)}, f32[384,768]{1,0:T(8,128)}) fusion(bf16[384,768]{1,0:T(8,128)(2,1)S(1)} %copy-done.1, f32[384]{0:T(512)S(1)} %add_rsqrt_fusion, f32[384,768]{1,0:T(8,128)S(1)} %copy-done.4, bf16[400,768]{1,0:T(8,128)(2,1)} %collective-permute-done.5, f32[384,384]{1,0:T(8,128)} %fusion.43, ...), kind=kOutput, calls=%fused_computation.80 | convolution fusion | flops 260827392 | bytes 4218628 | tf_op jit(solution)/shard_map/dot_general | solution.py:61
  130.8 2.4 %fusion.55 = bf16[384,768]{1,0:T(8,128)(2,1)} fusion(f32[384,768]{1,0:T(8,128)} %get-tuple-element.10, bf16[384,768]{1,0:T(8,128)(2,1)S(1)} %copy-done.1, f32[384]{0:T(512)S(1)} %get-tuple-element.9, f32[384]{0:T(512)S(1)} %add_rsqrt_fusion), kind=kLoop, calls=%fused_computation.83 | loop fusion | flops 1769472 | bytes 2362368 | tf_op jit(solution)/shard_map/convert_element_type | solution.py:155
  135.5 13.2 %all-to-all-start.2 = ((bf16[32,2,576]{2,1,0:T(2,128)(2,1)}), bf16[32,2,576]{2,1,0:T(2,128)(2,1)S(1)}, u32[]{:S(2)}, u32[]{:S(2)}) async-start(bf16[32,2,576]{2,1,0:T(2,128)(2,1)} %reshape.170), calls=%async_computation.2 | async-start | bytes 163840 | tf_op jit(solution)/shard_map/all_to_all | solution.py:52
  150.2 10.9 %all-to-all-done.2 = bf16[32,2,576]{2,1,0:T(2,128)(2,1)S(1)} async-done(((bf16[32,2,576]{2,1,0:T(2,128)(2,1)}), bf16[32,2,576]{2,1,0:T(2,128)(2,1)S(1)}, u32[]{:S(2)}, u32[]{:S(2)}) %all-to-all-start.2) | async-done | bytes 73760 | tf_op jit(solution)/shard_map/all_to_all | solution.py:52
  (59 shorter events, 22.2 us)
Async XLA Ops:
  0.6 1.3 copy-start
  0.6 3.0 %copy-start.1 = (bf16[384,768]{1,0:T(8,128)(2,1)S(1)}, bf16[384,768]{1,0:T(8,128)(2,1)}, u32[]{:S(2)}) copy-start(bf16[384,768]{1,0:T(8,128)(2,1)} %param.9) | copy-start | bytes 1769476
  0.7 3.3 %copy-start.10 = (s32[384]{0:T(512)S(1)}, s32[384]{0:T(512)}, u32[]{:S(2)}) copy-start(s32[384]{0:T(512)} %param.11) | copy-start | bytes 4612
  4.2 1.3 copy-start.2
  5.4 31.8 %collective-permute-start = (bf16[400,768]{1,0:T(8,128)(2,1)}, bf16[400,768]{1,0:T(8,128)(2,1)}, u32[]{:S(2)}, u32[]{:S(2)}) collective-permute-start(bf16[400,768]{1,0:T(8,128)(2,1)} %get-tuple-element.4), channel_id=1, source_target_pairs={{0,16},{16,64},{32,48},{48,96},{64,80},{80,128},{96,112},{112,160}... | collective-permute-start | bytes 1843208 | tf_op jit(solution)/shard_map/ppermute | solution.py:44
  7.3 60.5 %collective-permute-start.1 = (bf16[400,768]{1,0:T(8,128)(2,1)}, bf16[400,768]{1,0:T(8,128)(2,1)}, u32[]{:S(2)}, u32[]{:S(2)}) collective-permute-start(bf16[400,768]{1,0:T(8,128)(2,1)} %get-tuple-element.4), channel_id=1, source_target_pairs={{0,32},{16,48},{32,64},{48,80},{64,96},{80,112},{96,128},{112,144}... | collective-permute-start | bytes 1843208 | tf_op jit(solution)/shard_map/ppermute | solution.py:44
  13.4 22.2 %collective-permute-start.3 = (bf16[400,768]{1,0:T(8,128)(2,1)}, bf16[400,768]{1,0:T(8,128)(2,1)}, u32[]{:S(2)}, u32[]{:S(2)}) collective-permute-start(bf16[400,768]{1,0:T(8,128)(2,1)} %get-tuple-element.3), channel_id=1, source_target_pairs={{0,464},{16,0},{32,496},{48,32},{64,16},{80,64},{96,48},{112,96},{... | collective-permute-start | bytes 1843208 | tf_op jit(solution)/shard_map/ppermute | solution.py:44
  17.6 46.1 %collective-permute-start.4 = (bf16[400,768]{1,0:T(8,128)(2,1)}, bf16[400,768]{1,0:T(8,128)(2,1)}, u32[]{:S(2)}, u32[]{:S(2)}) collective-permute-start(bf16[400,768]{1,0:T(8,128)(2,1)} %get-tuple-element.3), channel_id=1, source_target_pairs={{0,480},{16,496},{32,0},{48,16},{64,32},{80,48},{96,64},{112,80},{... | collective-permute-start | bytes 1843208 | tf_op jit(solution)/shard_map/ppermute | solution.py:44
  22.5 42.0 %copy-start.8 = (bf16[109,109]{1,0:T(8,128)(2,1)}, bf16[109,109]{1,0:T(8,128)(2,1)S(1)}, u32[]{:S(2)}) copy-start(bf16[109,109]{1,0:T(8,128)(2,1)S(1)} %multiply_convert_fusion.2) | copy-start | bytes 71290
  22.8 1.7 %copy-start.5 = (bf16[384,109]{0,1:T(8,128)(2,1)}, bf16[384,109]{0,1:T(8,128)(2,1)S(1)}, u32[]{:S(2)}) copy-start(bf16[384,109]{0,1:T(8,128)(2,1)S(1)} %convolution_convert_fusion.6) | copy-start | bytes 251140
  24.8 1.5 copy-start.3
  26.3 1.5 copy-start.6
  71.5 23.1 %collective-permute-start.2 = (bf16[400,768]{1,0:T(8,128)(2,1)}, bf16[400,768]{1,0:T(8,128)(2,1)}, u32[]{:S(2)}, u32[]{:S(2)}) collective-permute-start(bf16[400,768]{1,0:T(8,128)(2,1)} %collective-permute-done.1), channel_id=1, source_target_pairs={{0,16},{16,0},{32,48},{48,32},{64,80},{80,64},{96,112},{112,96},{1... | collective-permute-start | bytes 1843208 | tf_op jit(solution)/shard_map/ppermute | solution.py:44
  78.3 45.2 %collective-permute-start.5 = (bf16[400,768]{1,0:T(8,128)(2,1)}, bf16[400,768]{1,0:T(8,128)(2,1)}, u32[]{:S(2)}, u32[]{:S(2)}) collective-permute-start(bf16[400,768]{1,0:T(8,128)(2,1)} %collective-permute-done.4), channel_id=1, source_target_pairs={{0,16},{16,0},{32,48},{48,32},{64,80},{80,64},{96,112},{112,96},{1... | collective-permute-start | bytes 1843208 | tf_op jit(solution)/shard_map/ppermute | solution.py:44
  117.0 7.2 %copy-start.9 = (bf16[109,109]{1,0:T(8,128)(2,1)S(1)}, bf16[109,109]{1,0:T(8,128)(2,1)}, u32[]{:S(2)}) copy-start(bf16[109,109]{1,0:T(8,128)(2,1)} %copy-done.8) | copy-start | bytes 71290
  118.0 15.2 %all-to-all-start.1 = ((bf16[8,96,384]{2,1,0:T(8,128)(2,1)}), bf16[8,96,384]{2,1,0:T(8,128)(2,1)}, u32[]{:S(2)}, u32[]{:S(2)}) async-start(bf16[8,96,384]{2,1,0:T(8,128)(2,1)} %bitcast.2), calls=%async_computation.1 | async-start | bytes 1179648 | tf_op jit(solution)/shard_map/all_to_all | solution.py:52
  125.1 2.5 %copy-start.4 = (f32[384,768]{1,0:T(8,128)S(1)}, f32[384,768]{1,0:T(8,128)}, u32[]{:S(2)}) copy-start(f32[384,768]{1,0:T(8,128)} %convolution_add_fusion.1) | copy-start | bytes 3538948
  133.1 15.6 %copy-start.7 = (bf16[384,768]{1,0:T(8,128)(2,1)S(1)}, bf16[384,768]{1,0:T(8,128)(2,1)}, u32[]{:S(2)}) copy-start(bf16[384,768]{1,0:T(8,128)(2,1)} %multiply_convert_fusion) | copy-start | bytes 1769476
  135.5 25.6 %all-to-all-start.2 = ((bf16[32,2,576]{2,1,0:T(2,128)(2,1)}), bf16[32,2,576]{2,1,0:T(2,128)(2,1)S(1)}, u32[]{:S(2)}, u32[]{:S(2)}) async-start(bf16[32,2,576]{2,1,0:T(2,128)(2,1)} %reshape.170), calls=%async_computation.2 | async-start | bytes 163840 | tf_op jit(solution)/shard_map/all_to_all | solution.py:52

commit v2 on v1

v2 whole, which is shorter than its diff:
```python
import jax
import jax.numpy as jnp
from jax import lax
from jax.experimental import pallas as pl
from jax.experimental.pallas import tpu as pltpu
from jax.sharding import PartitionSpec as P

D = 768
HALF = D // 2
ROWS = 384
TAIL = 16
LABELS = 128
N_BLK = 32
EPSILON = 1e-06
VMEM_BYTES = 48 * 1024 * 1024


def device_index(z_hi, x, core, z_lo, y):
    return ((z_hi * 4 + x) * 2 + core) * 16 + z_lo * 8 + y


NEAR_GROUPS = [
    [device_index(z, x, c, l, 2 * y_hi + y_lo) for x in range(4) for y_lo in range(2)]
    for z in range(4)
    for c in range(2)
    for l in range(2)
    for y_hi in range(4)
]
FAR_GROUPS = [
    [
        device_index(z, x, c, l, 2 * y_hi + y_lo)
        for z in range(4)
        for l in range(2)
        for y_hi in range(4)
    ]
    for x in range(4)
    for c in range(2)
    for y_lo in range(2)
]


def permute(value, target):
    pairs = [(i, target(i)) for i in range(N_BLK)]
    return lax.ppermute(value, "blk", [(i, j % N_BLK) for i, j in pairs if j is not None])


def swap_cores(value):
    return permute(value, lambda i: i ^ 1)


def exchange(value, groups):
    return lax.all_to_all(value, ("blk", "lane"), 0, 0, axis_index_groups=groups, tiled=True)


def dot(left, right, dims=((1,), (0,))):
    return lax.dot_general(left, right, (dims, ((), ())), preferred_element_type=jnp.float32)


def call(kernel, outs, args, flops, scalars=0):
    smem = pl.BlockSpec(memory_space=pltpu.SMEM)
    vmem = pl.BlockSpec(memory_space=pltpu.VMEM)
    moved = sum(a.size * a.dtype.itemsize for a in tuple(args) + tuple(outs))
    return pl.pallas_call(
        kernel,
        out_shape=outs,
        in_specs=[smem] * scalars + [vmem] * (len(args) - scalars),
        out_specs=[vmem] * len(outs),
        cost_estimate=pl.CostEstimate(flops=flops, bytes_accessed=moved, transcendentals=0),
        compiler_params=pltpu.CompilerParams(vmem_limit_bytes=VMEM_BYTES),
    )(*args)


def array(shape, dtype):
    return jax.ShapeDtypeStruct(shape, dtype)


def text_kernel(text_ref, tail_ref, out_ref):
    text = text_ref[...].astype(jnp.float32)
    inverse = lax.rsqrt(jnp.sum(text * text, axis=-1, keepdims=True) + EPSILON)
    out_ref[:ROWS, :] = (text * inverse).astype(jnp.bfloat16)
    out_ref[ROWS:, :] = tail_ref[...]


def image_kernel(feat_ref, head_ref, tail_ref, out_ref, unit_ref, inv_ref):
    projected = dot(feat_ref[...], head_ref[...])
    inverse = lax.rsqrt(jnp.sum(projected * projected, axis=-1, keepdims=True) + EPSILON)
    unit = projected * inverse
    unit_ref[...] = unit
    inv_ref[...] = inverse
    out_ref[:ROWS, :] = unit.astype(jnp.bfloat16)
    out_ref[ROWS:, :] = tail_ref[...]


def pair_term(scale, bias, own, own_rows, other_ref, positive):
    other = other_ref[:ROWS, :]
    langs = other_ref[ROWS : ROWS + 1, :ROWS].astype(jnp.int32)
    hot = lax.broadcasted_iota(jnp.int32, (LABELS, ROWS), 0) == langs
    weight = dot(own_rows, hot.astype(jnp.float32).astype(jnp.bfloat16))
    logit = scale * dot(own, other, ((1,), (1,))) + bias
    excess = 0.5 + 0.5 * jnp.tanh(0.5 * logit)
    if positive:
        row = lax.broadcasted_iota(jnp.int32, (ROWS, ROWS), 0)
        column = lax.broadcasted_iota(jnp.int32, (ROWS, ROWS), 1)
        excess = jnp.where(row == column, excess - 1.0, excess)
    return dot((weight * excess).astype(jnp.bfloat16), other)


def first_kernel(scalar_ref, own_ref, rows_ref, same_ref, mix_ref, sum_ref):
    scale, bias = scalar_ref[0], scalar_ref[1]
    own, rows = own_ref[:ROWS, :], rows_ref[...]
    sum_ref[...] = pair_term(scale, bias, own, rows, same_ref, True)
    sum_ref[...] += pair_term(scale, bias, own, rows, mix_ref, False)


def next_kernel(scalar_ref, own_ref, rows_ref, other_ref, before_ref, sum_ref):
    scale, bias = scalar_ref[0], scalar_ref[1]
    term = pair_term(scale, bias, own_ref[:ROWS, :], rows_ref[...], other_ref, False)
    sum_ref[...] = before_ref[...] + term


def image_last_kernel(
    scalar_ref, own_ref, rows_ref, other_ref, before_ref, unit_ref, inv_ref, order_ref,
    dir_ref, keep_ref, send_ref,
):
    scale, bias = scalar_ref[0], scalar_ref[1]
    term = pair_term(scale, bias, own_ref[:ROWS, :], rows_ref[...], other_ref, False)
    grad = scale * (before_ref[...] + term)
    unit = unit_ref[...]
    radial = jnp.sum(unit * grad, axis=-1, keepdims=True)
    direction = ((grad - unit * radial) * inv_ref[...]).astype(jnp.bfloat16)
    dir_ref[...] = direction
    turned = dot(order_ref[...], direction, ((1,), (1,))).astype(jnp.bfloat16)
    keep_ref[...] = turned[:HALF, :]
    send_ref[...] = turned[HALF:, :]


def text_last_kernel(
    scalar_ref, own_ref, rows_ref, other_ref, before_ref, text_ref, out_ref
):
    scale, bias = scalar_ref[0], scalar_ref[1]
    term = pair_term(scale, bias, own_ref[:ROWS, :], rows_ref[...], other_ref, False)
    grad = scale * (before_ref[...] + term)
    text = text_ref[...].astype(jnp.float32)
    inverse = lax.rsqrt(jnp.sum(text * text, axis=-1, keepdims=True) + EPSILON)
    unit = text * inverse
    radial = jnp.sum(unit * grad, axis=-1, keepdims=True)
    out_ref[...] = ((grad - unit * radial) * inverse).astype(jnp.bfloat16)


def head_kernel(keep_ref, feat_ref, got_ref, feat_near_ref, out_ref):
    head = dot(keep_ref[...], feat_ref[...]) + dot(got_ref[...], feat_near_ref[...])
    head = head.astype(jnp.bfloat16)
    for x in range(4):
        for y_lo in range(2):
            out_ref[2 * x + y_lo] = head[96 * x : 96 * x + 96, HALF * y_lo : HALF * y_lo + HALF]


def back_kernel(dir_ref, head_ref, out_ref):
    out_ref[...] = dot(dir_ref[...], head_ref[...], ((1,), (1,))).astype(jnp.bfloat16)


def column_order(core):
    new = jnp.arange(D, dtype=jnp.int32)
    side, x, z_hi, rest = new // 384, new // 96 % 4, new // 24 % 4, new % 24
    return z_hi * 192 + x * 48 + (side ^ core) * 24 + rest


def row_order():
    new = jnp.arange(D, dtype=jnp.int32)
    y_lo, z_lo, y_hi, rest = new // 384, new // 192 % 2, new // 48 % 4, new % 48
    return z_lo * 384 + (y_hi * 2 + y_lo) * 48 + rest


def order_matrix(old):
    return (old[:, None] == jnp.arange(D, dtype=jnp.int32)[None, :]).astype(jnp.bfloat16)


def on_device(
    image_feat, text_emb, head_weight, lang_ids, pair_mask, weight_codes, log_scale, logit_bias
):
    place = lax.axis_index("blk") % 8
    lang_count = pair_mask.shape[0]
    allowed = jnp.maximum(pair_mask, jnp.eye(lang_count, dtype=jnp.int32)).astype(jnp.float32)
    codes = weight_codes.astype(jnp.float32)
    table = (allowed * (0.25 * (codes[:, None] + codes[None, :]))).astype(jnp.bfloat16)
    extra = LABELS - lang_count
    table = jnp.pad(table, ((0, extra), (0, extra)))
    scalars = jnp.stack([jnp.exp(log_scale), logit_bias])
    tail = jnp.pad(lang_ids.astype(jnp.bfloat16)[None, :], ((0, TAIL - 1), (0, D - ROWS)))
    block = array((ROWS + TAIL, D), jnp.bfloat16)
    total = array((ROWS, D), jnp.float32)
    pair_flops = 2 * ROWS * ROWS * (2 * D + LABELS)

    (text_out,) = call(text_kernel, [block], (text_emb, tail), 4 * ROWS * D)
    text_far = permute(text_out, lambda i: i + 2 if i % 8 != 7 else None)
    text_via = permute(text_out, lambda i: i + 8 if i % 8 in (5, 7) else None)
    text_mix = permute(
        text_out, lambda i: i + 1 if i % 2 == 0 else (i + 3 if i % 8 != 5 else None)
    )

    image_out, image_unit, image_inv = call(
        image_kernel,
        [block, total, array((ROWS, 1), jnp.float32)],
        (image_feat, head_weight, tail),
        2 * ROWS * D * D,
    )
    image_far = permute(image_out, lambda i: i - 2 if i % 8 != 0 else None)
    image_via = permute(image_out, lambda i: i - 8 if i % 8 in (0, 2) else None)
    image_mix = permute(
        image_out, lambda i: i - 1 if i % 2 == 1 else (i - 3 if i % 8 != 2 else None)
    )

    own_hot = (lang_ids[:, None] == jnp.arange(LABELS)[None, :]).astype(jnp.bfloat16)
    image_rows = dot(own_hot, table).astype(jnp.bfloat16)
    text_rows = dot(own_hot, table, ((1,), (1,))).astype(jnp.bfloat16)
    feat_turned = dot(image_feat, order_matrix(row_order()), ((1,), (1,))).astype(jnp.bfloat16)
    feat_near = swap_cores(feat_turned)
    order = order_matrix(column_order(place % 2))

    text_hop = permute(text_via, lambda i: {7: i - 6, 5: i - 5}.get(i % 8))
    text_far = jnp.where(place == 1, text_hop, text_far)
    text_mix = jnp.where(place == 0, text_hop, text_mix)
    text_near = swap_cores(text_far)
    image_hop = permute(image_via, lambda i: {0: i + 6, 2: i + 5}.get(i % 8))
    image_far = jnp.where(place == 6, image_hop, image_far)
    image_mix = jnp.where(place == 7, image_hop, image_mix)
    image_near = swap_cores(image_far)

    (image_sum,) = call(
        first_kernel,
        [total],
        (scalars, image_out, image_rows, text_out, text_mix),
        2 * pair_flops,
        1,
    )
    (image_sum,) = call(
        next_kernel, [total], (scalars, image_out, image_rows, text_far, image_sum), pair_flops, 1
    )
    half = array((HALF, ROWS), jnp.bfloat16)
    image_dir, keep, send = call(
        image_last_kernel,
        [array((ROWS, D), jnp.bfloat16), half, half],
        (
            scalars, image_out, image_rows, text_near, image_sum, image_unit, image_inv, order
        ),
        pair_flops + 2 * ROWS * D * D,
        1,
    )
    got = swap_cores(send)
    (head,) = call(
        head_kernel,
        [array((8, 96, HALF), jnp.bfloat16)],
        (keep, feat_turned, got, feat_near),
        4 * HALF * ROWS * D,
    )
    head = exchange(head, NEAR_GROUPS)
    head = jnp.sum(head.astype(jnp.float32), axis=0).astype(jnp.bfloat16)
    head = jnp.swapaxes(head.reshape(4, 24, 8, 48), 1, 2).reshape(32, 24, 48)
    head = exchange(head, FAR_GROUPS)
    head_grad = jnp.sum(head.astype(jnp.float32), axis=0).T

    (image_back,) = call(
        back_kernel,
        [array((ROWS, D), jnp.bfloat16)],
        (image_dir, head_weight),
        2 * ROWS * D * D,
    )
    (text_sum,) = call(
        first_kernel,
        [total],
        (scalars, text_out, text_rows, image_out, image_mix),
        2 * pair_flops,
        1,
    )
    (text_sum,) = call(
        next_kernel, [total], (scalars, text_out, text_rows, image_far, text_sum), pair_flops, 1
    )
    (text_back,) = call(
        text_last_kernel,
        [array((ROWS, D), jnp.bfloat16)],
        (scalars, text_out, text_rows, image_near, text_sum, text_emb),
        pair_flops,
        1,
    )
    return (image_back, text_back, head_grad)


def solution(mesh):
    in_specs = (
        P(("blk", "lane"), None),
        P(("blk", "lane"), None),
        P(),
        P(("blk", "lane")),
        P(),
        P(),
        P(),
        P(),
    )
    out_specs = (P(("blk", "lane"), None), P(("blk", "lane"), None), P("lane", "blk"))
    return jax.shard_map(
        on_device, mesh=mesh, in_specs=in_specs, out_specs=out_specs, check_vma=False
    )
```

time: 164 us -> 139 us (0.85)
  starting transfers between devices: 37.1 us -> 95.1 us
  matrix products: 52.2 us -> 2.07 us
  waiting for transfers between devices: 42.2 us -> 4.98 us
  Pallas kernels: 0 us -> 19.7 us
  blocking collectives: 5.8 us -> 0 us
  local copies, waits for them, and re-layouts: 10.7 us -> 5.36 us
  other arithmetic: 11.6 us -> 8.56 us
    dot_general x24 -> x3, matrix products: 52.2 us -> 2.07 us  [dot(): lax.dot_general(left, right, (dims, ((), ())), preferred_element_type=jnp...]
    ppermute x6 -> x12, starting transfers between devices: 18.4 us -> 48.4 us  [permute(): lax.ppermute(value, 'blk', [(i, j % N_BLK) for i, j in pairs if j is not...]
    ppermute x6 -> x12, waiting for transfers between devices: 31.3 us -> 2.51 us  [permute(): lax.ppermute(value, 'blk', [(i, j % N_BLK) for i, j in pairs if j is not...]
    all_to_all x2, starting transfers between devices: 18.7 us -> 46.7 us  [exchange(): lax.all_to_all(value, ('blk', 'lane'), 0, 0, axis_index_groups=groups, ti...]
    pallas_call x0 -> x10, Pallas kernels: none -> 19.7 us  [call(): pl.pallas_call(kernel, out_shape=outs, in_specs=[smem] * scalars + [vmem]...]
    all_to_all x2, waiting for transfers between devices: 10.9 us -> 2.48 us  [exchange(): lax.all_to_all(value, ('blk', 'lane'), 0, 0, axis_index_groups=groups, ti...]
    all_to_all x1 -> x0, blocking collectives: 5.8 us -> none  [exchange(): lax.all_to_all(value, ('blk', 'lane'), 0, 0, axis_index_groups=groups, ti...]
    slice x6 -> x0, local copies, waits for them, and re-layouts: 5.35 us -> none  [the longest x3 3.22 us: on_device(): grad = pair_grad(image_low, own_rows, text, hot(block[ROWS, :ROWS]), False)]
  transfers between devices with their start and end apart: 8 -> 14, of which waited for: 3 -> 2; matrix products, arithmetic and copies ran while one was open for 39% -> 8% of each run, Pallas kernels for 0% -> 14%
where the time goes in v2:
time: 139 us; the launch traced here: 138 us
  starting transfers between devices  95.1 us (68%)
  Pallas kernels  19.7 us (14%)
  other arithmetic  8.56 us (6%)
  local copies, waits for them, and re-layouts  5.36 us (4%)
  waiting for transfers between devices  4.98 us (4%)
  between operations  2.32 us (2%)
  matrix products  2.07 us (1%)
    ppermute x12, starting transfers between devices, permute(): lax.ppermute(value, 'blk', [(i, j % N_BLK) for i, j in pairs if j is not...  48.4 us
    all_to_all x2, starting transfers between devices, exchange(): lax.all_to_all(value, ('blk', 'lane'), 0, 0, axis_index_groups=groups, ti...  46.7 us
    pallas_call x10, Pallas kernels, call(): pl.pallas_call(kernel, out_shape=outs, in_specs=[smem] * scalars + [vmem]...  19.7 us
    unnamed x28, local copies, waits for them, and re-layouts  5.13 us
  transfers between devices with their start and end apart: 14, of which 2 were waited for; matrix products, arithmetic and copies ran while one was open for 8% of the time, Pallas kernels for 14%

profile of v2, /device:TPU:6, one launch (start us, length us, event | category | flops | bytes accessed | tf_op | source)
XLA Modules:
  0.0 138.1 jit_solution(3180827530906427308)
XLA Ops:
  1.3 1.1 copy-done.1
  2.6 1.5 %collective-permute-start = (bf16[400,768]{1,0:T(8,128)(2,1)S(1)}, bf16[400,768]{1,0:T(8,128)(2,1)}, u32[]{:S(2)}, u32[]{:S(2)}) collective-permute-start(bf16[400,768]{1,0:T(8,128)(2,1)S(1)} %shard_map.104.same_ref.own_ref), channel_id=1, source_target_pairs={{80,208},{112,240},{208,336},{240,368},{336,464},{368,496},{464,80... | collective-permute-start | bytes 1843208 | tf_op jit(solution)/shard_map/ppermute | solution.py:44
  4.1 6.0 %collective-permute-start.2 = (bf16[400,768]{1,0:T(8,128)(2,1)S(1)}, bf16[400,768]{1,0:T(8,128)(2,1)}, u32[]{:S(2)}, u32[]{:S(2)}) collective-permute-start(bf16[400,768]{1,0:T(8,128)(2,1)S(1)} %shard_map.104.same_ref.own_ref), channel_id=1, source_target_pairs={{0,32},{16,48},{32,64},{48,80},{64,96},{80,112},{96,128},{128,160}... | collective-permute-start | bytes 1843208 | tf_op jit(solution)/shard_map/ppermute | solution.py:44
  10.1 1.9 %collective-permute-start.4 = (bf16[400,768]{1,0:T(8,128)(2,1)S(1)}, bf16[400,768]{1,0:T(8,128)(2,1)}, u32[]{:S(2)}, u32[]{:S(2)}) collective-permute-start(bf16[400,768]{1,0:T(8,128)(2,1)S(1)} %shard_map.104.same_ref.own_ref), channel_id=1, source_target_pairs={{0,16},{16,64},{32,48},{48,96},{64,80},{96,112},{112,160},{128,144... | collective-permute-start | bytes 1843208 | tf_op jit(solution)/shard_map/ppermute | solution.py:44
  12.1 1.6 %collective-permute-start.1 = (bf16[400,768]{1,0:T(8,128)(2,1)}, bf16[400,768]{1,0:T(8,128)(2,1)}, u32[]{:S(2)}, u32[]{:S(2)}) collective-permute-start(bf16[400,768]{1,0:T(8,128)(2,1)} %collective-permute-done), channel_id=1, source_target_pairs={{80,0},{112,16},{208,128},{240,144},{336,256},{368,272},{464,384},... | collective-permute-start | bytes 1843208 | tf_op jit(solution)/shard_map/ppermute | solution.py:44
  13.7 1.6 %fusion.3.feat_ref = bf16[384,768]{1,0:T(8,128)(2,1)} fusion(bf16[384,768]{1,0:T(8,128)(2,1)S(1)} %copy-done.7, s32[768]{0:T(1024)S(1)} %fusion.32), kind=kOutput, calls=%fused_computation.5 | convolution fusion | flops 453869568 | bytes 1182720 | tf_op jit(solution)/shard_map/dot_general | solution.py:56
  15.3 15.2 %collective-permute-start.11 = (bf16[384,768]{1,0:T(8,128)(2,1)}, bf16[384,768]{1,0:T(8,128)(2,1)}, u32[]{:S(2)}, u32[]{:S(2)}) collective-permute-start(bf16[384,768]{1,0:T(8,128)(2,1)} %fusion.3.feat_ref), channel_id=1, source_target_pairs={{0,16},{16,0},{32,48},{48,32},{64,80},{80,64},{96,112},{112,96},{1... | collective-permute-start | bytes 1769480 | tf_op jit(solution)/shard_map/ppermute | solution.py:44
  31.3 1.0 copy-done.3
  32.3 1.5 %collective-permute-start.5 = (bf16[400,768]{1,0:T(8,128)(2,1)S(1)}, bf16[400,768]{1,0:T(8,128)(2,1)}, u32[]{:S(2)}, u32[]{:S(2)}) collective-permute-start(bf16[400,768]{1,0:T(8,128)(2,1)S(1)} %get-tuple-element.9.own_ref.same_ref), channel_id=1, source_target_pairs={{0,384},{32,416},{128,0},{160,32},{256,128},{288,160},{384,256},{4... | collective-permute-start | bytes 1843208 | tf_op jit(solution)/shard_map/ppermute | solution.py:44
  34.2 2.4 %broadcast_select_fusion.2 = (bf16[400,768]{1,0:T(8,128)(2,1)}, bf16[400,768]{1,0:T(8,128)(2,1)S(1)}) fusion(bf16[400,768]{1,0:T(8,128)(2,1)} %collective-permute-done.1, bf16[400,768]{1,0:T(8,128)(2,1)} %collective-permute-done.4, pred[]{:T(512)S(6)} %eq.69, bf16[400,768]{1,0:T(8,128)(2,1)} %collective-permute-done.2, pred[]{:T(512)S(6)} %eq.68), kind=kLoop, calls=%fused_computation.11 | loop fusion | flops 614400 | bytes 3072002 | tf_op jit(solution)/shard_map/jit(_where)/select_n | solution.py:222
  36.6 7.2 %collective-permute-start.3 = (bf16[400,768]{1,0:T(8,128)(2,1)S(1)}, bf16[400,768]{1,0:T(8,128)(2,1)}, u32[]{:S(2)}, u32[]{:S(2)}) collective-permute-start(bf16[400,768]{1,0:T(8,128)(2,1)S(1)} %get-tuple-element.18.other_ref), channel_id=1, source_target_pairs={{0,16},{16,0},{32,48},{48,32},{64,80},{80,64},{96,112},{112,96},{1... | collective-permute-start | bytes 1843208 | tf_op jit(solution)/shard_map/ppermute | solution.py:44
  45.2 1.3 fusion.order_ref
  46.5 2.4 %shard_map.105.before_ref = f32[384,768]{1,0:T(8,128)S(1)} custom-call(f32[2]{0:T(128)S(1)} %pad_maximum_fusion.scalar_ref, bf16[400,768]{1,0:T(8,128)(2,1)S(1)} %get-tuple-element.9.own_ref.same_ref, bf16[384,128]{1,0:T(8,128)(2,1)S(1)} %convolution_convert_fusion.1.rows_ref, bf16[400,768]{1,0:T(8,128)(2,1)S(1)} %shard_map.104.same_ref.own_ref, ...), custom_call_target="tpu_custom_call" | custom-call | flops 981467136 | bytes 3121160 | tf_op jit(solution)/shard_map/pallas_call | solution.py:63
  48.9 1.5 %shard_map.106.before_ref = f32[384,768]{1,0:T(8,128)S(1)} custom-call(f32[2]{0:T(128)S(1)} %pad_maximum_fusion.scalar_ref, bf16[400,768]{1,0:T(8,128)(2,1)S(1)} %get-tuple-element.9.own_ref.same_ref, bf16[384,128]{1,0:T(8,128)(2,1)S(1)} %convolution_convert_fusion.1.rows_ref, bf16[400,768]{1,0:T(8,128)(2,1)S(1)} %get-tuple-element.18.other_ref, ...), custom_call_target="tpu_custom_call" | custom-call | flops 490733568 | bytes 3686408 | tf_op jit(solution)/shard_map/pallas_call | solution.py:63
  50.5 3.4 %shard_map.107 = (bf16[384,768]{1,0:T(8,128)(2,1)S(1)}, bf16[384,384]{1,0:T(8,128)(2,1)S(1)}, bf16[384,384]{1,0:T(8,128)(2,1)S(1)}) custom-call(f32[2]{0:T(128)S(1)} %pad_maximum_fusion.scalar_ref, bf16[400,768]{1,0:T(8,128)(2,1)S(1)} %get-tuple-element.9.own_ref.same_ref, bf16[384,128]{1,0:T(8,128)(2,1)S(1)} %convolution_convert_fusion.1.rows_ref, ...), custom_call_target="tpu_custom_call" | custom-call | flops 943718400 | bytes 6047240 | tf_op jit(solution)/shard_map/pallas_call | solution.py:63
  54.8 1.9 %collective-permute-start.10 = (bf16[384,384]{1,0:T(8,128)(2,1)S(1)}, bf16[384,384]{1,0:T(8,128)(2,1)S(1)}, u32[]{:S(2)}, u32[]{:S(2)}) collective-permute-start(bf16[384,384]{1,0:T(8,128)(2,1)S(1)} %get-tuple-element.14), channel_id=1, source_target_pairs={{0,16},{16,0},{32,48},{48,32},{64,80},{80,64},{96,112},{112,96},{1... | collective-permute-start | bytes 884744 | tf_op jit(solution)/shard_map/ppermute | solution.py:44
  56.7 2.1 %collective-permute-start.7 = (bf16[400,768]{1,0:T(8,128)(2,1)S(1)}, bf16[400,768]{1,0:T(8,128)(2,1)}, u32[]{:S(2)}, u32[]{:S(2)}) collective-permute-start(bf16[400,768]{1,0:T(8,128)(2,1)S(1)} %get-tuple-element.9.own_ref.same_ref), channel_id=1, source_target_pairs={{16,496},{32,0},{48,16},{64,32},{80,48},{96,64},{112,80},{144,112}... | collective-permute-start | bytes 1843208 | tf_op jit(solution)/shard_map/ppermute | solution.py:44
  58.8 6.2 %collective-permute-start.9 = (bf16[400,768]{1,0:T(8,128)(2,1)S(1)}, bf16[400,768]{1,0:T(8,128)(2,1)}, u32[]{:S(2)}, u32[]{:S(2)}) collective-permute-start(bf16[400,768]{1,0:T(8,128)(2,1)S(1)} %get-tuple-element.9.own_ref.same_ref), channel_id=1, source_target_pairs={{0,464},{16,0},{48,32},{64,16},{80,64},{96,48},{112,96},{128,80},{... | collective-permute-start | bytes 1843208 | tf_op jit(solution)/shard_map/ppermute | solution.py:44
  65.0 1.3 collective-permute-start.6
  66.3 2.8 %shard_map.112 = bf16[8,96,384]{2,1,0:T(8,128)(2,1)} custom-call(bf16[384,384]{1,0:T(8,128)(2,1)S(1)} %get-tuple-element.13.keep_ref, bf16[384,768]{1,0:T(8,128)(2,1)} %fusion.3.feat_ref, bf16[384,384]{1,0:T(8,128)(2,1)S(1)} %collective-permute-done.10.got_ref, bf16[384,768]{1,0:T(8,128)(2,1)} %collective-permute-done.11.feat_near_ref), custom_call_target="tpu_custom_call" | custom-call | flops 452984832 | bytes 2359296 | tf_op jit(solution)/shard_map/pallas_call | solution.py:63
  69.2 22.3 %all-to-all-start = ((bf16[8,96,384]{2,1,0:T(8,128)(2,1)}), bf16[8,96,384]{2,1,0:T(8,128)(2,1)}, u32[]{:S(2)}, u32[]{:S(2)}) async-start(bf16[8,96,384]{2,1,0:T(8,128)(2,1)} %shard_map.112), calls=%async_computation | async-start | bytes 1179648 | tf_op jit(solution)/shard_map/all_to_all | solution.py:52
  91.4 2.5 %collective-permute-done.6 = bf16[400,768]{1,0:T(8,128)(2,1)} collective-permute-done((bf16[400,768]{1,0:T(8,128)(2,1)}, bf16[400,768]{1,0:T(8,128)(2,1)}, u32[]{:S(2)}, u32[]{:S(2)}) %collective-permute-start.6) | collective-permute-done | bytes 614432 | tf_op jit(solution)/shard_map/ppermute | solution.py:44
  93.9 2.2 %broadcast_select_fusion = (bf16[400,768]{1,0:T(8,128)(2,1)}, bf16[400,768]{1,0:T(8,128)(2,1)S(1)}) fusion(bf16[400,768]{1,0:T(8,128)(2,1)} %collective-permute-done.6, bf16[400,768]{1,0:T(8,128)(2,1)} %collective-permute-done.9, pred[]{:T(512)S(6)} %eq.74, bf16[400,768]{1,0:T(8,128)(2,1)} %collective-permute-done.7, pred[]{:T(512)S(6)} %eq.73), kind=kLoop, calls=%fused_computation.9 | loop fusion | flops 614400 | bytes 3072002 | tf_op jit(solution)/shard_map/jit(_where)/select_n | solution.py:226
  96.1 1.9 %collective-permute-start.8 = (bf16[400,768]{1,0:T(8,128)(2,1)S(1)}, bf16[400,768]{1,0:T(8,128)(2,1)}, u32[]{:S(2)}, u32[]{:S(2)}) collective-permute-start(bf16[400,768]{1,0:T(8,128)(2,1)S(1)} %get-tuple-element.16.other_ref), channel_id=1, source_target_pairs={{0,16},{16,0},{32,48},{48,32},{64,80},{80,64},{96,112},{112,96},{1... | collective-permute-start | bytes 1843208 | tf_op jit(solution)/shard_map/ppermute | solution.py:44
  98.3 1.1 reduce_sum.21
  100.6 24.5 %all-to-all-start.1 = ((bf16[32,2,576]{2,1,0:T(2,128)(2,1)}), bf16[32,2,576]{2,1,0:T(2,128)(2,1)S(1)}, u32[]{:S(2)}, u32[]{:S(2)}) async-start(bf16[32,2,576]{2,1,0:T(2,128)(2,1)} %reshape.131), calls=%async_computation.1 | async-start | bytes 163840 | tf_op jit(solution)/shard_map/all_to_all | solution.py:52
  125.1 1.1 copy-done.5
  126.1 2.4 %shard_map.109.before_ref = f32[384,768]{1,0:T(8,128)S(1)} custom-call(f32[2]{0:T(128)S(1)} %pad_maximum_fusion.scalar_ref, bf16[400,768]{1,0:T(8,128)(2,1)S(1)} %shard_map.104.same_ref.own_ref, bf16[384,128]{1,0:T(8,128)(2,1)S(1)} %convolution_convert_fusion.rows_ref, bf16[400,768]{1,0:T(8,128)(2,1)S(1)} %get-tuple-element.9.own_ref.same_ref, ...), custom_call_target="tpu_custom_call" | custom-call | flops 981467136 | bytes 3121160 | tf_op jit(solution)/shard_map/pallas_call | solution.py:63
  128.5 1.6 %shard_map.110.before_ref = f32[384,768]{1,0:T(8,128)S(1)} custom-call(f32[2]{0:T(128)S(1)} %pad_maximum_fusion.scalar_ref, bf16[400,768]{1,0:T(8,128)(2,1)S(1)} %shard_map.104.same_ref.own_ref, bf16[384,128]{1,0:T(8,128)(2,1)S(1)} %convolution_convert_fusion.rows_ref, bf16[400,768]{1,0:T(8,128)(2,1)S(1)} %get-tuple-element.16.other_ref, ...), custom_call_target="tpu_custom_call" | custom-call | flops 490733568 | bytes 3686408 | tf_op jit(solution)/shard_map/pallas_call | solution.py:63
  130.1 1.5 %shard_map.108 = bf16[384,768]{1,0:T(8,128)(2,1)} custom-call(bf16[384,768]{1,0:T(8,128)(2,1)S(1)} %copy-done.9, bf16[768,768]{1,0:T(8,128)(2,1)S(1)} %copy-done), custom_call_target="tpu_custom_call" | custom-call | flops 452984832 | bytes 2359296 | tf_op jit(solution)/shard_map/pallas_call | solution.py:63
  131.6 3.1 %shard_map.111 = bf16[384,768]{1,0:T(8,128)(2,1)} custom-call(f32[2]{0:T(128)S(1)} %pad_maximum_fusion.scalar_ref, bf16[400,768]{1,0:T(8,128)(2,1)S(1)} %shard_map.104.same_ref.own_ref, bf16[384,128]{1,0:T(8,128)(2,1)S(1)} %convolution_convert_fusion.rows_ref, bf16[400,768]{1,0:T(8,128)(2,1)} %collective-permute-done.8.other_ref, ...), custom_call_target="tpu_custom_call" | custom-call | flops 490733568 | bytes 3686408 | tf_op jit(solution)/shard_map/pallas_call | solution.py:63
  134.8 2.5 %all-to-all-done.1 = bf16[32,2,576]{2,1,0:T(2,128)(2,1)S(1)} async-done(((bf16[32,2,576]{2,1,0:T(2,128)(2,1)}), bf16[32,2,576]{2,1,0:T(2,128)(2,1)S(1)}, u32[]{:S(2)}, u32[]{:S(2)}) %all-to-all-start.1) | async-done | bytes 73760 | tf_op jit(solution)/shard_map/all_to_all | solution.py:52
  (52 shorter events, 5.2 us)
Async XLA Ops:
  1.3 1.1 copy-start.1
  2.4 11.3 %copy-start.7 = (bf16[384,768]{1,0:T(8,128)(2,1)S(1)}, bf16[384,768]{1,0:T(8,128)(2,1)}, u32[]{:S(2)}) copy-start(bf16[384,768]{1,0:T(8,128)(2,1)} %feat_ref.1) | copy-start | bytes 1769476
  2.6 9.5 %collective-permute-start = (bf16[400,768]{1,0:T(8,128)(2,1)S(1)}, bf16[400,768]{1,0:T(8,128)(2,1)}, u32[]{:S(2)}, u32[]{:S(2)}) collective-permute-start(bf16[400,768]{1,0:T(8,128)(2,1)S(1)} %shard_map.104.same_ref.own_ref), channel_id=1, source_target_pairs={{80,208},{112,240},{208,336},{240,368},{336,464},{368,496},{464,80... | collective-permute-start | bytes 1843208 | tf_op jit(solution)/shard_map/ppermute | solution.py:44
  4.1 30.1 %collective-permute-start.2 = (bf16[400,768]{1,0:T(8,128)(2,1)S(1)}, bf16[400,768]{1,0:T(8,128)(2,1)}, u32[]{:S(2)}, u32[]{:S(2)}) collective-permute-start(bf16[400,768]{1,0:T(8,128)(2,1)S(1)} %shard_map.104.same_ref.own_ref), channel_id=1, source_target_pairs={{0,32},{16,48},{32,64},{48,80},{64,96},{80,112},{96,128},{128,160}... | collective-permute-start | bytes 1843208 | tf_op jit(solution)/shard_map/ppermute | solution.py:44
  10.1 24.1 %collective-permute-start.4 = (bf16[400,768]{1,0:T(8,128)(2,1)S(1)}, bf16[400,768]{1,0:T(8,128)(2,1)}, u32[]{:S(2)}, u32[]{:S(2)}) collective-permute-start(bf16[400,768]{1,0:T(8,128)(2,1)S(1)} %shard_map.104.same_ref.own_ref), channel_id=1, source_target_pairs={{0,16},{16,64},{32,48},{48,96},{64,80},{96,112},{112,160},{128,144... | collective-permute-start | bytes 1843208 | tf_op jit(solution)/shard_map/ppermute | solution.py:44
  12.1 18.5 %copy-start = (bf16[768,768]{1,0:T(8,128)(2,1)S(1)}, bf16[768,768]{1,0:T(8,128)(2,1)}, u32[]{:S(2)}) copy-start(bf16[768,768]{1,0:T(8,128)(2,1)} %head_ref.3) | copy-start | bytes 3538948
  12.1 22.1 %collective-permute-start.1 = (bf16[400,768]{1,0:T(8,128)(2,1)}, bf16[400,768]{1,0:T(8,128)(2,1)}, u32[]{:S(2)}, u32[]{:S(2)}) collective-permute-start(bf16[400,768]{1,0:T(8,128)(2,1)} %collective-permute-done), channel_id=1, source_target_pairs={{80,0},{112,16},{208,128},{240,144},{336,256},{368,272},{464,384},... | collective-permute-start | bytes 1843208 | tf_op jit(solution)/shard_map/ppermute | solution.py:44
  15.3 18.5 %copy-start.12 = (s32[109]{0:T(128)S(1)}, s32[109]{0:T(128)}, u32[]{:S(2)}) copy-start(s32[109]{0:T(128)} %param.13) | copy-start | bytes 1312
  15.3 18.5 %copy-start.10 = (s32[109,109]{1,0:T(8,128)S(1)}, s32[109,109]{1,0:T(8,128)}, u32[]{:S(2)}) copy-start(s32[109,109]{1,0:T(8,128)} %param.12) | copy-start | bytes 142576
  15.3 18.6 %copy-start.11 = (s32[384]{0:T(512)S(1)}, s32[384]{0:T(512)}, u32[]{:S(2)}) copy-start(s32[384]{0:T(512)} %param.11) | copy-start | bytes 4612
  15.3 51.0 %collective-permute-start.11 = (bf16[384,768]{1,0:T(8,128)(2,1)}, bf16[384,768]{1,0:T(8,128)(2,1)}, u32[]{:S(2)}, u32[]{:S(2)}) collective-permute-start(bf16[384,768]{1,0:T(8,128)(2,1)} %fusion.3.feat_ref), channel_id=1, source_target_pairs={{0,16},{16,0},{32,48},{48,32},{64,80},{80,64},{96,112},{112,96},{1... | collective-permute-start | bytes 1769480 | tf_op jit(solution)/shard_map/ppermute | solution.py:44
  31.3 1.0 copy-start.3
  32.3 32.7 %collective-permute-start.5 = (bf16[400,768]{1,0:T(8,128)(2,1)S(1)}, bf16[400,768]{1,0:T(8,128)(2,1)}, u32[]{:S(2)}, u32[]{:S(2)}) collective-permute-start(bf16[400,768]{1,0:T(8,128)(2,1)S(1)} %get-tuple-element.9.own_ref.same_ref), channel_id=1, source_target_pairs={{0,384},{32,416},{128,0},{160,32},{256,128},{288,160},{384,256},{4... | collective-permute-start | bytes 1843208 | tf_op jit(solution)/shard_map/ppermute | solution.py:44
  36.6 13.9 %collective-permute-start.3 = (bf16[400,768]{1,0:T(8,128)(2,1)S(1)}, bf16[400,768]{1,0:T(8,128)(2,1)}, u32[]{:S(2)}, u32[]{:S(2)}) collective-permute-start(bf16[400,768]{1,0:T(8,128)(2,1)S(1)} %get-tuple-element.18.other_ref), channel_id=1, source_target_pairs={{0,16},{16,0},{32,48},{48,32},{64,80},{80,64},{96,112},{112,96},{1... | collective-permute-start | bytes 1843208 | tf_op jit(solution)/shard_map/ppermute | solution.py:44
  45.2 1.4 copy-start.6
  48.9 1.6 %copy-start.4 = (f32[384,768]{1,0:T(8,128)S(1)}, f32[384,768]{1,0:T(8,128)}, u32[]{:S(2)}) copy-start(f32[384,768]{1,0:T(8,128)} %copy-done.3) | copy-start | bytes 3538948
  53.9 0.8 copy-start.8
  54.8 11.6 %collective-permute-start.10 = (bf16[384,384]{1,0:T(8,128)(2,1)S(1)}, bf16[384,384]{1,0:T(8,128)(2,1)S(1)}, u32[]{:S(2)}, u32[]{:S(2)}) collective-permute-start(bf16[384,384]{1,0:T(8,128)(2,1)S(1)} %get-tuple-element.14), channel_id=1, source_target_pairs={{0,16},{16,0},{32,48},{48,32},{64,80},{80,64},{96,112},{112,96},{1... | collective-permute-start | bytes 884744 | tf_op jit(solution)/shard_map/ppermute | solution.py:44
  56.7 34.7 %collective-permute-start.7 = (bf16[400,768]{1,0:T(8,128)(2,1)S(1)}, bf16[400,768]{1,0:T(8,128)(2,1)}, u32[]{:S(2)}, u32[]{:S(2)}) collective-permute-start(bf16[400,768]{1,0:T(8,128)(2,1)S(1)} %get-tuple-element.9.own_ref.same_ref), channel_id=1, source_target_pairs={{16,496},{32,0},{48,16},{64,32},{80,48},{96,64},{112,80},{144,112}... | collective-permute-start | bytes 1843208 | tf_op jit(solution)/shard_map/ppermute | solution.py:44
  58.8 32.6 %collective-permute-start.9 = (bf16[400,768]{1,0:T(8,128)(2,1)S(1)}, bf16[400,768]{1,0:T(8,128)(2,1)}, u32[]{:S(2)}, u32[]{:S(2)}) collective-permute-start(bf16[400,768]{1,0:T(8,128)(2,1)S(1)} %get-tuple-element.9.own_ref.same_ref), channel_id=1, source_target_pairs={{0,464},{16,0},{48,32},{64,16},{80,64},{96,48},{112,96},{128,80},{... | collective-permute-start | bytes 1843208 | tf_op jit(solution)/shard_map/ppermute | solution.py:44
  65.0 28.9 %collective-permute-start.6 = (bf16[400,768]{1,0:T(8,128)(2,1)}, bf16[400,768]{1,0:T(8,128)(2,1)}, u32[]{:S(2)}, u32[]{:S(2)}) collective-permute-start(bf16[400,768]{1,0:T(8,128)(2,1)} %collective-permute-done.5), channel_id=1, source_target_pairs={{0,96},{32,112},{128,224},{160,240},{256,352},{288,368},{384,480},... | collective-permute-start | bytes 1843208 | tf_op jit(solution)/shard_map/ppermute | solution.py:44
  69.2 29.1 %all-to-all-start = ((bf16[8,96,384]{2,1,0:T(8,128)(2,1)}), bf16[8,96,384]{2,1,0:T(8,128)(2,1)}, u32[]{:S(2)}, u32[]{:S(2)}) async-start(bf16[8,96,384]{2,1,0:T(8,128)(2,1)} %shard_map.112), calls=%async_computation | async-start | bytes 1179648 | tf_op jit(solution)/shard_map/all_to_all | solution.py:52
  96.1 35.5 %collective-permute-start.8 = (bf16[400,768]{1,0:T(8,128)(2,1)S(1)}, bf16[400,768]{1,0:T(8,128)(2,1)}, u32[]{:S(2)}, u32[]{:S(2)}) collective-permute-start(bf16[400,768]{1,0:T(8,128)(2,1)S(1)} %get-tuple-element.16.other_ref), channel_id=1, source_target_pairs={{0,16},{16,0},{32,48},{48,32},{64,80},{80,64},{96,112},{112,96},{1... | collective-permute-start | bytes 1843208 | tf_op jit(solution)/shard_map/ppermute | solution.py:44
  100.6 36.7 %all-to-all-start.1 = ((bf16[32,2,576]{2,1,0:T(2,128)(2,1)}), bf16[32,2,576]{2,1,0:T(2,128)(2,1)S(1)}, u32[]{:S(2)}, u32[]{:S(2)}) async-start(bf16[32,2,576]{2,1,0:T(2,128)(2,1)} %reshape.131), calls=%async_computation.1 | async-start | bytes 163840 | tf_op jit(solution)/shard_map/all_to_all | solution.py:52
  125.1 1.1 copy-start.5
  128.5 1.6 %copy-start.9 = (bf16[384,768]{1,0:T(8,128)(2,1)S(1)}, bf16[384,768]{1,0:T(8,128)(2,1)}, u32[]{:S(2)}) copy-start(bf16[384,768]{1,0:T(8,128)(2,1)} %copy-done.8) | copy-start | bytes 1769476
  130.1 1.5 %copy-start.2 = (bf16[384,768]{1,0:T(8,128)(2,1)S(1)}, bf16[384,768]{1,0:T(8,128)(2,1)}, u32[]{:S(2)}) copy-start(bf16[384,768]{1,0:T(8,128)(2,1)} %text_ref.3) | copy-start | bytes 1769476

commit v3 on v2

v3 whole, which is shorter than its diff:
```python
import jax
import jax.numpy as jnp
from jax import lax
from jax.experimental import pallas as pl
from jax.experimental.pallas import tpu as pltpu
from jax.sharding import PartitionSpec as P

D = 768
HALF = D // 2
ROWS = 384
TAIL = 16
LABELS = 128
N_BLK = 32
EPSILON = 1e-06
VMEM_BYTES = 20 * 1024 * 1024


def device_index(z_hi, x, core, z_lo, y):
    return ((z_hi * 4 + x) * 2 + core) * 16 + z_lo * 8 + y


NEAR_GROUPS = [
    [device_index(z, x, c, l, 2 * y_hi + y_lo) for x in range(4) for y_lo in range(2)]
    for z in range(4)
    for c in range(2)
    for l in range(2)
    for y_hi in range(4)
]
FAR_GROUPS = [
    [
        device_index(z, x, c, l, 2 * y_hi + y_lo)
        for z in range(4)
        for l in range(2)
        for y_hi in range(4)
    ]
    for x in range(4)
    for c in range(2)
    for y_lo in range(2)
]


def permute(value, target):
    pairs = [(i, target(i)) for i in range(N_BLK)]
    return lax.ppermute(value, "blk", [(i, j % N_BLK) for i, j in pairs if j is not None])


def swap_cores(value):
    return permute(value, lambda i: i ^ 1)


def exchange(value, groups):
    return lax.all_to_all(value, ("blk", "lane"), 0, 0, axis_index_groups=groups, tiled=True)


def dot(left, right, dims=((1,), (0,))):
    return lax.dot_general(left, right, (dims, ((), ())), preferred_element_type=jnp.float32)


def call(kernel, micros, outs, args, scalars=0, scratch=(), after=()):
    smem = pl.BlockSpec(memory_space=pltpu.SMEM)
    vmem = pl.BlockSpec(memory_space=pltpu.VMEM)
    anywhere = pl.BlockSpec(memory_space=pl.ANY)
    count, skipped = len(args), len(args) + len(after)

    def body(*refs):
        kernel(*refs[:count], *refs[skipped:])

    return pl.pallas_call(
        body,
        out_shape=outs,
        in_specs=[smem] * scalars + [vmem] * (count - scalars) + [anywhere] * len(after),
        out_specs=[vmem] * len(outs),
        scratch_shapes=scratch,
        cost_estimate=pl.CostEstimate(
            flops=int(micros * 1.1e9), bytes_accessed=int(micros * 3.0e6), transcendentals=0
        ),
        compiler_params=pltpu.CompilerParams(vmem_limit_bytes=VMEM_BYTES),
    )(*args, *after)


def array(shape, dtype):
    return jax.ShapeDtypeStruct(shape, dtype)


def put_langs(langs_ref, out_ref):
    langs = langs_ref[...].astype(jnp.float32)
    row = jnp.concatenate([langs, jnp.zeros((1, D - ROWS), jnp.float32)], axis=1)
    out_ref[ROWS:, :] = jnp.broadcast_to(row, (TAIL, D)).astype(jnp.bfloat16)


def text_kernel(text_ref, langs_ref, out_ref):
    text = text_ref[...].astype(jnp.float32)
    inverse = lax.rsqrt(jnp.sum(text * text, axis=-1, keepdims=True) + EPSILON)
    out_ref[:ROWS, :] = (text * inverse).astype(jnp.bfloat16)
    put_langs(langs_ref, out_ref)


def image_kernel(feat_ref, head_ref, langs_ref, out_ref, unit_ref, inv_ref):
    projected = dot(feat_ref[...], head_ref[...])
    inverse = lax.rsqrt(jnp.sum(projected * projected, axis=-1, keepdims=True) + EPSILON)
    unit = projected * inverse
    unit_ref[...] = unit
    inv_ref[...] = inverse
    out_ref[:ROWS, :] = unit.astype(jnp.bfloat16)
    put_langs(langs_ref, out_ref)


def pair_term(scale, bias, own, own_rows, other_ref, positive):
    other = other_ref[:ROWS, :]
    langs = other_ref[ROWS : ROWS + 1, :ROWS].astype(jnp.int32)
    hot = lax.broadcasted_iota(jnp.int32, (LABELS, ROWS), 0) == langs
    weight = dot(own_rows, hot.astype(jnp.float32).astype(jnp.bfloat16))
    logit = scale * dot(own, other, ((1,), (1,))) + bias
    excess = 0.5 + 0.5 * jnp.tanh(0.5 * logit)
    if positive:
        row = lax.broadcasted_iota(jnp.int32, (ROWS, ROWS), 0)
        column = lax.broadcasted_iota(jnp.int32, (ROWS, ROWS), 1)
        excess = jnp.where(row == column, excess - 1.0, excess)
    return dot((weight * excess).astype(jnp.bfloat16), other)


def own_kernel(
    scalar_ref, image_ref, image_rows_ref, text_ref, text_rows_ref, image_sum_ref, text_sum_ref
):
    scale, bias = scalar_ref[0], scalar_ref[1]
    image_sum_ref[...] = pair_term(
        scale, bias, image_ref[:ROWS, :], image_rows_ref[...], text_ref, True
    )
    text_sum_ref[...] = pair_term(
        scale, bias, text_ref[:ROWS, :], text_rows_ref[...], image_ref, True
    )


def middle_kernel(
    scalar_ref, own_ref, rows_ref, mix_ref, far_ref, near_ref, before_ref, sum_ref
):
    scale, bias = scalar_ref[0], scalar_ref[1]
    own, rows = own_ref[:ROWS, :], rows_ref[...]
    sum_ref[...] = before_ref[...]

    @pl.when(scalar_ref[4] == 0.0)
    def _():
        sum_ref[...] += pair_term(scale, bias, own, rows, mix_ref, False)

    @pl.when(scalar_ref[3] == 0.0)
    def _():
        sum_ref[...] += pair_term(scale, bias, own, rows, far_ref, False)

    @pl.when(scalar_ref[2] == 0.0)
    def _():
        sum_ref[...] += pair_term(scale, bias, own, rows, near_ref, False)


def last_sum(
    scalar_ref, own_ref, rows_ref, hop_ref, skip_ref, corner_ref, before_ref, block_ref, sum_ref
):
    scale, bias = scalar_ref[0], scalar_ref[1]
    sum_ref[...] = before_ref[...]

    @pl.when(scalar_ref[2] > 0.0)
    def _():
        block_ref[...] = corner_ref[...]

    @pl.when(scalar_ref[3] > 0.0)
    def _():
        block_ref[...] = hop_ref[...]

    @pl.when(scalar_ref[4] > 0.0)
    def _():
        block_ref[...] = skip_ref[...]

    @pl.when(scalar_ref[2] + scalar_ref[3] + scalar_ref[4] > 0.0)
    def _():
        own, rows = own_ref[:ROWS, :], rows_ref[...]
        sum_ref[...] += pair_term(scale, bias, own, rows, block_ref, False)

    return scale * sum_ref[...]


def image_last_kernel(
    scalar_ref, own_ref, rows_ref, hop_ref, skip_ref, corner_ref, before_ref, unit_ref, inv_ref,
    order_ref, dir_ref, keep_ref, send_ref, block_ref, sum_ref,
):
    grad = last_sum(
        scalar_ref, own_ref, rows_ref, hop_ref, skip_ref, corner_ref, before_ref, block_ref,
        sum_ref,
    )
    unit = unit_ref[...]
    radial = jnp.sum(unit * grad, axis=-1, keepdims=True)
    direction = ((grad - unit * radial) * inv_ref[...]).astype(jnp.bfloat16)
    dir_ref[...] = direction
    turned = dot(order_ref[...], direction, ((1,), (1,))).astype(jnp.bfloat16)
    keep_ref[...] = turned[:HALF, :]
    send_ref[...] = turned[HALF:, :]


def text_last_kernel(
    scalar_ref, own_ref, rows_ref, hop_ref, skip_ref, corner_ref, before_ref, text_ref, out_ref,
    block_ref, sum_ref,
):
    grad = last_sum(
        scalar_ref, own_ref, rows_ref, hop_ref, skip_ref, corner_ref, before_ref, block_ref,
        sum_ref,
    )
    text = text_ref[...].astype(jnp.float32)
    inverse = lax.rsqrt(jnp.sum(text * text, axis=-1, keepdims=True) + EPSILON)
    unit = text * inverse
    radial = jnp.sum(unit * grad, axis=-1, keepdims=True)
    out_ref[...] = ((grad - unit * radial) * inverse).astype(jnp.bfloat16)


def head_kernel(keep_ref, got_ref, feat_ref, out_ref, both_ref):
    both_ref[:, :ROWS] = keep_ref[...]
    both_ref[:, ROWS:] = got_ref[...]
    for y_lo in range(2):
        head = dot(both_ref[...], feat_ref[:, HALF * y_lo : HALF * y_lo + HALF])
        for x in range(4):
            out_ref[2 * x + y_lo] = head[96 * x : 96 * x + 96, :].astype(jnp.bfloat16)


def back_kernel(dir_ref, head_ref, out_ref):
    out_ref[...] = dot(dir_ref[...], head_ref[...], ((1,), (1,))).astype(jnp.bfloat16)


def column_order(core):
    new = jnp.arange(D, dtype=jnp.int32)
    side, x, z_hi, rest = new // 384, new // 96 % 4, new // 24 % 4, new % 24
    return z_hi * 192 + x * 48 + (side ^ core) * 24 + rest


def row_order():
    new = jnp.arange(D, dtype=jnp.int32)
    y_lo, z_lo, y_hi, rest = new // 384, new // 192 % 2, new // 48 % 4, new % 48
    return z_lo * 384 + (y_hi * 2 + y_lo) * 48 + rest


def order_matrix(old):
    return (old[:, None] == jnp.arange(D, dtype=jnp.int32)[None, :]).astype(jnp.bfloat16)


def on_device(
    image_feat, text_emb, head_weight, lang_ids, pair_mask, weight_codes, log_scale, logit_bias
):
    place = lax.axis_index("blk") % 8
    lang_count = pair_mask.shape[0]
    allowed = jnp.maximum(pair_mask, jnp.eye(lang_count, dtype=jnp.int32)).astype(jnp.float32)
    codes = weight_codes.astype(jnp.float32)
    table = (allowed * (0.25 * (codes[:, None] + codes[None, :]))).astype(jnp.bfloat16)
    extra = LABELS - lang_count
    table = jnp.pad(table, ((0, extra), (0, extra)))
    scale = jnp.exp(log_scale)
    text_scalars, image_scalars = [
        jnp.stack([scale, logit_bias] + [flag.astype(jnp.float32) for flag in flags])
        for flags in (
            [place == 0, place == 1, place == 2],
            [place == 7, place == 6, place == 5],
        )
    ]
    langs = lang_ids.reshape(1, ROWS)
    block = array((ROWS + TAIL, D), jnp.bfloat16)
    total = array((ROWS, D), jnp.float32)
    scratch = [pltpu.VMEM(block.shape, block.dtype), pltpu.VMEM(total.shape, total.dtype)]

    (text_out,) = call(text_kernel, 0.3, [block], (text_emb, langs))
    text_far = permute(text_out, lambda i: i + 2 if i % 8 != 7 else i - 6)
    text_mix = permute(
        text_out, lambda i: i + 1 if i % 2 == 0 else (i + 3 if i % 8 != 7 else i - 5)
    )

    image_out, image_unit, image_inv = call(
        image_kernel,
        1.0,
        [block, total, array((ROWS, 1), jnp.float32)],
        (image_feat, head_weight, langs),
    )
    image_far = permute(image_out, lambda i: i - 2 if i % 8 != 0 else i + 6)
    image_mix = permute(
        image_out, lambda i: i - 1 if i % 2 == 1 else (i - 3 if i % 8 != 0 else i + 5)
    )

    own_hot = (lang_ids[:, None] == jnp.arange(LABELS)[None, :]).astype(jnp.bfloat16)
    image_rows = dot(own_hot, table).astype(jnp.bfloat16)
    text_rows = dot(own_hot, table, ((1,), (1,))).astype(jnp.bfloat16)
    feat_turned = dot(image_feat, order_matrix(row_order()), ((1,), (1,))).astype(jnp.bfloat16)
    feat_near = swap_cores(feat_turned)
    feat_both = jnp.concatenate([feat_turned, feat_near], axis=0)
    order = order_matrix(column_order(place % 2))
    image_sum, text_sum = call(
        own_kernel,
        2.6,
        [total, total],
        (text_scalars, image_out, image_rows, text_out, text_rows),
        1,
    )
    text_far, text_mix, image_sum, text_sum, feat_both, order = lax.optimization_barrier(
        (text_far, text_mix, image_sum, text_sum, feat_both, order)
    )

    text_hop = permute(text_far, lambda i: {1: i + 8}.get(i % 8))
    text_near = permute(text_far, lambda i: i ^ 1 if i % 8 != 1 else None)
    text_skip = permute(text_mix, lambda i: {2: i + 8}.get(i % 8))
    image_hop = permute(image_far, lambda i: {6: i - 8}.get(i % 8))
    image_near = permute(image_far, lambda i: i ^ 1 if i % 8 != 6 else None)
    image_skip = permute(image_mix, lambda i: {5: i - 8}.get(i % 8))
    (image_sum,) = call(
        middle_kernel,
        4.0,
        [total],
        (text_scalars, image_out, image_rows, text_mix, text_far, text_near, image_sum),
        1,
        (),
        (image_far, image_mix),
    )
    text_hop, text_skip, image_sum = lax.optimization_barrier((text_hop, text_skip, image_sum))
    text_corner = permute(text_hop, lambda i: {1: i - 1}.get(i % 8))
    half = array((HALF, ROWS), jnp.bfloat16)
    image_dir, keep, send = call(
        image_last_kernel,
        3.0,
        [array((ROWS, D), jnp.bfloat16), half, half],
        (
            text_scalars, image_out, image_rows, text_hop, text_skip, text_corner, image_sum,
            image_unit, image_inv, order,
        ),
        1,
        scratch,
        (image_hop, image_near, image_skip),
    )
    got = swap_cores(send)
    (head,) = call(
        head_kernel,
        1.5,
        [array((8, 96, HALF), jnp.bfloat16)],
        (keep, got, feat_both),
        0,
        [pltpu.VMEM((HALF, D), jnp.bfloat16)],
    )
    head = exchange(head, NEAR_GROUPS)
    image_corner = permute(image_hop, lambda i: {6: i + 1}.get(i % 8))
    head = jnp.sum(head.astype(jnp.float32), axis=0).astype(jnp.bfloat16)
    head = jnp.swapaxes(head.reshape(4, 24, 8, 48), 1, 2).reshape(32, 24, 48)
    head = exchange(head, FAR_GROUPS)
    head_grad = jnp.sum(head.astype(jnp.float32), axis=0).T

    (image_back,) = call(
        back_kernel, 1.5, [array((ROWS, D), jnp.bfloat16)], (image_dir, head_weight)
    )
    (text_sum,) = call(
        middle_kernel,
        4.0,
        [total],
        (image_scalars, text_out, text_rows, image_mix, image_far, image_near, text_sum),
        1,
    )
    (text_back,) = call(
        text_last_kernel,
        3.0,
        [array((ROWS, D), jnp.bfloat16)],
        (
            image_scalars, text_out, text_rows, image_hop, image_skip, image_corner, text_sum,
            text_emb,
        ),
        1,
        scratch,
    )
    return (image_back, text_back, head_grad)


def solution(mesh):
    in_specs = (
        P(("blk", "lane"), None),
        P(("blk", "lane"), None),
        P(),
        P(("blk", "lane")),
        P(),
        P(),
        P(),
        P(),
    )
    out_specs = (P(("blk", "lane"), None), P(("blk", "lane"), None), P("lane", "blk"))
    return jax.shard_map(
        on_device, mesh=mesh, in_specs=in_specs, out_specs=out_specs, check_vma=False
    )
```

time: 139 us -> 120 us (0.86)
  starting transfers between devices: 95.1 us -> 51.1 us
  waiting for transfers between devices: 4.98 us -> 29.1 us
  other arithmetic: 8.56 us -> 4 us
  Pallas kernels: 19.7 us -> 22.2 us
  local copies, waits for them, and re-layouts: 5.36 us -> 7.64 us
    all_to_all x2, starting transfers between devices: 46.7 us -> 15.9 us  [exchange(): lax.all_to_all(value, ('blk', 'lane'), 0, 0, axis_index_groups=groups, ti...]
    ppermute x12 -> x14, waiting for transfers between devices: 2.51 us -> 18.2 us  [permute(): lax.ppermute(value, 'blk', [(i, j % N_BLK) for i, j in pairs if j is not...]
    ppermute x12 -> x14, starting transfers between devices: 48.4 us -> 35.2 us  [permute(): lax.ppermute(value, 'blk', [(i, j % N_BLK) for i, j in pairs if j is not...]
    all_to_all x2, waiting for transfers between devices: 2.48 us -> 10.9 us  [exchange(): lax.all_to_all(value, ('blk', 'lane'), 0, 0, axis_index_groups=groups, ti...]
    select_n x2 -> x0, other arithmetic: 4.6 us -> none  [the longest x1 2.39 us: on_device(): text_mix = jnp.where(place == 0, text_hop, text_mix)]
    pallas_call x10 -> x9, Pallas kernels: 19.7 us -> 22.2 us  [call(): pl.pallas_call(body, out_shape=outs, in_specs=[smem] * scalars + [vmem] *...]
    concatenate x0 -> x1, other arithmetic: none -> 1.75 us  [on_device(): feat_both = jnp.concatenate([feat_turned, feat_near], axis=0)]
    unnamed x28 -> x40, local copies, waits for them, and re-layouts: 5.13 us -> 6.47 us
  transfers between devices with their start and end apart: 14 -> 16, of which waited for: 2 -> 4; matrix products, arithmetic and copies ran while one was open for 8% -> 4% of each run, Pallas kernels for 14% -> 15%
where the time goes in v3:
time: 120 us; the launch traced here: 119 us
  starting transfers between devices  51.1 us (43%)
  waiting for transfers between devices  29.1 us (24%)
  Pallas kernels  22.2 us (18%)
  local copies, waits for them, and re-layouts  7.64 us (6%)
  other arithmetic  4 us (3%)
  between operations  2.46 us (2%)
  matrix products  2.05 us (2%)
    ppermute x14, starting transfers between devices, permute(): lax.ppermute(value, 'blk', [(i, j % N_BLK) for i, j in pairs if j is not...  35.2 us
    pallas_call x9, Pallas kernels, call(): pl.pallas_call(body, out_shape=outs, in_specs=[smem] * scalars + [vmem] *...  22.2 us
    ppermute x14, waiting for transfers between devices, permute(): lax.ppermute(value, 'blk', [(i, j % N_BLK) for i, j in pairs if j is not...  18.2 us
    all_to_all x2, starting transfers between devices, exchange(): lax.all_to_all(value, ('blk', 'lane'), 0, 0, axis_index_groups=groups, ti...  15.9 us
    all_to_all x2, waiting for transfers between devices, exchange(): lax.all_to_all(value, ('blk', 'lane'), 0, 0, axis_index_groups=groups, ti...  10.9 us
    unnamed x40, local copies, waits for them, and re-layouts  6.47 us
  transfers between devices with their start and end apart: 16, of which 4 were waited for; matrix products, arithmetic and copies ran while one was open for 4% of the time, Pallas kernels for 15%

profile of v3, /device:TPU:6, one launch (start us, length us, event | category | flops | bytes accessed | tf_op | source)
XLA Modules:
  0.0 118.5 jit_solution(11774621502964099438)
XLA Ops:
  1.4 1.1 copy-done.8
  2.7 6.0 %collective-permute-start = (bf16[400,768]{1,0:T(8,128)(2,1)S(1)}, bf16[400,768]{1,0:T(8,128)(2,1)}, u32[]{:S(2)}, u32[]{:S(2)}) collective-permute-start(bf16[400,768]{1,0:T(8,128)(2,1)S(1)} %shard_map.104.refs_3_.refs_1_), channel_id=1, source_target_pairs={{0,32},{16,48},{32,64},{48,80},{64,96},{80,112},{96,128},{112,16},... | collective-permute-start | bytes 1843208 | tf_op jit(solution)/shard_map/ppermute | solution.py:44
  8.7 1.9 %collective-permute-start.1 = (bf16[400,768]{1,0:T(8,128)(2,1)S(1)}, bf16[400,768]{1,0:T(8,128)(2,1)}, u32[]{:S(2)}, u32[]{:S(2)}) collective-permute-start(bf16[400,768]{1,0:T(8,128)(2,1)S(1)} %shard_map.104.refs_3_.refs_1_), channel_id=1, source_target_pairs={{0,16},{16,64},{32,48},{48,96},{64,80},{80,128},{96,112},{112,32},... | collective-permute-start | bytes 1843208 | tf_op jit(solution)/shard_map/ppermute | solution.py:44
  10.7 1.1 copy-done.7
  11.7 1.6 %shard_map.103 = (bf16[400,768]{1,0:T(8,128)(2,1)}, f32[384,768]{1,0:T(8,128)S(1)}, f32[384,1]{1,0:T(8,128)S(1)}) custom-call(bf16[384,768]{1,0:T(8,128)(2,1)S(1)} %copy-done.7, bf16[768,768]{1,0:T(8,128)(2,1)S(1)} %copy-done, s32[1,384]{1,0:T(1,128)S(1)} %reshape.132.refs_2_.refs_1_), custom_call_target="tpu_custom_call" | custom-call | flops 1100000000 | bytes 3000000 | tf_op jit(solution)/shard_map/pallas_call | solution.py:68
  13.3 1.9 %collective-permute-start.6 = (bf16[400,768]{1,0:T(8,128)(2,1)}, bf16[400,768]{1,0:T(8,128)(2,1)}, u32[]{:S(2)}, u32[]{:S(2)}) collective-permute-start(bf16[400,768]{1,0:T(8,128)(2,1)} %get-tuple-element.20.refs_1_), channel_id=1, source_target_pairs={{0,96},{16,496},{32,0},{48,16},{64,32},{80,48},{96,64},{112,80},{1... | collective-permute-start | bytes 1843208 | tf_op jit(solution)/shard_map/ppermute | solution.py:44
  15.2 5.2 %collective-permute-start.7 = (bf16[400,768]{1,0:T(8,128)(2,1)}, bf16[400,768]{1,0:T(8,128)(2,1)}, u32[]{:S(2)}, u32[]{:S(2)}) collective-permute-start(bf16[400,768]{1,0:T(8,128)(2,1)} %get-tuple-element.20.refs_1_), channel_id=1, source_target_pairs={{0,80},{16,0},{32,496},{48,32},{64,16},{80,64},{96,48},{112,96},{1... | collective-permute-start | bytes 1843208 | tf_op jit(solution)/shard_map/ppermute | solution.py:44
  20.4 1.6 %fusion.3 = bf16[384,768]{1,0:T(8,128)(2,1)} fusion(bf16[384,768]{1,0:T(8,128)(2,1)S(1)} %copy-done.7, s32[768]{0:T(1024)S(1)} %fusion.24), kind=kOutput, calls=%fused_computation.5 | convolution fusion | flops 453869568 | bytes 1182720 | tf_op jit(solution)/shard_map/dot_general | solution.py:56
  22.0 2.0 %collective-permute-start.2 = (bf16[384,768]{1,0:T(8,128)(2,1)}, bf16[384,768]{1,0:T(8,128)(2,1)}, u32[]{:S(2)}, u32[]{:S(2)}) collective-permute-start(bf16[384,768]{1,0:T(8,128)(2,1)} %fusion.3), channel_id=1, source_target_pairs={{0,16},{16,0},{32,48},{48,32},{64,80},{80,64},{96,112},{112,96},{1... | collective-permute-start | bytes 1769480 | tf_op jit(solution)/shard_map/ppermute | solution.py:44
  26.4 2.8 %shard_map.105 = (f32[384,768]{1,0:T(8,128)S(1)}, f32[384,768]{1,0:T(8,128)S(1)}) custom-call(f32[5]{0:T(128)S(1)} %stack.58.refs_0_, bf16[400,768]{1,0:T(8,128)(2,1)} %get-tuple-element.20.refs_1_, bf16[384,128]{1,0:T(8,128)(2,1)S(1)} %convolution_convert_fusion.1.refs_2_, bf16[400,768]{1,0:T(8,128)(2,1)S(1)} %shard_map.104.refs_3_.refs_1_, ...), custom_call_target="tpu_custom_call" | custom-call | flops 2860000000 | bytes 7800000 | tf_op jit(solution)/shard_map/pallas_call | solution.py:68
  29.3 1.7 %pad_maximum_fusion.refs_2_ = bf16[768,768]{1,0:T(8,128)(2,1)S(1)} fusion(bf16[384,768]{1,0:T(8,128)(2,1)} %collective-permute-done.2, bf16[384,768]{1,0:T(8,128)(2,1)} %fusion.3), kind=kLoop, calls=%fused_computation.6 | loop fusion | flops 2359296 | bytes 2359296 | tf_op jit(solution)/shard_map/concatenate | solution.py:286
  31.0 2.5 %collective-permute-start.5 = (bf16[400,768]{1,0:T(8,128)(2,1)}, bf16[400,768]{1,0:T(8,128)(2,1)S(1)}, u32[]{:S(2)}, u32[]{:S(2)}) collective-permute-start(bf16[400,768]{1,0:T(8,128)(2,1)} %collective-permute-done.refs_4_), channel_id=1, source_target_pairs={{0,16},{32,48},{48,32},{64,80},{80,64},{96,112},{112,96},{128,144}... | collective-permute-start | bytes 1843208 | tf_op jit(solution)/shard_map/ppermute | solution.py:44
  35.0 6.5 %collective-permute-done.6.refs_7_.refs_4_ = bf16[400,768]{1,0:T(8,128)(2,1)} collective-permute-done((bf16[400,768]{1,0:T(8,128)(2,1)}, bf16[400,768]{1,0:T(8,128)(2,1)}, u32[]{:S(2)}, u32[]{:S(2)}) %collective-permute-start.6) | collective-permute-done | bytes 614432 | tf_op jit(solution)/shard_map/ppermute | solution.py:44
  41.5 7.3 %collective-permute-start.9 = (bf16[400,768]{1,0:T(8,128)(2,1)}, bf16[400,768]{1,0:T(8,128)(2,1)S(1)}, u32[]{:S(2)}, u32[]{:S(2)}) collective-permute-start(bf16[400,768]{1,0:T(8,128)(2,1)} %collective-permute-done.6.refs_7_.refs_4_), channel_id=1, source_target_pairs={{96,480},{224,96},{352,224},{480,352},{97,481},{225,97},{353,225},... | collective-permute-start | bytes 1843208 | tf_op jit(solution)/shard_map/ppermute | solution.py:44
  48.8 1.3 %collective-permute-start.10 = (bf16[400,768]{1,0:T(8,128)(2,1)}, bf16[400,768]{1,0:T(8,128)(2,1)S(1)}, u32[]{:S(2)}, u32[]{:S(2)}) collective-permute-start(bf16[400,768]{1,0:T(8,128)(2,1)} %collective-permute-done.6.refs_7_.refs_4_), channel_id=1, source_target_pairs={{0,16},{16,0},{32,48},{48,32},{64,80},{80,64},{112,96},{128,144},{... | collective-permute-start | bytes 1843208 | tf_op jit(solution)/shard_map/ppermute | solution.py:44
  50.9 4.6 %shard_map.106.refs_6_ = f32[384,768]{1,0:T(8,128)S(1)} custom-call(f32[5]{0:T(128)S(1)} %stack.58.refs_0_, bf16[400,768]{1,0:T(8,128)(2,1)} %get-tuple-element.20.refs_1_, bf16[384,128]{1,0:T(8,128)(2,1)S(1)} %convolution_convert_fusion.1.refs_2_, bf16[400,768]{1,0:T(8,128)(2,1)} %collective-permute-done.1.refs_3_, ...), custom_call_target="tpu_custom_call" | custom-call | flops 4400000000 | bytes 12000000 | tf_op jit(solution)/shard_map/pallas_call | solution.py:68
  56.2 10.1 %collective-permute-done.9.refs_10_.refs_3_ = bf16[400,768]{1,0:T(8,128)(2,1)S(1)} collective-permute-done((bf16[400,768]{1,0:T(8,128)(2,1)}, bf16[400,768]{1,0:T(8,128)(2,1)S(1)}, u32[]{:S(2)}, u32[]{:S(2)}) %collective-permute-start.9) | collective-permute-done | bytes 614432 | tf_op jit(solution)/shard_map/ppermute | solution.py:44
  66.3 2.8 %shard_map.107 = (bf16[384,768]{1,0:T(8,128)(2,1)S(1)}, bf16[384,384]{1,0:T(8,128)(2,1)S(1)}, bf16[384,384]{1,0:T(8,128)(2,1)S(1)}) custom-call(f32[5]{0:T(128)S(1)} %stack.58.refs_0_, bf16[400,768]{1,0:T(8,128)(2,1)} %get-tuple-element.20.refs_1_, bf16[384,128]{1,0:T(8,128)(2,1)S(1)} %convolution_convert_fusion.1.refs_2_, ...), custom_call_target="tpu_custom_call" | custom-call | flops 3300000000 | bytes 9000000 | tf_op jit(solution)/shard_map/pallas_call | solution.py:68
  69.9 1.9 %collective-permute-start.13 = (bf16[384,384]{1,0:T(8,128)(2,1)S(1)}, bf16[384,384]{1,0:T(8,128)(2,1)S(1)}, u32[]{:S(2)}, u32[]{:S(2)}) collective-permute-start(bf16[384,384]{1,0:T(8,128)(2,1)S(1)} %get-tuple-element.35), channel_id=1, source_target_pairs={{0,16},{16,0},{32,48},{48,32},{64,80},{80,64},{96,112},{112,96},{1... | collective-permute-start | bytes 884744 | tf_op jit(solution)/shard_map/ppermute | solution.py:44
  71.8 1.5 %collective-permute-done.13.refs_1_ = bf16[384,384]{1,0:T(8,128)(2,1)S(1)} collective-permute-done((bf16[384,384]{1,0:T(8,128)(2,1)S(1)}, bf16[384,384]{1,0:T(8,128)(2,1)S(1)}, u32[]{:S(2)}, u32[]{:S(2)}) %collective-permute-start.13) | collective-permute-done | bytes 294944 | tf_op jit(solution)/shard_map/ppermute | solution.py:44
  73.4 1.6 %shard_map.111 = bf16[8,96,384]{2,1,0:T(8,128)(2,1)} custom-call(bf16[384,384]{1,0:T(8,128)(2,1)S(1)} %get-tuple-element.34.refs_0_, bf16[384,384]{1,0:T(8,128)(2,1)S(1)} %collective-permute-done.13.refs_1_, bf16[768,768]{1,0:T(8,128)(2,1)S(1)} %pad_maximum_fusion.refs_2_), custom_call_target="tpu_custom_call" | custom-call | flops 1650000000 | bytes 4500000 | tf_op jit(solution)/shard_map/pallas_call | solution.py:68
  75.0 5.7 %all-to-all-start = ((bf16[8,96,384]{2,1,0:T(8,128)(2,1)}), bf16[8,96,384]{2,1,0:T(8,128)(2,1)}, u32[]{:S(2)}, u32[]{:S(2)}) async-start(bf16[8,96,384]{2,1,0:T(8,128)(2,1)} %shard_map.111), calls=%async_computation | async-start | bytes 1179648 | tf_op jit(solution)/shard_map/all_to_all | solution.py:52
  80.7 2.3 %collective-permute-start.12 = (bf16[400,768]{1,0:T(8,128)(2,1)S(1)}, bf16[400,768]{1,0:T(8,128)(2,1)}, u32[]{:S(2)}, u32[]{:S(2)}) collective-permute-start(bf16[400,768]{1,0:T(8,128)(2,1)S(1)} %copy-done.2), channel_id=1, source_target_pairs={{96,112},{224,240},{352,368},{480,496},{97,113},{225,241},{353,369... | collective-permute-start | bytes 1843208 | tf_op jit(solution)/shard_map/ppermute | solution.py:44
  83.1 1.1 copy-done.6
  84.2 1.3 %copy-done.15 = f32[384,768]{1,0:T(8,128)S(1)} copy-done((f32[384,768]{1,0:T(8,128)S(1)}, f32[384,768]{1,0:T(8,128)}, u32[]{:S(2)}) %copy-start.15) | copy-done | bytes 1179672
  85.4 3.7 %shard_map.109.refs_6_ = f32[384,768]{1,0:T(8,128)S(1)} custom-call(f32[5]{0:T(128)S(1)} %stack.65.refs_0_, bf16[400,768]{1,0:T(8,128)(2,1)S(1)} %shard_map.104.refs_3_.refs_1_, bf16[384,128]{1,0:T(8,128)(2,1)S(1)} %convolution_convert_fusion.refs_4_.refs_2_, bf16[400,768]{1,0:T(8,128)(2,1)} %collective-permute-done.7.refs_8_.refs_3_, ...), custom_call_target="tpu_custom_call" | custom-call | flops 4400000000 | bytes 12000000 | tf_op jit(solution)/shard_map/pallas_call | solution.py:68
  89.2 3.5 %shard_map.110 = bf16[384,768]{1,0:T(8,128)(2,1)} custom-call(f32[5]{0:T(128)S(1)} %stack.65.refs_0_, bf16[400,768]{1,0:T(8,128)(2,1)S(1)} %shard_map.104.refs_3_.refs_1_, bf16[384,128]{1,0:T(8,128)(2,1)S(1)} %convolution_convert_fusion.refs_4_.refs_2_, bf16[400,768]{1,0:T(8,128)(2,1)S(1)} %copy-done.2, bf16[400,768]{1,0:T(8,128)(2,1)S(1)} %copy-done.4, ...), custom_call_target="tpu_custom_call" | custom-call | flops 3300000000 | bytes 9000000 | tf_op jit(solution)/shard_map/pallas_call | solution.py:68
  92.6 1.2 %reduce_sum.21 = bf16[96,384]{1,0:T(8,128)(2,1)S(1)} reduce(bf16[8,96,384]{2,1,0:T(8,128)(2,1)} %all-to-all-done, bf16[]{:T(256)} %constant.112.clone.1), dimensions={0}, to_apply=%region_0.1 | reduce | flops 258048 | bytes 663554 | tf_op jit(solution)/shard_map/reduce_sum | solution.py:340
  94.1 0.9 reshape.141
  95.0 10.2 %all-to-all-start.1 = ((bf16[32,2,576]{2,1,0:T(2,128)(2,1)}), bf16[32,2,576]{2,1,0:T(2,128)(2,1)S(1)}, u32[]{:S(2)}, u32[]{:S(2)}) async-start(bf16[32,2,576]{2,1,0:T(2,128)(2,1)} %reshape.141), calls=%async_computation.1 | async-start | bytes 163840 | tf_op jit(solution)/shard_map/all_to_all | solution.py:52
  105.3 1.5 %shard_map.108 = bf16[384,768]{1,0:T(8,128)(2,1)} custom-call(bf16[384,768]{1,0:T(8,128)(2,1)S(1)} %copy-done.13, bf16[768,768]{1,0:T(8,128)(2,1)S(1)} %copy-done), custom_call_target="tpu_custom_call" | custom-call | flops 1650000000 | bytes 4500000 | tf_op jit(solution)/shard_map/pallas_call | solution.py:68
  106.7 10.9 %all-to-all-done.1 = bf16[32,2,576]{2,1,0:T(2,128)(2,1)S(1)} async-done(((bf16[32,2,576]{2,1,0:T(2,128)(2,1)}), bf16[32,2,576]{2,1,0:T(2,128)(2,1)S(1)}, u32[]{:S(2)}, u32[]{:S(2)}) %all-to-all-start.1) | async-done | bytes 73760 | tf_op jit(solution)/shard_map/all_to_all | solution.py:52
  (65 shorter events, 6.8 us)
Async XLA Ops:
  0.6 10.0 %copy-start = (bf16[768,768]{1,0:T(8,128)(2,1)S(1)}, bf16[768,768]{1,0:T(8,128)(2,1)}, u32[]{:S(2)}) copy-start(bf16[768,768]{1,0:T(8,128)(2,1)} %refs_1_.3) | copy-start | bytes 3538948
  2.7 28.3 %collective-permute-start = (bf16[400,768]{1,0:T(8,128)(2,1)S(1)}, bf16[400,768]{1,0:T(8,128)(2,1)}, u32[]{:S(2)}, u32[]{:S(2)}) collective-permute-start(bf16[400,768]{1,0:T(8,128)(2,1)S(1)} %shard_map.104.refs_3_.refs_1_), channel_id=1, source_target_pairs={{0,32},{16,48},{32,64},{48,80},{64,96},{80,112},{96,128},{112,16},... | collective-permute-start | bytes 1843208 | tf_op jit(solution)/shard_map/ppermute | solution.py:44
  8.7 22.3 %collective-permute-start.1 = (bf16[400,768]{1,0:T(8,128)(2,1)S(1)}, bf16[400,768]{1,0:T(8,128)(2,1)}, u32[]{:S(2)}, u32[]{:S(2)}) collective-permute-start(bf16[400,768]{1,0:T(8,128)(2,1)S(1)} %shard_map.104.refs_3_.refs_1_), channel_id=1, source_target_pairs={{0,16},{16,64},{32,48},{48,96},{64,80},{80,128},{96,112},{112,32},... | collective-permute-start | bytes 1843208 | tf_op jit(solution)/shard_map/ppermute | solution.py:44
  13.3 8.7 %copy-start.10 = (f32[384,768]{1,0:T(8,128)}, f32[384,768]{1,0:T(8,128)S(1)}, u32[]{:S(2)}) copy-start(f32[384,768]{1,0:T(8,128)S(1)} %get-tuple-element.29.refs_7_) | copy-start | bytes 3538948
  13.3 28.2 %collective-permute-start.6 = (bf16[400,768]{1,0:T(8,128)(2,1)}, bf16[400,768]{1,0:T(8,128)(2,1)}, u32[]{:S(2)}, u32[]{:S(2)}) collective-permute-start(bf16[400,768]{1,0:T(8,128)(2,1)} %get-tuple-element.20.refs_1_), channel_id=1, source_target_pairs={{0,96},{16,496},{32,0},{48,16},{64,32},{80,48},{96,64},{112,80},{1... | collective-permute-start | bytes 1843208 | tf_op jit(solution)/shard_map/ppermute | solution.py:44
  15.2 33.6 %collective-permute-start.7 = (bf16[400,768]{1,0:T(8,128)(2,1)}, bf16[400,768]{1,0:T(8,128)(2,1)}, u32[]{:S(2)}, u32[]{:S(2)}) collective-permute-start(bf16[400,768]{1,0:T(8,128)(2,1)} %get-tuple-element.20.refs_1_), channel_id=1, source_target_pairs={{0,80},{16,0},{32,496},{48,32},{64,16},{80,64},{96,48},{112,96},{1... | collective-permute-start | bytes 1843208 | tf_op jit(solution)/shard_map/ppermute | solution.py:44
  20.4 3.7 %copy-start.18 = (s32[109]{0:T(128)S(1)}, s32[109]{0:T(128)}, u32[]{:S(2)}) copy-start(s32[109]{0:T(128)} %param.13) | copy-start | bytes 1312
  22.0 2.4 %copy-start.16 = (s32[109,109]{1,0:T(8,128)S(1)}, s32[109,109]{1,0:T(8,128)}, u32[]{:S(2)}) copy-start(s32[109,109]{1,0:T(8,128)} %param.12) | copy-start | bytes 142576
  22.0 2.5 %copy-start.17 = (s32[384]{0:T(512)S(1)}, s32[384]{0:T(512)}, u32[]{:S(2)}) copy-start(s32[384]{0:T(512)} %param.11) | copy-start | bytes 4612
  22.0 7.2 %collective-permute-start.2 = (bf16[384,768]{1,0:T(8,128)(2,1)}, bf16[384,768]{1,0:T(8,128)(2,1)}, u32[]{:S(2)}, u32[]{:S(2)}) collective-permute-start(bf16[384,768]{1,0:T(8,128)(2,1)} %fusion.3), channel_id=1, source_target_pairs={{0,16},{16,0},{32,48},{48,32},{64,80},{80,64},{96,112},{112,96},{1... | collective-permute-start | bytes 1769480 | tf_op jit(solution)/shard_map/ppermute | solution.py:44
  29.2 1.8 %copy-start.14 = (f32[384,768]{1,0:T(8,128)}, f32[384,768]{1,0:T(8,128)S(1)}, u32[]{:S(2)}) copy-start(f32[384,768]{1,0:T(8,128)S(1)} %get-tuple-element.33.refs_6_) | copy-start | bytes 3538948
  31.0 35.3 %copy-start.11 = (f32[384,768]{1,0:T(8,128)S(1)}, f32[384,768]{1,0:T(8,128)}, u32[]{:S(2)}) copy-start(f32[384,768]{1,0:T(8,128)} %copy-done.10) | copy-start | bytes 3538948
  31.0 19.1 %collective-permute-start.5 = (bf16[400,768]{1,0:T(8,128)(2,1)}, bf16[400,768]{1,0:T(8,128)(2,1)S(1)}, u32[]{:S(2)}, u32[]{:S(2)}) collective-permute-start(bf16[400,768]{1,0:T(8,128)(2,1)} %collective-permute-done.refs_4_), channel_id=1, source_target_pairs={{0,16},{32,48},{48,32},{64,80},{80,64},{96,112},{112,96},{128,144}... | collective-permute-start | bytes 1843208 | tf_op jit(solution)/shard_map/ppermute | solution.py:44
  33.6 21.9 %collective-permute-start.3 = (bf16[400,768]{1,0:T(8,128)(2,1)}, bf16[400,768]{1,0:T(8,128)(2,1)S(1)}, u32[]{:S(2)}, u32[]{:S(2)}) collective-permute-start(bf16[400,768]{1,0:T(8,128)(2,1)} %collective-permute-done.refs_4_), channel_id=1, source_target_pairs={{16,144},{144,272},{272,400},{400,16},{17,145},{145,273},{273,401}... | collective-permute-start | bytes 1843208 | tf_op jit(solution)/shard_map/ppermute | solution.py:44
  34.3 21.2 %collective-permute-start.4 = (bf16[400,768]{1,0:T(8,128)(2,1)}, bf16[400,768]{1,0:T(8,128)(2,1)S(1)}, u32[]{:S(2)}, u32[]{:S(2)}) collective-permute-start(bf16[400,768]{1,0:T(8,128)(2,1)} %collective-permute-done.1.refs_3_), channel_id=1, source_target_pairs={{32,160},{160,288},{288,416},{416,32},{33,161},{161,289},{289,417}... | collective-permute-start | bytes 1843208 | tf_op jit(solution)/shard_map/ppermute | solution.py:44
  41.5 24.7 %collective-permute-start.9 = (bf16[400,768]{1,0:T(8,128)(2,1)}, bf16[400,768]{1,0:T(8,128)(2,1)S(1)}, u32[]{:S(2)}, u32[]{:S(2)}) collective-permute-start(bf16[400,768]{1,0:T(8,128)(2,1)} %collective-permute-done.6.refs_7_.refs_4_), channel_id=1, source_target_pairs={{96,480},{224,96},{352,224},{480,352},{97,481},{225,97},{353,225},... | collective-permute-start | bytes 1843208 | tf_op jit(solution)/shard_map/ppermute | solution.py:44
  48.8 17.4 %collective-permute-start.10 = (bf16[400,768]{1,0:T(8,128)(2,1)}, bf16[400,768]{1,0:T(8,128)(2,1)S(1)}, u32[]{:S(2)}, u32[]{:S(2)}) collective-permute-start(bf16[400,768]{1,0:T(8,128)(2,1)} %collective-permute-done.6.refs_7_.refs_4_), channel_id=1, source_target_pairs={{0,16},{16,0},{32,48},{48,32},{64,80},{80,64},{112,96},{128,144},{... | collective-permute-start | bytes 1843208 | tf_op jit(solution)/shard_map/ppermute | solution.py:44
  50.1 16.1 %collective-permute-start.11 = (bf16[400,768]{1,0:T(8,128)(2,1)}, bf16[400,768]{1,0:T(8,128)(2,1)S(1)}, u32[]{:S(2)}, u32[]{:S(2)}) collective-permute-start(bf16[400,768]{1,0:T(8,128)(2,1)} %collective-permute-done.7.refs_8_.refs_3_), channel_id=1, source_target_pairs={{80,464},{208,80},{336,208},{464,336},{81,465},{209,81},{337,209},... | collective-permute-start | bytes 1843208 | tf_op jit(solution)/shard_map/ppermute | solution.py:44
  55.5 10.8 %collective-permute-start.8 = (bf16[400,768]{1,0:T(8,128)(2,1)S(1)}, bf16[400,768]{1,0:T(8,128)(2,1)S(1)}, u32[]{:S(2)}, u32[]{:S(2)}) collective-permute-start(bf16[400,768]{1,0:T(8,128)(2,1)S(1)} %collective-permute-done.3.refs_3_), channel_id=1, source_target_pairs={{16,0},{144,128},{272,256},{400,384},{17,1},{145,129},{273,257},{4... | collective-permute-start | bytes 1843208 | tf_op jit(solution)/shard_map/ppermute | solution.py:44
  66.3 2.8 %copy-start.1 = (bf16[400,768]{1,0:T(8,128)(2,1)}, bf16[400,768]{1,0:T(8,128)(2,1)S(1)}, u32[]{:S(2)}) copy-start(bf16[400,768]{1,0:T(8,128)(2,1)S(1)} %collective-permute-done.9.refs_10_.refs_3_) | copy-start | bytes 1843204
  66.3 2.8 %copy-start.5 = (bf16[400,768]{1,0:T(8,128)(2,1)}, bf16[400,768]{1,0:T(8,128)(2,1)S(1)}, u32[]{:S(2)}) copy-start(bf16[400,768]{1,0:T(8,128)(2,1)S(1)} %collective-permute-done.10.refs_11_.refs_5_) | copy-start | bytes 1843204
  66.3 2.8 %copy-start.3 = (bf16[400,768]{1,0:T(8,128)(2,1)}, bf16[400,768]{1,0:T(8,128)(2,1)S(1)}, u32[]{:S(2)}) copy-start(bf16[400,768]{1,0:T(8,128)(2,1)S(1)} %collective-permute-done.11.refs_12_.refs_4_) | copy-start | bytes 1843204
  69.9 3.5 %collective-permute-start.13 = (bf16[384,384]{1,0:T(8,128)(2,1)S(1)}, bf16[384,384]{1,0:T(8,128)(2,1)S(1)}, u32[]{:S(2)}, u32[]{:S(2)}) collective-permute-start(bf16[384,384]{1,0:T(8,128)(2,1)S(1)} %get-tuple-element.35), channel_id=1, source_target_pairs={{0,16},{16,0},{32,48},{48,32},{64,80},{80,64},{96,112},{112,96},{1... | collective-permute-start | bytes 884744 | tf_op jit(solution)/shard_map/ppermute | solution.py:44
  75.0 5.7 %copy-start.2 = (bf16[400,768]{1,0:T(8,128)(2,1)S(1)}, bf16[400,768]{1,0:T(8,128)(2,1)}, u32[]{:S(2)}) copy-start(bf16[400,768]{1,0:T(8,128)(2,1)} %copy-done.1) | copy-start | bytes 1843204
  75.0 17.6 %all-to-all-start = ((bf16[8,96,384]{2,1,0:T(8,128)(2,1)}), bf16[8,96,384]{2,1,0:T(8,128)(2,1)}, u32[]{:S(2)}, u32[]{:S(2)}) async-start(bf16[8,96,384]{2,1,0:T(8,128)(2,1)} %shard_map.111), calls=%async_computation | async-start | bytes 1179648 | tf_op jit(solution)/shard_map/all_to_all | solution.py:52
  80.7 8.5 %collective-permute-start.12 = (bf16[400,768]{1,0:T(8,128)(2,1)S(1)}, bf16[400,768]{1,0:T(8,128)(2,1)}, u32[]{:S(2)}, u32[]{:S(2)}) collective-permute-start(bf16[400,768]{1,0:T(8,128)(2,1)S(1)} %copy-done.2), channel_id=1, source_target_pairs={{96,112},{224,240},{352,368},{480,496},{97,113},{225,241},{353,369... | collective-permute-start | bytes 1843208 | tf_op jit(solution)/shard_map/ppermute | solution.py:44
  83.1 1.1 copy-start.6
  84.2 1.3 %copy-start.15 = (f32[384,768]{1,0:T(8,128)S(1)}, f32[384,768]{1,0:T(8,128)}, u32[]{:S(2)}) copy-start(f32[384,768]{1,0:T(8,128)} %copy-done.14) | copy-start | bytes 3538948
  85.4 3.7 %copy-start.4 = (bf16[400,768]{1,0:T(8,128)(2,1)S(1)}, bf16[400,768]{1,0:T(8,128)(2,1)}, u32[]{:S(2)}) copy-start(bf16[400,768]{1,0:T(8,128)(2,1)} %copy-done.3) | copy-start | bytes 1843204
  85.4 3.7 %copy-start.9 = (bf16[384,768]{1,0:T(8,128)(2,1)S(1)}, bf16[384,768]{1,0:T(8,128)(2,1)}, u32[]{:S(2)}) copy-start(bf16[384,768]{1,0:T(8,128)(2,1)} %refs_7_.1) | copy-start | bytes 1769476
  92.6 12.6 %copy-start.13 = (bf16[384,768]{1,0:T(8,128)(2,1)S(1)}, bf16[384,768]{1,0:T(8,128)(2,1)}, u32[]{:S(2)}) copy-start(bf16[384,768]{1,0:T(8,128)(2,1)} %copy-done.12) | copy-start | bytes 1769476
  95.0 22.6 %all-to-all-start.1 = ((bf16[32,2,576]{2,1,0:T(2,128)(2,1)}), bf16[32,2,576]{2,1,0:T(2,128)(2,1)S(1)}, u32[]{:S(2)}, u32[]{:S(2)}) async-start(bf16[32,2,576]{2,1,0:T(2,128)(2,1)} %reshape.141), calls=%async_computation.1 | async-start | bytes 163840 | tf_op jit(solution)/shard_map/all_to_all | solution.py:52
  (3 other events, 2.9 us)

commit v4 on v2

v4 whole, which is shorter than its diff:
```python
import jax
import jax.numpy as jnp
from jax import lax
from jax.experimental import pallas as pl
from jax.experimental.pallas import tpu as pltpu
from jax.sharding import PartitionSpec as P

D = 768
HALF = D // 2
ROWS = 384
TAIL = 16
LABELS = 128
N_BLK = 32
EPSILON = 1e-06
VMEM_BYTES = 20 * 1024 * 1024


def device_index(z_hi, x, core, z_lo, y):
    return ((z_hi * 4 + x) * 2 + core) * 16 + z_lo * 8 + y


NEAR_GROUPS = [
    [device_index(z_hi, x, core, z_lo, 2 * y_hi + y_lo) for x in range(4) for y_lo in range(2)]
    for z_hi in range(4)
    for core in range(2)
    for z_lo in range(2)
    for y_hi in range(4)
]
FAR_GROUPS = [
    [
        device_index(z_hi, x, core, z_lo, 2 * y_hi + y_lo)
        for z_hi in range(4)
        for z_lo in range(2)
        for y_hi in range(4)
    ]
    for x in range(4)
    for core in range(2)
    for y_lo in range(2)
]


def permute(value, target):
    pairs = [(i, target(i)) for i in range(N_BLK)]
    return lax.ppermute(value, "blk", [(i, j % N_BLK) for i, j in pairs if j is not None])


def swap_cores(value):
    return permute(value, lambda i: i ^ 1)


def exchange(value, groups):
    return lax.all_to_all(value, ("blk", "lane"), 0, 0, axis_index_groups=groups, tiled=True)


def dot(left, right, dims=((1,), (0,))):
    return lax.dot_general(left, right, (dims, ((), ())), preferred_element_type=jnp.float32)


def call(kernel, micros, outs, args, scalars=0, scratch=(), after=()):
    smem = pl.BlockSpec(memory_space=pltpu.SMEM)
    vmem = pl.BlockSpec(memory_space=pltpu.VMEM)
    args = list(args)
    if after:
        args[scalars] = lax.optimization_barrier((args[scalars], *after))[0]
    return pl.pallas_call(
        kernel,
        out_shape=outs,
        in_specs=[smem] * scalars + [vmem] * (len(args) - scalars),
        out_specs=[vmem] * len(outs),
        scratch_shapes=scratch,
        cost_estimate=pl.CostEstimate(
            flops=int(micros * 1.1e9), bytes_accessed=int(micros * 3.0e6), transcendentals=0
        ),
        compiler_params=pltpu.CompilerParams(vmem_limit_bytes=VMEM_BYTES),
    )(*args)


def pick(index, first, second, third):
    anywhere = pl.BlockSpec(memory_space=pl.ANY)
    return pl.pallas_call(
        pick_kernel,
        out_shape=array(first.shape, first.dtype),
        in_specs=[pl.BlockSpec(memory_space=pltpu.SMEM)] + [anywhere] * 3,
        out_specs=pl.BlockSpec(memory_space=pltpu.VMEM),
        scratch_shapes=[pltpu.SemaphoreType.DMA(())],
        cost_estimate=pl.CostEstimate(flops=0, bytes_accessed=3000000, transcendentals=0),
    )(index, first, second, third)


def array(shape, dtype):
    return jax.ShapeDtypeStruct(shape, dtype)


def put_langs(langs_ref, out_ref):
    langs = langs_ref[...].astype(jnp.float32)
    row = jnp.concatenate([langs, jnp.zeros((1, D - ROWS), jnp.float32)], axis=1)
    out_ref[ROWS:, :] = jnp.broadcast_to(row, (TAIL, D)).astype(jnp.bfloat16)


def text_kernel(text_ref, langs_ref, out_ref):
    text = text_ref[...].astype(jnp.float32)
    inverse = lax.rsqrt(jnp.sum(text * text, axis=-1, keepdims=True) + EPSILON)
    out_ref[:ROWS, :] = (text * inverse).astype(jnp.bfloat16)
    put_langs(langs_ref, out_ref)


def image_kernel(feat_ref, head_ref, langs_ref, out_ref, inv_ref):
    projected = dot(feat_ref[...], head_ref[...])
    inverse = lax.rsqrt(jnp.sum(projected * projected, axis=-1, keepdims=True) + EPSILON)
    inv_ref[...] = inverse
    out_ref[:ROWS, :] = (projected * inverse).astype(jnp.bfloat16)
    put_langs(langs_ref, out_ref)


def pair_term(scale, bias, own, own_rows, other_ref, positive):
    other = other_ref[:ROWS, :]
    langs = other_ref[ROWS : ROWS + 1, :ROWS].astype(jnp.int32)
    hot = lax.broadcasted_iota(jnp.int32, (LABELS, ROWS), 0) == langs
    weight = dot(own_rows, hot.astype(jnp.float32).astype(jnp.bfloat16))
    logit = scale * dot(own, other, ((1,), (1,))) + bias
    excess = 0.5 + 0.5 * jnp.tanh(0.5 * logit)
    if positive:
        row = lax.broadcasted_iota(jnp.int32, (ROWS, ROWS), 0)
        column = lax.broadcasted_iota(jnp.int32, (ROWS, ROWS), 1)
        excess = jnp.where(row == column, excess - 1.0, excess)
    return dot((weight * excess).astype(jnp.bfloat16), other)


def own_kernel(scalar_ref, own_ref, rows_ref, other_ref, sum_ref):
    sum_ref[...] = pair_term(
        scalar_ref[0], scalar_ref[1], own_ref[:ROWS, :], rows_ref[...], other_ref, True
    )


def add_term(scalar_ref, own_ref, rows_ref, other_ref, off, sum_ref):
    @pl.when(off == 0.0)
    def _():
        sum_ref[...] += pair_term(
            scalar_ref[0], scalar_ref[1], own_ref[:ROWS, :], rows_ref[...], other_ref, False
        )


def middle_kernel(scalar_ref, own_ref, rows_ref, mix_ref, far_ref, before_ref, sum_ref):
    sum_ref[...] = before_ref[...]
    add_term(scalar_ref, own_ref, rows_ref, mix_ref, scalar_ref[2], sum_ref)
    add_term(scalar_ref, own_ref, rows_ref, far_ref, scalar_ref[3], sum_ref)


def pick_kernel(pick_ref, first_ref, second_ref, third_ref, out_ref, sem_ref):
    for index, ref in enumerate((first_ref, second_ref, third_ref)):

        @pl.when(pick_ref[0] == index)
        def _():
            copy = pltpu.make_async_copy(ref, out_ref, sem_ref)
            copy.start()
            copy.wait()


def image_last_kernel(
    scalar_ref, own_ref, rows_ref, near_ref, hop_ref, skip_ref, direct_ref, before_ref, inv_ref,
    order_ref, dir_ref, keep_ref, send_ref, sum_ref,
):
    sum_ref[...] = before_ref[...]
    add_term(scalar_ref, own_ref, rows_ref, near_ref, scalar_ref[4], sum_ref)
    add_term(scalar_ref, own_ref, rows_ref, hop_ref, scalar_ref[6], sum_ref)
    add_term(scalar_ref, own_ref, rows_ref, skip_ref, scalar_ref[7], sum_ref)
    add_term(scalar_ref, own_ref, rows_ref, direct_ref, 1.0 - scalar_ref[4], sum_ref)
    grad = scalar_ref[0] * sum_ref[...]
    unit = own_ref[:ROWS, :].astype(jnp.float32)
    radial = jnp.sum(unit * grad, axis=-1, keepdims=True)
    direction = ((grad - unit * radial) * inv_ref[...]).astype(jnp.bfloat16)
    dir_ref[...] = direction
    turned = dot(order_ref[...], direction, ((1,), (1,))).astype(jnp.bfloat16)
    keep_ref[...] = turned[:HALF, :]
    send_ref[...] = turned[HALF:, :]


def text_back_kernel(
    scalar_ref, own_ref, rows_ref, same_ref, mix_ref, far_ref, near_ref, late_ref, text_ref,
    out_ref, sum_ref,
):
    own_kernel(scalar_ref, own_ref, rows_ref, same_ref, sum_ref)
    add_term(scalar_ref, own_ref, rows_ref, mix_ref, scalar_ref[2], sum_ref)
    add_term(scalar_ref, own_ref, rows_ref, far_ref, scalar_ref[3], sum_ref)
    add_term(scalar_ref, own_ref, rows_ref, near_ref, scalar_ref[4], sum_ref)
    add_term(scalar_ref, own_ref, rows_ref, late_ref, scalar_ref[5], sum_ref)
    grad = scalar_ref[0] * sum_ref[...]
    text = text_ref[...].astype(jnp.float32)
    inverse = lax.rsqrt(jnp.sum(text * text, axis=-1, keepdims=True) + EPSILON)
    unit = text * inverse
    radial = jnp.sum(unit * grad, axis=-1, keepdims=True)
    out_ref[...] = ((grad - unit * radial) * inverse).astype(jnp.bfloat16)


def head_kernel(keep_ref, got_ref, feat_ref, feat_near_ref, out_ref):
    for y_lo in range(2):
        columns = slice(HALF * y_lo, HALF * y_lo + HALF)
        head = dot(keep_ref[...], feat_ref[:, columns])
        head += dot(got_ref[...], feat_near_ref[:, columns])
        for x in range(4):
            out_ref[2 * x + y_lo] = head[96 * x : 96 * x + 96, :].astype(jnp.bfloat16)


def near_sum_kernel(parts_ref, out_ref):
    total = parts_ref[0].astype(jnp.float32)
    for k in range(1, 8):
        total += parts_ref[k].astype(jnp.float32)
    for z_hi in range(4):
        for k in range(8):
            piece = total[24 * z_hi : 24 * z_hi + 24, 48 * k : 48 * k + 48]
            blank = jnp.zeros((8, 32), jnp.float32)
            upper = jnp.concatenate([piece[:8], piece[8:16], blank], axis=1)
            lower = jnp.concatenate([piece[16:], piece[16:], blank], axis=1)
            packed = jnp.concatenate([upper, lower], axis=0)
            out_ref[8 * z_hi + k] = packed.astype(jnp.bfloat16)


def far_sum_kernel(parts_ref, out_ref):
    total = parts_ref[0].astype(jnp.float32)
    for k in range(1, 32):
        total += parts_ref[k].astype(jnp.float32)
    head = jnp.concatenate([total[:8, :48], total[:8, 48:96], total[8:, :48]], axis=0)
    out_ref[...] = head


def back_kernel(dir_ref, head_ref, out_ref):
    out_ref[...] = dot(dir_ref[...], head_ref[...], ((1,), (1,))).astype(jnp.bfloat16)


def column_order(core):
    new = jnp.arange(D, dtype=jnp.int32)
    side, x, z_hi, rest = new // 384, new // 96 % 4, new // 24 % 4, new % 24
    return z_hi * 192 + x * 48 + (side ^ core) * 24 + rest


def row_order():
    new = jnp.arange(D, dtype=jnp.int32)
    y_lo, z_lo, y_hi, rest = new // 384, new // 192 % 2, new // 48 % 4, new % 48
    return z_lo * 384 + (y_hi * 2 + y_lo) * 48 + rest


def order_matrix(old):
    return (old[:, None] == jnp.arange(D, dtype=jnp.int32)[None, :]).astype(jnp.bfloat16)


def on_device(
    image_feat, text_emb, head_weight, lang_ids, pair_mask, weight_codes, log_scale, logit_bias
):
    place = lax.axis_index("blk") % 8
    lang_count = pair_mask.shape[0]
    allowed = jnp.maximum(pair_mask, jnp.eye(lang_count, dtype=jnp.int32)).astype(jnp.float32)
    codes = weight_codes.astype(jnp.float32)
    table = (allowed * (0.25 * (codes[:, None] + codes[None, :]))).astype(jnp.bfloat16)
    extra = LABELS - lang_count
    table = jnp.pad(table, ((0, extra), (0, extra)))
    scale = jnp.exp(log_scale)
    text_scalars, image_scalars = [
        jnp.stack([scale, logit_bias] + [flag.astype(jnp.float32) for flag in flags])
        for flags in (
            [
                relay | inner, spot == 1, spot == 0, (spot % 2 == 1) & (spot != 1),
                (spot != 1) & ~inner, ~relay,
            ]
            for spot, relay, inner in [
                (spot, spot == 2, (spot == 4) | (spot == 6)) for spot in (place, 7 - place)
            ]
        )
    ]
    image_pick = jnp.where(place == 0, 2, jnp.where(place == 5, 1, 0)).reshape(1)
    langs = lang_ids.reshape(1, ROWS)
    block = array((ROWS + TAIL, D), jnp.bfloat16)
    total = array((ROWS, D), jnp.float32)
    scratch = [pltpu.VMEM(total.shape, total.dtype)]

    (text_out,) = call(text_kernel, 0.3, [block], (text_emb, langs))
    text_far = permute(text_out, lambda i: i + 2 if i % 8 != 7 else i - 6)
    text_mix = permute(
        text_out, lambda i: i + 1 if i % 2 == 0 else {5: i + 3, 7: i - 5}.get(i % 8)
    )

    image_out, image_inv = call(
        image_kernel,
        1.0,
        [block, array((ROWS, 1), jnp.float32)],
        (image_feat, head_weight, langs),
    )
    image_far = permute(image_out, lambda i: i - 2 if i % 8 != 0 else i + 6)
    image_mix = permute(
        image_out, lambda i: i - 1 if i % 2 == 1 else {2: i - 3, 0: i + 5}.get(i % 8)
    )

    own_hot = (lang_ids[:, None] == jnp.arange(LABELS)[None, :]).astype(jnp.bfloat16)
    image_rows = dot(own_hot, table).astype(jnp.bfloat16)
    text_rows = dot(own_hot, table, ((1,), (1,))).astype(jnp.bfloat16)
    feat_turned = dot(image_feat, order_matrix(row_order()), ((1,), (1,))).astype(jnp.bfloat16)
    feat_near = swap_cores(feat_turned)
    order = order_matrix(column_order(place % 2))
    (image_sum,) = call(
        own_kernel, 1.5, [total], (text_scalars, image_out, image_rows, text_out), 1
    )
    text_far, text_own, feat_near, image_sum, order = lax.optimization_barrier(
        (text_far, text_out, feat_near, image_sum, order)
    )

    text_near = permute(text_far, lambda i: i ^ 1 if i % 8 != 1 else None)
    text_hop = permute(text_far, lambda i: {1: i + 8, 3: i + 1, 5: i + 1}.get(i % 8))
    text_skip = permute(text_mix, lambda i: {2: i + 8}.get(i % 8))
    text_direct = permute(text_own, lambda i: {7: i + 1}.get(i % 8))
    (image_sum,) = call(
        middle_kernel,
        2.6,
        [total],
        (text_scalars, image_out, image_rows, text_mix, text_far, image_sum),
        1,
    )
    image_pass = pick(image_pick, image_far, image_mix, image_out)
    image_late = permute(
        image_pass, lambda i: {6: i - 8, 5: i - 8, 4: i - 1, 2: i - 1, 0: i - 1}.get(i % 8)
    )
    image_near = permute(image_far, lambda i: i ^ 1 if i % 8 != 6 else None)
    half = array((HALF, ROWS), jnp.bfloat16)
    image_dir, keep, send = call(
        image_last_kernel,
        0.01,
        [array((ROWS, D), jnp.bfloat16), half, half],
        (
            text_scalars, image_out, image_rows, text_near, text_hop, text_skip, text_direct,
            image_sum, image_inv, order,
        ),
        1,
        scratch,
    )
    got = swap_cores(send)
    (head,) = call(
        head_kernel,
        0.01,
        [array((8, 96, HALF), jnp.bfloat16)],
        (keep, got, feat_turned, feat_near),
        after=(image_late, image_near),
    )
    sent = head
    head = exchange(head, NEAR_GROUPS)
    (text_back,) = call(
        text_back_kernel,
        6.0,
        [array((ROWS, D), jnp.bfloat16)],
        (
            image_scalars, text_out, text_rows, image_out, image_mix, image_far, image_near,
            image_late, text_emb,
        ),
        1,
        scratch,
        (sent,),
    )
    (head,) = call(
        near_sum_kernel,
        0.5,
        [array((32, 16, 128), jnp.bfloat16)],
        (head,),
        after=(text_back,),
    )
    near_done = head
    head = exchange(head, FAR_GROUPS)
    (head_grad,) = call(far_sum_kernel, 0.5, [array((24, 48), jnp.float32)], (head,))

    (image_back,) = call(
        back_kernel,
        1.5,
        [array((ROWS, D), jnp.bfloat16)],
        (image_dir, head_weight),
        after=(near_done,),
    )
    return (image_back, text_back, head_grad.T)


def solution(mesh):
    in_specs = (
        P(("blk", "lane"), None),
        P(("blk", "lane"), None),
        P(),
        P(("blk", "lane")),
        P(),
        P(),
        P(),
        P(),
    )
    out_specs = (P(("blk", "lane"), None), P(("blk", "lane"), None), P("lane", "blk"))
    return jax.shard_map(
        on_device, mesh=mesh, in_specs=in_specs, out_specs=out_specs, check_vma=False
    )
```

time: 139 us -> 113 us (0.81)
  starting transfers between devices: 95.1 us -> 51.6 us
  waiting for transfers between devices: 4.98 us -> 19.2 us
  other arithmetic: 8.56 us -> 0.39 us
  Pallas kernels: 19.7 us -> 25.3 us
  local copies, waits for them, and re-layouts: 5.36 us -> 10 us
    all_to_all x2, starting transfers between devices: 46.7 us -> 18.3 us  [exchange(): lax.all_to_all(value, ('blk', 'lane'), 0, 0, axis_index_groups=groups, ti...]
    ppermute x12, starting transfers between devices: 48.4 us -> 33.3 us  [permute(): lax.ppermute(value, 'blk', [(i, j % N_BLK) for i, j in pairs if j is not...]
    all_to_all x2, waiting for transfers between devices: 2.48 us -> 11.2 us  [exchange(): lax.all_to_all(value, ('blk', 'lane'), 0, 0, axis_index_groups=groups, ti...]
    ppermute x12, waiting for transfers between devices: 2.51 us -> 7.95 us  [permute(): lax.ppermute(value, 'blk', [(i, j % N_BLK) for i, j in pairs if j is not...]
    select_n x2 -> x0, other arithmetic: 4.6 us -> none  [the longest x1 2.39 us: on_device(): text_mix = jnp.where(place == 0, text_hop, text_mix)]
    unnamed x28 -> x44, local copies, waits for them, and re-layouts: 5.13 us -> 9.1 us
    pallas_call x10, Pallas kernels: 19.7 us -> 23.3 us  [call(): pl.pallas_call(kernel, out_shape=outs, in_specs=[smem] * scalars + [vmem]...]
    pallas_call x0 -> x1, Pallas kernels: none -> 2.03 us  [pick(): pl.pallas_call(pick_kernel, out_shape=array(first.shape, first.dtype), in...]
  transfers between devices with their start and end apart: 14 -> 14, of which waited for: 2 -> 3; matrix products, arithmetic and copies ran while one was open for 8% -> 2% of each run, Pallas kernels for 14% -> 18%
where the time goes in v4:
time: 113 us; the launch traced here: 111 us
  starting transfers between devices  51.6 us (46%)
  Pallas kernels  25.3 us (22%)
  waiting for transfers between devices  19.2 us (17%)
  local copies, waits for them, and re-layouts  10 us (9%)
  between operations  2.4 us (2%)
  matrix products  2.06 us (2%)
    ppermute x12, starting transfers between devices, permute(): lax.ppermute(value, 'blk', [(i, j % N_BLK) for i, j in pairs if j is not...  33.3 us
    pallas_call x10, Pallas kernels, call(): pl.pallas_call(kernel, out_shape=outs, in_specs=[smem] * scalars + [vmem]...  23.3 us
    all_to_all x2, starting transfers between devices, exchange(): lax.all_to_all(value, ('blk', 'lane'), 0, 0, axis_index_groups=groups, ti...  18.3 us
    all_to_all x2, waiting for transfers between devices, exchange(): lax.all_to_all(value, ('blk', 'lane'), 0, 0, axis_index_groups=groups, ti...  11.2 us
    unnamed x44, local copies, waits for them, and re-layouts  9.1 us
    ppermute x12, waiting for transfers between devices, permute(): lax.ppermute(value, 'blk', [(i, j % N_BLK) for i, j in pairs if j is not...  7.95 us
  transfers between devices with their start and end apart: 14, of which 3 were waited for; matrix products, arithmetic and copies ran while one was open for 2% of the time, Pallas kernels for 18%

profile of v4, /device:TPU:6, one launch (start us, length us, event | category | flops | bytes accessed | tf_op | source)
XLA Modules:
  0.0 111.0 jit_solution(8423393585954095031)
XLA Ops:
  1.4 1.1 copy-done.13
  2.5 1.0 shard_map.104.other_ref.own_ref
  3.5 6.0 %collective-permute-start = (bf16[400,768]{1,0:T(8,128)(2,1)}, bf16[400,768]{1,0:T(8,128)(2,1)}, u32[]{:S(2)}, u32[]{:S(2)}) collective-permute-start(bf16[400,768]{1,0:T(8,128)(2,1)} %shard_map.104.other_ref.own_ref), channel_id=1, source_target_pairs={{0,32},{16,48},{32,64},{48,80},{64,96},{80,112},{96,128},{112,16},... | collective-permute-start | bytes 1843208 | tf_op jit(solution)/shard_map/ppermute | solution.py:44
  9.5 2.1 %collective-permute-start.4 = (bf16[400,768]{1,0:T(8,128)(2,1)}, bf16[400,768]{1,0:T(8,128)(2,1)}, u32[]{:S(2)}, u32[]{:S(2)}) collective-permute-start(bf16[400,768]{1,0:T(8,128)(2,1)} %shard_map.104.other_ref.own_ref), channel_id=1, source_target_pairs={{0,16},{32,48},{64,80},{80,128},{96,112},{112,32},{128,144},{160,1... | collective-permute-start | bytes 1843208 | tf_op jit(solution)/shard_map/ppermute | solution.py:44
  11.7 1.1 copy-done.12
  13.5 1.9 %collective-permute-start.7 = (bf16[400,768]{1,0:T(8,128)(2,1)S(1)}, bf16[400,768]{1,0:T(8,128)(2,1)S(1)}, u32[]{:S(2)}, u32[]{:S(2)}) collective-permute-start(bf16[400,768]{1,0:T(8,128)(2,1)S(1)} %get-tuple-element.17.own_ref.third_ref.same_ref), channel_id=1, source_target_pairs={{0,96},{16,496},{32,0},{48,16},{64,32},{80,48},{96,64},{112,80},{1... | collective-permute-start | bytes 1843208 | tf_op jit(solution)/shard_map/ppermute | solution.py:44
  15.4 1.3 %collective-permute-start.8 = (bf16[400,768]{1,0:T(8,128)(2,1)S(1)}, bf16[400,768]{1,0:T(8,128)(2,1)S(1)}, u32[]{:S(2)}, u32[]{:S(2)}) collective-permute-start(bf16[400,768]{1,0:T(8,128)(2,1)S(1)} %get-tuple-element.17.own_ref.third_ref.same_ref), channel_id=1, source_target_pairs={{0,80},{16,0},{32,496},{48,32},{80,64},{112,96},{128,208},{144,128... | collective-permute-start | bytes 1843208 | tf_op jit(solution)/shard_map/ppermute | solution.py:44
  16.8 1.6 %fusion.3.feat_ref = bf16[384,768]{1,0:T(8,128)(2,1)} fusion(bf16[384,768]{1,0:T(8,128)(2,1)S(1)} %copy-done.12, s32[768]{0:T(1024)S(1)} %fusion.24), kind=kOutput, calls=%fused_computation.5 | convolution fusion | flops 453869568 | bytes 1182720 | tf_op jit(solution)/shard_map/dot_general | solution.py:56
  18.3 4.5 %collective-permute-start.1 = (bf16[384,768]{1,0:T(8,128)(2,1)}, bf16[384,768]{1,0:T(8,128)(2,1)}, u32[]{:S(2)}, u32[]{:S(2)}) collective-permute-start(bf16[384,768]{1,0:T(8,128)(2,1)} %fusion.3.feat_ref), channel_id=1, source_target_pairs={{0,16},{16,0},{32,48},{48,32},{64,80},{80,64},{96,112},{112,96},{1... | collective-permute-start | bytes 1769480 | tf_op jit(solution)/shard_map/ppermute | solution.py:44
  24.7 2.1 %shard_map.105.before_ref = f32[384,768]{1,0:T(8,128)S(1)} custom-call(f32[8]{0:T(128)S(1)} %stack.100.scalar_ref, bf16[400,768]{1,0:T(8,128)(2,1)S(1)} %get-tuple-element.17.own_ref.third_ref.same_ref, bf16[384,128]{1,0:T(8,128)(2,1)S(1)} %convolution_convert_fusion.1.rows_ref, bf16[400,768]{1,0:T(8,128)(2,1)} %shard_map.104.other_ref.own_ref), custom_call_target="tpu_custom_call" | custom-call | flops 1650000000 | bytes 4500000 | tf_op jit(solution)/shard_map/pallas_call | solution.py:65
  27.1 1.9 %collective-permute-start.2 = (bf16[400,768]{1,0:T(8,128)(2,1)}, bf16[400,768]{1,0:T(8,128)(2,1)}, u32[]{:S(2)}, u32[]{:S(2)}) collective-permute-start(bf16[400,768]{1,0:T(8,128)(2,1)} %collective-permute-done.far_ref), channel_id=1, source_target_pairs={{0,16},{32,48},{48,32},{64,80},{80,64},{96,112},{112,96},{128,144}... | collective-permute-start | bytes 1843208 | tf_op jit(solution)/shard_map/ppermute | solution.py:44
  29.0 1.3 %collective-permute-start.3 = (bf16[400,768]{1,0:T(8,128)(2,1)}, bf16[400,768]{1,0:T(8,128)(2,1)}, u32[]{:S(2)}, u32[]{:S(2)}) collective-permute-start(bf16[400,768]{1,0:T(8,128)(2,1)} %collective-permute-done.far_ref), channel_id=1, source_target_pairs={{16,144},{48,64},{80,96},{144,272},{176,192},{208,224},{272,400},{... | collective-permute-start | bytes 1843208 | tf_op jit(solution)/shard_map/ppermute | solution.py:44
  30.4 1.5 %collective-permute-start.6 = (bf16[400,768]{1,0:T(8,128)(2,1)}, bf16[400,768]{1,0:T(8,128)(2,1)}, u32[]{:S(2)}, u32[]{:S(2)}) collective-permute-start(bf16[400,768]{1,0:T(8,128)(2,1)} %shard_map.104.other_ref.own_ref), channel_id=1, source_target_pairs={{112,128},{240,256},{368,384},{496,0},{113,129},{241,257},{369,385... | collective-permute-start | bytes 1843208 | tf_op jit(solution)/shard_map/ppermute | solution.py:44
  31.9 7.6 %collective-permute-done.7.first_ref.far_ref = bf16[400,768]{1,0:T(8,128)(2,1)S(1)} collective-permute-done((bf16[400,768]{1,0:T(8,128)(2,1)S(1)}, bf16[400,768]{1,0:T(8,128)(2,1)S(1)}, u32[]{:S(2)}, u32[]{:S(2)}) %collective-permute-start.7) | collective-permute-done | bytes 614432 | tf_op jit(solution)/shard_map/ppermute | solution.py:44
  39.4 1.5 %collective-permute-start.5 = (bf16[400,768]{1,0:T(8,128)(2,1)}, bf16[400,768]{1,0:T(8,128)(2,1)}, u32[]{:S(2)}, u32[]{:S(2)}) collective-permute-start(bf16[400,768]{1,0:T(8,128)(2,1)} %collective-permute-done.4.mix_ref), channel_id=1, source_target_pairs={{32,160},{160,288},{288,416},{416,32},{33,161},{161,289},{289,417}... | collective-permute-start | bytes 1843208 | tf_op jit(solution)/shard_map/ppermute | solution.py:44
  40.9 0.8 copy-done.4
  41.8 2.0 %shard_map.108 = bf16[400,768]{1,0:T(8,128)(2,1)} custom-call(s32[1]{0:T(128)} %bitcast.9.pick_ref, bf16[400,768]{1,0:T(8,128)(2,1)} %copy-done.2, bf16[400,768]{1,0:T(8,128)(2,1)} %copy-done.4, bf16[400,768]{1,0:T(8,128)(2,1)} %copy-done), custom_call_target="tpu_custom_call" | custom-call | bytes 3000000 | tf_op jit(solution)/shard_map/pallas_call | solution.py:80
  43.8 6.9 %collective-permute-start.9 = (bf16[400,768]{1,0:T(8,128)(2,1)}, bf16[400,768]{1,0:T(8,128)(2,1)S(1)}, u32[]{:S(2)}, u32[]{:S(2)}) collective-permute-start(bf16[400,768]{1,0:T(8,128)(2,1)} %shard_map.108), channel_id=1, source_target_pairs={{0,496},{32,16},{64,48},{80,464},{96,480},{128,112},{160,144},{192... | collective-permute-start | bytes 1843208 | tf_op jit(solution)/shard_map/ppermute | solution.py:44
  50.7 1.3 %collective-permute-start.10 = (bf16[400,768]{1,0:T(8,128)(2,1)}, bf16[400,768]{1,0:T(8,128)(2,1)S(1)}, u32[]{:S(2)}, u32[]{:S(2)}) collective-permute-start(bf16[400,768]{1,0:T(8,128)(2,1)} %copy-done.2), channel_id=1, source_target_pairs={{0,16},{16,0},{32,48},{48,32},{64,80},{80,64},{112,96},{128,144},{... | collective-permute-start | bytes 1843208 | tf_op jit(solution)/shard_map/ppermute | solution.py:44
  52.1 1.3 %copy-done.18 = f32[384,768]{1,0:T(8,128)S(1)} copy-done((f32[384,768]{1,0:T(8,128)S(1)}, f32[384,768]{1,0:T(8,128)}, u32[]{:S(2)}) %copy-start.18) | copy-done | bytes 1179672
  53.3 2.3 %shard_map.106.before_ref = f32[384,768]{1,0:T(8,128)S(1)} custom-call(f32[8]{0:T(128)S(1)} %stack.100.scalar_ref, bf16[400,768]{1,0:T(8,128)(2,1)S(1)} %copy-done.1, bf16[384,128]{1,0:T(8,128)(2,1)S(1)} %convolution_convert_fusion.1.rows_ref, bf16[400,768]{1,0:T(8,128)(2,1)} %collective-permute-done.4.mix_ref, ...), custom_call_target="tpu_custom_call" | custom-call | flops 2860000000 | bytes 7800000 | tf_op jit(solution)/shard_map/pallas_call | solution.py:65
  55.7 4.8 %shard_map.107 = (bf16[384,768]{1,0:T(8,128)(2,1)S(1)}, bf16[384,384]{1,0:T(8,128)(2,1)S(1)}, bf16[384,384]{1,0:T(8,128)(2,1)S(1)}) custom-call(f32[8]{0:T(128)S(1)} %stack.100.scalar_ref, bf16[400,768]{1,0:T(8,128)(2,1)S(1)} %copy-done.1, bf16[384,128]{1,0:T(8,128)(2,1)S(1)} %convolution_convert_fusion.1.rows_ref, ...), custom_call_target="tpu_custom_call" | custom-call | flops 11000000 | bytes 30000 | tf_op jit(solution)/shard_map/pallas_call | solution.py:65
  61.3 3.1 %collective-permute-start.11 = (bf16[384,384]{1,0:T(8,128)(2,1)S(1)}, bf16[384,384]{1,0:T(8,128)(2,1)S(1)}, u32[]{:S(2)}, u32[]{:S(2)}) collective-permute-start(bf16[384,384]{1,0:T(8,128)(2,1)S(1)} %get-tuple-element.26), channel_id=1, source_target_pairs={{0,16},{16,0},{32,48},{48,32},{64,80},{80,64},{96,112},{112,96},{1... | collective-permute-start | bytes 884744 | tf_op jit(solution)/shard_map/ppermute | solution.py:44
  65.6 2.9 %shard_map.109 = bf16[8,96,384]{2,1,0:T(8,128)(2,1)} custom-call(bf16[384,384]{1,0:T(8,128)(2,1)S(1)} %get-tuple-element.25.keep_ref, bf16[384,384]{1,0:T(8,128)(2,1)S(1)} %collective-permute-done.11.got_ref, bf16[384,768]{1,0:T(8,128)(2,1)} %fusion.3.feat_ref, bf16[384,768]{1,0:T(8,128)(2,1)} %collective-permute-done.1.feat_near_ref), custom_call_target="tpu_custom_call" | custom-call | flops 11000000 | bytes 30000 | tf_op jit(solution)/shard_map/pallas_call | solution.py:65
  68.6 6.8 %all-to-all-start = ((bf16[8,96,384]{2,1,0:T(8,128)(2,1)}), bf16[8,96,384]{2,1,0:T(8,128)(2,1)S(1)}, u32[]{:S(2)}, u32[]{:S(2)}) async-start(bf16[8,96,384]{2,1,0:T(8,128)(2,1)} %shard_map.109), calls=%async_computation | async-start | bytes 1179648 | tf_op jit(solution)/shard_map/all_to_all | solution.py:52
  75.7 1.1 copy-done.9
  76.8 1.1 copy-done.11
  77.9 1.1 copy-done.14
  78.9 6.4 %shard_map.110 = bf16[384,768]{1,0:T(8,128)(2,1)} custom-call(f32[8]{0:T(128)S(1)} %stack.113.scalar_ref, bf16[400,768]{1,0:T(8,128)(2,1)} %shard_map.104.other_ref.own_ref, bf16[384,128]{1,0:T(8,128)(2,1)S(1)} %convolution_convert_fusion.rows_ref, bf16[400,768]{1,0:T(8,128)(2,1)S(1)} %copy-done.1, bf16[400,768]{1,0:T(8,128)(2,1)S(1)} %copy-done.5, ...), custom_call_target="tpu_custom_call" | custom-call | flops 6600000000 | bytes 18000000 | tf_op jit(solution)/shard_map/pallas_call | solution.py:65
  86.1 11.5 %all-to-all-start.1 = ((bf16[32,16,128]{2,1,0:T(8,128)(2,1)}), bf16[32,16,128]{2,1,0:T(8,128)(2,1)S(1)}, u32[]{:S(2)}, u32[]{:S(2)}) async-start(bf16[32,16,128]{2,1,0:T(8,128)(2,1)} %shard_map.111), calls=%async_computation.1 | async-start | bytes 262144 | tf_op jit(solution)/shard_map/all_to_all | solution.py:52
  97.6 1.5 %shard_map.112 = bf16[384,768]{1,0:T(8,128)(2,1)} custom-call(bf16[384,768]{1,0:T(8,128)(2,1)S(1)} %copy-done.16, bf16[768,768]{1,0:T(8,128)(2,1)S(1)} %copy-done.7), custom_call_target="tpu_custom_call" | custom-call | flops 1650000000 | bytes 4500000 | tf_op jit(solution)/shard_map/pallas_call | solution.py:65
  99.1 11.2 %all-to-all-done.1.parts_ref = bf16[32,16,128]{2,1,0:T(8,128)(2,1)S(1)} async-done(((bf16[32,16,128]{2,1,0:T(8,128)(2,1)}), bf16[32,16,128]{2,1,0:T(8,128)(2,1)S(1)}, u32[]{:S(2)}, u32[]{:S(2)}) %all-to-all-start.1) | async-done | bytes 131104 | tf_op jit(solution)/shard_map/all_to_all | solution.py:52
  (62 shorter events, 6.1 us)
Async XLA Ops:
  0.6 11.0 %copy-start.6 = (bf16[768,768]{1,0:T(8,128)(2,1)S(1)}, bf16[768,768]{1,0:T(8,128)(2,1)}, u32[]{:S(2)}) copy-start(bf16[768,768]{1,0:T(8,128)(2,1)} %head_ref.3) | copy-start | bytes 3538948
  1.4 1.1 copy-start.13
  3.5 23.6 %collective-permute-start = (bf16[400,768]{1,0:T(8,128)(2,1)}, bf16[400,768]{1,0:T(8,128)(2,1)}, u32[]{:S(2)}, u32[]{:S(2)}) collective-permute-start(bf16[400,768]{1,0:T(8,128)(2,1)} %shard_map.104.other_ref.own_ref), channel_id=1, source_target_pairs={{0,32},{16,48},{32,64},{48,80},{64,96},{80,112},{96,128},{112,16},... | collective-permute-start | bytes 1843208 | tf_op jit(solution)/shard_map/ppermute | solution.py:44
  9.5 20.8 %collective-permute-start.4 = (bf16[400,768]{1,0:T(8,128)(2,1)}, bf16[400,768]{1,0:T(8,128)(2,1)}, u32[]{:S(2)}, u32[]{:S(2)}) collective-permute-start(bf16[400,768]{1,0:T(8,128)(2,1)} %shard_map.104.other_ref.own_ref), channel_id=1, source_target_pairs={{0,16},{32,48},{64,80},{80,128},{96,112},{112,32},{128,144},{160,1... | collective-permute-start | bytes 1843208 | tf_op jit(solution)/shard_map/ppermute | solution.py:44
  11.7 1.1 copy-start.12
  13.5 11.2 %copy-start = (bf16[400,768]{1,0:T(8,128)(2,1)}, bf16[400,768]{1,0:T(8,128)(2,1)S(1)}, u32[]{:S(2)}) copy-start(bf16[400,768]{1,0:T(8,128)(2,1)S(1)} %get-tuple-element.17.own_ref.third_ref.same_ref) | copy-start | bytes 1843204
  13.5 26.0 %collective-permute-start.7 = (bf16[400,768]{1,0:T(8,128)(2,1)S(1)}, bf16[400,768]{1,0:T(8,128)(2,1)S(1)}, u32[]{:S(2)}, u32[]{:S(2)}) collective-permute-start(bf16[400,768]{1,0:T(8,128)(2,1)S(1)} %get-tuple-element.17.own_ref.third_ref.same_ref), channel_id=1, source_target_pairs={{0,96},{16,496},{32,0},{48,16},{64,32},{80,48},{96,64},{112,80},{1... | collective-permute-start | bytes 1843208 | tf_op jit(solution)/shard_map/ppermute | solution.py:44
  15.4 25.5 %collective-permute-start.8 = (bf16[400,768]{1,0:T(8,128)(2,1)S(1)}, bf16[400,768]{1,0:T(8,128)(2,1)S(1)}, u32[]{:S(2)}, u32[]{:S(2)}) collective-permute-start(bf16[400,768]{1,0:T(8,128)(2,1)S(1)} %get-tuple-element.17.own_ref.third_ref.same_ref), channel_id=1, source_target_pairs={{0,80},{16,0},{32,496},{48,32},{80,64},{112,96},{128,208},{144,128... | collective-permute-start | bytes 1843208 | tf_op jit(solution)/shard_map/ppermute | solution.py:44
  16.7 6.1 %copy-start.21 = (s32[109]{0:T(128)S(1)}, s32[109]{0:T(128)}, u32[]{:S(2)}) copy-start(s32[109]{0:T(128)} %param.13) | copy-start | bytes 1312
  16.7 6.1 %copy-start.19 = (s32[109,109]{1,0:T(8,128)S(1)}, s32[109,109]{1,0:T(8,128)}, u32[]{:S(2)}) copy-start(s32[109,109]{1,0:T(8,128)} %param.12) | copy-start | bytes 142576
  16.7 6.2 %copy-start.20 = (s32[384]{0:T(512)S(1)}, s32[384]{0:T(512)}, u32[]{:S(2)}) copy-start(s32[384]{0:T(512)} %param.11) | copy-start | bytes 4612
  18.3 8.8 %collective-permute-start.1 = (bf16[384,768]{1,0:T(8,128)(2,1)}, bf16[384,768]{1,0:T(8,128)(2,1)}, u32[]{:S(2)}, u32[]{:S(2)}) collective-permute-start(bf16[384,768]{1,0:T(8,128)(2,1)} %fusion.3.feat_ref), channel_id=1, source_target_pairs={{0,16},{16,0},{32,48},{48,32},{64,80},{80,64},{96,112},{112,96},{1... | collective-permute-start | bytes 1769480 | tf_op jit(solution)/shard_map/ppermute | solution.py:44
  26.8 12.6 %copy-start.17 = (f32[384,768]{1,0:T(8,128)}, f32[384,768]{1,0:T(8,128)S(1)}, u32[]{:S(2)}) copy-start(f32[384,768]{1,0:T(8,128)S(1)} %shard_map.105.before_ref) | copy-start | bytes 3538948
  27.1 23.6 %collective-permute-start.2 = (bf16[400,768]{1,0:T(8,128)(2,1)}, bf16[400,768]{1,0:T(8,128)(2,1)}, u32[]{:S(2)}, u32[]{:S(2)}) collective-permute-start(bf16[400,768]{1,0:T(8,128)(2,1)} %collective-permute-done.far_ref), channel_id=1, source_target_pairs={{0,16},{32,48},{48,32},{64,80},{80,64},{96,112},{112,96},{128,144}... | collective-permute-start | bytes 1843208 | tf_op jit(solution)/shard_map/ppermute | solution.py:44
  29.0 26.6 %collective-permute-start.3 = (bf16[400,768]{1,0:T(8,128)(2,1)}, bf16[400,768]{1,0:T(8,128)(2,1)}, u32[]{:S(2)}, u32[]{:S(2)}) collective-permute-start(bf16[400,768]{1,0:T(8,128)(2,1)} %collective-permute-done.far_ref), channel_id=1, source_target_pairs={{16,144},{48,64},{80,96},{144,272},{176,192},{208,224},{272,400},{... | collective-permute-start | bytes 1843208 | tf_op jit(solution)/shard_map/ppermute | solution.py:44
  30.4 25.3 %collective-permute-start.6 = (bf16[400,768]{1,0:T(8,128)(2,1)}, bf16[400,768]{1,0:T(8,128)(2,1)}, u32[]{:S(2)}, u32[]{:S(2)}) collective-permute-start(bf16[400,768]{1,0:T(8,128)(2,1)} %shard_map.104.other_ref.own_ref), channel_id=1, source_target_pairs={{112,128},{240,256},{368,384},{496,0},{113,129},{241,257},{369,385... | collective-permute-start | bytes 1843208 | tf_op jit(solution)/shard_map/ppermute | solution.py:44
  39.4 1.5 %copy-start.2 = (bf16[400,768]{1,0:T(8,128)(2,1)}, bf16[400,768]{1,0:T(8,128)(2,1)S(1)}, u32[]{:S(2)}) copy-start(bf16[400,768]{1,0:T(8,128)(2,1)S(1)} %collective-permute-done.7.first_ref.far_ref) | copy-start | bytes 1843204
  39.4 16.3 %collective-permute-start.5 = (bf16[400,768]{1,0:T(8,128)(2,1)}, bf16[400,768]{1,0:T(8,128)(2,1)}, u32[]{:S(2)}, u32[]{:S(2)}) collective-permute-start(bf16[400,768]{1,0:T(8,128)(2,1)} %collective-permute-done.4.mix_ref), channel_id=1, source_target_pairs={{32,160},{160,288},{288,416},{416,32},{33,161},{161,289},{289,417}... | collective-permute-start | bytes 1843208 | tf_op jit(solution)/shard_map/ppermute | solution.py:44
  41.8 10.3 %copy-start.1 = (bf16[400,768]{1,0:T(8,128)(2,1)S(1)}, bf16[400,768]{1,0:T(8,128)(2,1)}, u32[]{:S(2)}) copy-start(bf16[400,768]{1,0:T(8,128)(2,1)} %copy-done) | copy-start | bytes 1843204
  43.8 20.6 %collective-permute-start.9 = (bf16[400,768]{1,0:T(8,128)(2,1)}, bf16[400,768]{1,0:T(8,128)(2,1)S(1)}, u32[]{:S(2)}, u32[]{:S(2)}) collective-permute-start(bf16[400,768]{1,0:T(8,128)(2,1)} %shard_map.108), channel_id=1, source_target_pairs={{0,496},{32,16},{64,48},{80,464},{96,480},{128,112},{160,144},{192... | collective-permute-start | bytes 1843208 | tf_op jit(solution)/shard_map/ppermute | solution.py:44
  50.7 14.5 %collective-permute-start.10 = (bf16[400,768]{1,0:T(8,128)(2,1)}, bf16[400,768]{1,0:T(8,128)(2,1)S(1)}, u32[]{:S(2)}, u32[]{:S(2)}) collective-permute-start(bf16[400,768]{1,0:T(8,128)(2,1)} %copy-done.2), channel_id=1, source_target_pairs={{0,16},{16,0},{32,48},{48,32},{64,80},{80,64},{112,96},{128,144},{... | collective-permute-start | bytes 1843208 | tf_op jit(solution)/shard_map/ppermute | solution.py:44
  52.0 1.3 %copy-start.18 = (f32[384,768]{1,0:T(8,128)S(1)}, f32[384,768]{1,0:T(8,128)}, u32[]{:S(2)}) copy-start(f32[384,768]{1,0:T(8,128)} %copy-done.17) | copy-start | bytes 3538948
  61.3 4.3 %collective-permute-start.11 = (bf16[384,384]{1,0:T(8,128)(2,1)S(1)}, bf16[384,384]{1,0:T(8,128)(2,1)S(1)}, u32[]{:S(2)}, u32[]{:S(2)}) collective-permute-start(bf16[384,384]{1,0:T(8,128)(2,1)S(1)} %get-tuple-element.26), channel_id=1, source_target_pairs={{0,16},{16,0},{32,48},{48,32},{64,80},{80,64},{96,112},{112,96},{1... | collective-permute-start | bytes 884744 | tf_op jit(solution)/shard_map/ppermute | solution.py:44
  65.2 3.3 %copy-start.10 = (bf16[400,768]{1,0:T(8,128)(2,1)}, bf16[400,768]{1,0:T(8,128)(2,1)S(1)}, u32[]{:S(2)}) copy-start(bf16[400,768]{1,0:T(8,128)(2,1)S(1)} %collective-permute-done.10.near_ref) | copy-start | bytes 1843204
  68.5 7.2 %copy-start.3 = (bf16[400,768]{1,0:T(8,128)(2,1)S(1)}, bf16[400,768]{1,0:T(8,128)(2,1)}, u32[]{:S(2)}) copy-start(bf16[400,768]{1,0:T(8,128)(2,1)} %copy-done.2) | copy-start | bytes 1843204
  68.6 7.2 %copy-start.5 = (bf16[400,768]{1,0:T(8,128)(2,1)S(1)}, bf16[400,768]{1,0:T(8,128)(2,1)}, u32[]{:S(2)}) copy-start(bf16[400,768]{1,0:T(8,128)(2,1)} %copy-done.4) | copy-start | bytes 1843204
  68.6 16.8 %all-to-all-start = ((bf16[8,96,384]{2,1,0:T(8,128)(2,1)}), bf16[8,96,384]{2,1,0:T(8,128)(2,1)S(1)}, u32[]{:S(2)}, u32[]{:S(2)}) async-start(bf16[8,96,384]{2,1,0:T(8,128)(2,1)} %shard_map.109), calls=%async_computation | async-start | bytes 1179648 | tf_op jit(solution)/shard_map/all_to_all | solution.py:52
  75.7 1.1 copy-start.9
  76.8 1.1 copy-start.11
  85.3 12.3 %copy-start.7 = (bf16[768,768]{1,0:T(8,128)(2,1)S(1)}, bf16[768,768]{1,0:T(8,128)(2,1)}, u32[]{:S(2)}) copy-start(bf16[768,768]{1,0:T(8,128)(2,1)} %head_ref.3) | copy-start | bytes 3538948
  85.3 12.3 %copy-start.16 = (bf16[384,768]{1,0:T(8,128)(2,1)S(1)}, bf16[384,768]{1,0:T(8,128)(2,1)}, u32[]{:S(2)}) copy-start(bf16[384,768]{1,0:T(8,128)(2,1)} %copy-done.15) | copy-start | bytes 1769476
  86.1 24.2 %all-to-all-start.1 = ((bf16[32,16,128]{2,1,0:T(8,128)(2,1)}), bf16[32,16,128]{2,1,0:T(8,128)(2,1)S(1)}, u32[]{:S(2)}, u32[]{:S(2)}) async-start(bf16[32,16,128]{2,1,0:T(8,128)(2,1)} %shard_map.111), calls=%async_computation.1 | async-start | bytes 262144 | tf_op jit(solution)/shard_map/all_to_all | solution.py:52
  (4 other events, 3.5 us)

commit v5 on v4

--- a/solution.py
+++ b/solution.py
@@ -56,12 +56,9 @@
     return lax.dot_general(left, right, (dims, ((), ())), preferred_element_type=jnp.float32)
 
 
-def call(kernel, micros, outs, args, scalars=0, scratch=(), after=()):
+def call(kernel, micros, outs, args, scalars=0, scratch=()):
     smem = pl.BlockSpec(memory_space=pltpu.SMEM)
     vmem = pl.BlockSpec(memory_space=pltpu.VMEM)
-    args = list(args)
-    if after:
-        args[scalars] = lax.optimization_barrier((args[scalars], *after))[0]
     return pl.pallas_call(
         kernel,
         out_shape=outs,
@@ -146,6 +143,11 @@
     add_term(scalar_ref, own_ref, rows_ref, far_ref, scalar_ref[3], sum_ref)
 
 
+def near_kernel(scalar_ref, own_ref, rows_ref, near_ref, before_ref, sum_ref):
+    sum_ref[...] = before_ref[...]
+    add_term(scalar_ref, own_ref, rows_ref, near_ref, scalar_ref[4], sum_ref)
+
+
 def pick_kernel(pick_ref, first_ref, second_ref, third_ref, out_ref, sem_ref):
     for index, ref in enumerate((first_ref, second_ref, third_ref)):
 
@@ -157,14 +159,13 @@
 
 
 def image_last_kernel(
-    scalar_ref, own_ref, rows_ref, near_ref, hop_ref, skip_ref, direct_ref, before_ref, inv_ref,
-    order_ref, dir_ref, keep_ref, send_ref, sum_ref,
+    scalar_ref, own_ref, rows_ref, hop_ref, skip_ref, corner_ref, before_ref, inv_ref, order_ref,
+    dir_ref, keep_ref, send_ref, sum_ref,
 ):
     sum_ref[...] = before_ref[...]
-    add_term(scalar_ref, own_ref, rows_ref, near_ref, scalar_ref[4], sum_ref)
     add_term(scalar_ref, own_ref, rows_ref, hop_ref, scalar_ref[6], sum_ref)
     add_term(scalar_ref, own_ref, rows_ref, skip_ref, scalar_ref[7], sum_ref)
-    add_term(scalar_ref, own_ref, rows_ref, direct_ref, 1.0 - scalar_ref[4], sum_ref)
+    add_term(scalar_ref, own_ref, rows_ref, corner_ref, 1.0 - scalar_ref[4], sum_ref)
     grad = scalar_ref[0] * sum_ref[...]
     unit = own_ref[:ROWS, :].astype(jnp.float32)
     radial = jnp.sum(unit * grad, axis=-1, keepdims=True)
@@ -175,14 +176,19 @@
     send_ref[...] = turned[HALF:, :]
 
 
-def text_back_kernel(
-    scalar_ref, own_ref, rows_ref, same_ref, mix_ref, far_ref, near_ref, late_ref, text_ref,
-    out_ref, sum_ref,
+def text_middle_kernel(
+    scalar_ref, own_ref, rows_ref, same_ref, mix_ref, far_ref, near_ref, sum_ref
 ):
     own_kernel(scalar_ref, own_ref, rows_ref, same_ref, sum_ref)
     add_term(scalar_ref, own_ref, rows_ref, mix_ref, scalar_ref[2], sum_ref)
     add_term(scalar_ref, own_ref, rows_ref, far_ref, scalar_ref[3], sum_ref)
     add_term(scalar_ref, own_ref, rows_ref, near_ref, scalar_ref[4], sum_ref)
+
+
+def text_last_kernel(
+    scalar_ref, own_ref, rows_ref, late_ref, before_ref, text_ref, out_ref, sum_ref
+):
+    sum_ref[...] = before_ref[...]
     add_term(scalar_ref, own_ref, rows_ref, late_ref, scalar_ref[5], sum_ref)
     grad = scalar_ref[0] * sum_ref[...]
     text = text_ref[...].astype(jnp.float32)
@@ -193,12 +199,26 @@
 
 
 def head_kernel(keep_ref, got_ref, feat_ref, feat_near_ref, out_ref):
-    for y_lo in range(2):
-        columns = slice(HALF * y_lo, HALF * y_lo + HALF)
-        head = dot(keep_ref[...], feat_ref[:, columns])
-        head += dot(got_ref[...], feat_near_ref[:, columns])
-        for x in range(4):
-            out_ref[2 * x + y_lo] = head[96 * x : 96 * x + 96, :].astype(jnp.bfloat16)
+    head = dot(keep_ref[...], feat_ref[...]) + dot(got_ref[...], feat_near_ref[...])
+    for x in range(4):
+        out_ref[x, 0] = head[96 * x : 96 * x + 96, :].astype(jnp.bfloat16)
+
+
+def head_product(keep, got, feat, feat_near):
+    whole = pl.BlockSpec((HALF, ROWS), lambda y_lo: (0, 0))
+    side = pl.BlockSpec((ROWS, HALF), lambda y_lo: (0, y_lo))
+    head = pl.pallas_call(
+        head_kernel,
+        grid=(2,),
+        out_shape=array((4, 2, 96, HALF), jnp.bfloat16),
+        in_specs=[whole, whole, side, side],
+        out_specs=pl.BlockSpec((4, 1, 96, HALF), lambda y_lo: (0, y_lo, 0, 0)),
+        cost_estimate=pl.CostEstimate(
+            flops=int(1.9e9), bytes_accessed=int(5.1e6), transcendentals=0
+        ),
+        compiler_params=pltpu.CompilerParams(vmem_limit_bytes=VMEM_BYTES),
+    )(keep, got, feat, feat_near)
+    return head.reshape(8, 96, HALF)
 
 
 def near_sum_kernel(parts_ref, out_ref):
@@ -298,14 +318,13 @@
     (image_sum,) = call(
         own_kernel, 1.5, [total], (text_scalars, image_out, image_rows, text_out), 1
     )
-    text_far, text_own, feat_near, image_sum, order = lax.optimization_barrier(
-        (text_far, text_out, feat_near, image_sum, order)
-    )
-
-    text_near = permute(text_far, lambda i: i ^ 1 if i % 8 != 1 else None)
+    text_far, feat_near, image_sum, order = lax.optimization_barrier(
+        (text_far, feat_near, image_sum, order)
+    )
+
     text_hop = permute(text_far, lambda i: {1: i + 8, 3: i + 1, 5: i + 1}.get(i % 8))
     text_skip = permute(text_mix, lambda i: {2: i + 8}.get(i % 8))
-    text_direct = permute(text_own, lambda i: {7: i + 1}.get(i % 8))
+    text_near = permute(text_far, lambda i: i ^ 1 if i % 8 != 1 else None)
     (image_sum,) = call(
         middle_kernel,
         2.6,
@@ -314,61 +333,65 @@
         1,
     )
     image_pass = pick(image_pick, image_far, image_mix, image_out)
-    image_late = permute(
-        image_pass, lambda i: {6: i - 8, 5: i - 8, 4: i - 1, 2: i - 1, 0: i - 1}.get(i % 8)
-    )
-    image_near = permute(image_far, lambda i: i ^ 1 if i % 8 != 6 else None)
+    text_hop, text_skip, image_sum, image_pass = lax.optimization_barrier(
+        (text_hop, text_skip, image_sum, image_pass)
+    )
+    text_corner = permute(text_hop, lambda i: {1: i - 1}.get(i % 8))
+    (image_sum,) = call(
+        near_kernel,
+        1.6,
+        [total],
+        (text_scalars, image_out, image_rows, text_near, image_sum),
+        1,
+    )
     half = array((HALF, ROWS), jnp.bfloat16)
     image_dir, keep, send = call(
         image_last_kernel,
-        0.01,
+        3.0,
         [array((ROWS, D), jnp.bfloat16), half, half],
         (
-            text_scalars, image_out, image_rows, text_near, text_hop, text_skip, text_direct,
-            image_sum, image_inv, order,
+            text_scalars, image_out, image_rows, text_hop, text_skip, text_corner, image_sum,
+            image_inv, order,
         ),
         1,
         scratch,
     )
     got = swap_cores(send)
-    (head,) = call(
-        head_kernel,
-        0.01,
-        [array((8, 96, HALF), jnp.bfloat16)],
-        (keep, got, feat_turned, feat_near),
-        after=(image_late, image_near),
-    )
-    sent = head
+    (image_back,) = call(
+        back_kernel, 1.5, [array((ROWS, D), jnp.bfloat16)], (image_dir, head_weight)
+    )
+    got, image_back = lax.optimization_barrier((got, image_back))
+    head = head_product(keep, got, feat_turned, feat_near)
+    image_far, image_pass, head = lax.optimization_barrier((image_far, image_pass, head))
+    image_late = permute(
+        image_pass, lambda i: {6: i - 8, 5: i - 8, 4: i - 1, 2: i - 1, 0: i - 1}.get(i % 8)
+    )
+    image_near = permute(image_far, lambda i: i ^ 1 if i % 8 != 6 else None)
     head = exchange(head, NEAR_GROUPS)
-    (text_back,) = call(
-        text_back_kernel,
-        6.0,
-        [array((ROWS, D), jnp.bfloat16)],
-        (
-            image_scalars, text_out, text_rows, image_out, image_mix, image_far, image_near,
-            image_late, text_emb,
-        ),
-        1,
-        scratch,
-        (sent,),
-    )
     (head,) = call(
         near_sum_kernel,
         0.5,
         [array((32, 16, 128), jnp.bfloat16)],
         (head,),
-        after=(text_back,),
-    )
-    near_done = head
+    )
+    text_out, head = lax.optimization_barrier((text_out, head))
     head = exchange(head, FAR_GROUPS)
     (head_grad,) = call(far_sum_kernel, 0.5, [array((24, 48), jnp.float32)], (head,))
 
-    (image_back,) = call(
-        back_kernel,
-        1.5,
+    (text_sum,) = call(
+        text_middle_kernel,
+        5.0,
+        [total],
+        (image_scalars, text_out, text_rows, image_out, image_mix, image_far, image_near),
+        1,
+    )
+    (text_back,) = call(
+        text_last_kernel,
+        3.0,
         [array((ROWS, D), jnp.bfloat16)],
-        (image_dir, head_weight),
-        after=(near_done,),
+        (image_scalars, text_out, text_rows, image_late, text_sum, text_emb),
+        1,
+        scratch,
     )
     return (image_back, text_back, head_grad.T)
 

time: 113 us -> 109 us (0.965)
  waiting for transfers between devices: 19.2 us -> 13.1 us
  starting transfers between devices: 51.6 us -> 55.3 us
  local copies, waits for them, and re-layouts: 10 us -> 6.49 us
  Pallas kernels: 25.3 us -> 27.6 us
    all_to_all x2, starting transfers between devices: 18.3 us -> 25.6 us  [exchange(): lax.all_to_all(value, ('blk', 'lane'), 0, 0, axis_index_groups=groups, ti...]
    all_to_all x2, waiting for transfers between devices: 11.2 us -> 6.67 us  [exchange(): lax.all_to_all(value, ('blk', 'lane'), 0, 0, axis_index_groups=groups, ti...]
    ppermute x12, starting transfers between devices: 33.3 us -> 29.7 us  [permute(): lax.ppermute(value, 'blk', [(i, j % N_BLK) for i, j in pairs if j is not...]
    unnamed x44 -> x32, local copies, waits for them, and re-layouts: 9.1 us -> 5.53 us
    pallas_call x0 -> x1, Pallas kernels: none -> 2.84 us  [head_product(): pl.pallas_call(head_kernel, grid=(2,), out_shape=array((4, 2, 96, HALF),...]
    ppermute x12, waiting for transfers between devices: 7.95 us -> 6.43 us  [permute(): lax.ppermute(value, 'blk', [(i, j % N_BLK) for i, j in pairs if j is not...]
    pallas_call x10 -> x11, Pallas kernels: 23.3 us -> 22.8 us  [call(): pl.pallas_call(kernel, out_shape=outs, in_specs=[smem] * scalars + [vmem]...]
  transfers between devices with their start and end apart: 14 -> 14, of which waited for: 3 -> 4; matrix products, arithmetic and copies ran while one was open for 2% -> 2% of each run, Pallas kernels for 18% -> 18%
where the time goes in v5:
time: 109 us; the launch traced here: 107 us
  starting transfers between devices  55.3 us (51%)
  Pallas kernels  27.6 us (25%)
  waiting for transfers between devices  13.1 us (12%)
  local copies, waits for them, and re-layouts  6.49 us (6%)
  between operations  2.46 us (2%)
  matrix products  2.07 us (2%)
    ppermute x12, starting transfers between devices, permute(): lax.ppermute(value, 'blk', [(i, j % N_BLK) for i, j in pairs if j is not...  29.7 us
    all_to_all x2, starting transfers between devices, exchange(): lax.all_to_all(value, ('blk', 'lane'), 0, 0, axis_index_groups=groups, ti...  25.6 us
    pallas_call x11, Pallas kernels, call(): pl.pallas_call(kernel, out_shape=outs, in_specs=[smem] * scalars + [vmem]...  22.8 us
    all_to_all x2, waiting for transfers between devices, exchange(): lax.all_to_all(value, ('blk', 'lane'), 0, 0, axis_index_groups=groups, ti...  6.67 us
    ppermute x12, waiting for transfers between devices, permute(): lax.ppermute(value, 'blk', [(i, j % N_BLK) for i, j in pairs if j is not...  6.43 us
    unnamed x32, local copies, waits for them, and re-layouts  5.53 us
    pallas_call x1, Pallas kernels, head_product(): pl.pallas_call(head_kernel, grid=(2,), out_shape=array((4, 2, 96, HALF),...  2.84 us
  transfers between devices with their start and end apart: 14, of which 4 were waited for; matrix products, arithmetic and copies ran while one was open for 2% of the time, Pallas kernels for 18%

profile of v5, /device:TPU:6, one launch (start us, length us, event | category | flops | bytes accessed | tf_op | source)
XLA Modules:
  0.0 107.4 jit_solution(8717565310513582780)
XLA Ops:
  1.4 1.1 copy-done.9
  2.5 1.0 shard_map.104.other_ref.own_ref
  3.5 6.0 %collective-permute-start = (bf16[400,768]{1,0:T(8,128)(2,1)}, bf16[400,768]{1,0:T(8,128)(2,1)}, u32[]{:S(2)}, u32[]{:S(2)}) collective-permute-start(bf16[400,768]{1,0:T(8,128)(2,1)} %shard_map.104.other_ref.own_ref), channel_id=1, source_target_pairs={{0,32},{16,48},{32,64},{48,80},{64,96},{80,112},{96,128},{112,16},... | collective-permute-start | bytes 1843208 | tf_op jit(solution)/shard_map/ppermute | solution.py:44
  9.5 2.1 %collective-permute-start.3 = (bf16[400,768]{1,0:T(8,128)(2,1)}, bf16[400,768]{1,0:T(8,128)(2,1)}, u32[]{:S(2)}, u32[]{:S(2)}) collective-permute-start(bf16[400,768]{1,0:T(8,128)(2,1)} %shard_map.104.other_ref.own_ref), channel_id=1, source_target_pairs={{0,16},{32,48},{64,80},{80,128},{96,112},{112,32},{128,144},{160,1... | collective-permute-start | bytes 1843208 | tf_op jit(solution)/shard_map/ppermute | solution.py:44
  11.6 1.1 copy-done.8
  13.4 1.9 %collective-permute-start.5 = (bf16[400,768]{1,0:T(8,128)(2,1)S(1)}, bf16[400,768]{1,0:T(8,128)(2,1)S(1)}, u32[]{:S(2)}, u32[]{:S(2)}) collective-permute-start(bf16[400,768]{1,0:T(8,128)(2,1)S(1)} %get-tuple-element.23.own_ref.third_ref.same_ref), channel_id=1, source_target_pairs={{0,96},{16,496},{32,0},{48,16},{64,32},{80,48},{96,64},{112,80},{1... | collective-permute-start | bytes 1843208 | tf_op jit(solution)/shard_map/ppermute | solution.py:44
  15.4 1.3 %collective-permute-start.6 = (bf16[400,768]{1,0:T(8,128)(2,1)S(1)}, bf16[400,768]{1,0:T(8,128)(2,1)S(1)}, u32[]{:S(2)}, u32[]{:S(2)}) collective-permute-start(bf16[400,768]{1,0:T(8,128)(2,1)S(1)} %get-tuple-element.23.own_ref.third_ref.same_ref), channel_id=1, source_target_pairs={{0,80},{16,0},{32,496},{48,32},{80,64},{112,96},{128,208},{144,128... | collective-permute-start | bytes 1843208 | tf_op jit(solution)/shard_map/ppermute | solution.py:44
  16.7 1.6 %fusion.3.feat_ref = bf16[384,768]{1,0:T(8,128)(2,1)} fusion(bf16[384,768]{1,0:T(8,128)(2,1)S(1)} %copy-done.8, s32[768]{0:T(1024)S(1)} %fusion.24), kind=kOutput, calls=%fused_computation.5 | convolution fusion | flops 453869568 | bytes 1182720 | tf_op jit(solution)/shard_map/dot_general | solution.py:56
  18.3 4.5 %collective-permute-start.1 = (bf16[384,768]{1,0:T(8,128)(2,1)}, bf16[384,768]{1,0:T(8,128)(2,1)}, u32[]{:S(2)}, u32[]{:S(2)}) collective-permute-start(bf16[384,768]{1,0:T(8,128)(2,1)} %fusion.3.feat_ref), channel_id=1, source_target_pairs={{0,16},{16,0},{32,48},{48,32},{64,80},{80,64},{96,112},{112,96},{1... | collective-permute-start | bytes 1769480 | tf_op jit(solution)/shard_map/ppermute | solution.py:44
  24.7 2.1 %shard_map.105.before_ref = f32[384,768]{1,0:T(8,128)S(1)} custom-call(f32[8]{0:T(128)S(1)} %stack.100.scalar_ref, bf16[400,768]{1,0:T(8,128)(2,1)S(1)} %get-tuple-element.23.own_ref.third_ref.same_ref, bf16[384,128]{1,0:T(8,128)(2,1)S(1)} %convolution_convert_fusion.1.rows_ref, bf16[400,768]{1,0:T(8,128)(2,1)} %shard_map.104.other_ref.own_ref), custom_call_target="tpu_custom_call" | custom-call | flops 1650000000 | bytes 4500000 | tf_op jit(solution)/shard_map/pallas_call | solution.py:62
  26.8 1.0 copy-done.11
  28.1 1.3 %collective-permute-start.2 = (bf16[400,768]{1,0:T(8,128)(2,1)}, bf16[400,768]{1,0:T(8,128)(2,1)}, u32[]{:S(2)}, u32[]{:S(2)}) collective-permute-start(bf16[400,768]{1,0:T(8,128)(2,1)} %collective-permute-done.far_ref), channel_id=1, source_target_pairs={{16,144},{48,64},{80,96},{144,272},{176,192},{208,224},{272,400},{... | collective-permute-start | bytes 1843208 | tf_op jit(solution)/shard_map/ppermute | solution.py:44
  29.4 1.5 %collective-permute-start.4 = (bf16[400,768]{1,0:T(8,128)(2,1)}, bf16[400,768]{1,0:T(8,128)(2,1)}, u32[]{:S(2)}, u32[]{:S(2)}) collective-permute-start(bf16[400,768]{1,0:T(8,128)(2,1)} %collective-permute-done.3.mix_ref), channel_id=1, source_target_pairs={{32,160},{160,288},{288,416},{416,32},{33,161},{161,289},{289,417}... | collective-permute-start | bytes 1843208 | tf_op jit(solution)/shard_map/ppermute | solution.py:44
  31.0 2.1 %collective-permute-start.8 = (bf16[400,768]{1,0:T(8,128)(2,1)}, bf16[400,768]{1,0:T(8,128)(2,1)}, u32[]{:S(2)}, u32[]{:S(2)}) collective-permute-start(bf16[400,768]{1,0:T(8,128)(2,1)} %collective-permute-done.far_ref), channel_id=1, source_target_pairs={{0,16},{32,48},{48,32},{64,80},{80,64},{96,112},{112,96},{128,144}... | collective-permute-start | bytes 1843208 | tf_op jit(solution)/shard_map/ppermute | solution.py:44
  33.1 6.3 %collective-permute-done.5.first_ref.far_ref = bf16[400,768]{1,0:T(8,128)(2,1)S(1)} collective-permute-done((bf16[400,768]{1,0:T(8,128)(2,1)S(1)}, bf16[400,768]{1,0:T(8,128)(2,1)S(1)}, u32[]{:S(2)}, u32[]{:S(2)}) %collective-permute-start.5) | collective-permute-done | bytes 614432 | tf_op jit(solution)/shard_map/ppermute | solution.py:44
  39.4 0.9 copy-done.2
  40.5 2.0 %shard_map.107 = bf16[400,768]{1,0:T(8,128)(2,1)} custom-call(s32[1]{0:T(128)} %bitcast.9.pick_ref, bf16[400,768]{1,0:T(8,128)(2,1)} %copy-done.2, bf16[400,768]{1,0:T(8,128)(2,1)} %copy-done.4, bf16[400,768]{1,0:T(8,128)(2,1)} %copy-done), custom_call_target="tpu_custom_call" | custom-call | bytes 3000000 | tf_op jit(solution)/shard_map/pallas_call | solution.py:77
  42.5 1.3 %copy-done.12 = f32[384,768]{1,0:T(8,128)S(1)} copy-done((f32[384,768]{1,0:T(8,128)S(1)}, f32[384,768]{1,0:T(8,128)}, u32[]{:S(2)}) %copy-start.12) | copy-done | bytes 1179672
  43.7 2.3 %shard_map.106.before_ref = f32[384,768]{1,0:T(8,128)S(1)} custom-call(f32[8]{0:T(128)S(1)} %stack.100.scalar_ref, bf16[400,768]{1,0:T(8,128)(2,1)S(1)} %copy-done.1, bf16[384,128]{1,0:T(8,128)(2,1)S(1)} %convolution_convert_fusion.1.rows_ref, bf16[400,768]{1,0:T(8,128)(2,1)} %collective-permute-done.3.mix_ref, ...), custom_call_target="tpu_custom_call" | custom-call | flops 2860000000 | bytes 7800000 | tf_op jit(solution)/shard_map/pallas_call | solution.py:62
  46.8 2.2 %shard_map.108.before_ref = f32[384,768]{1,0:T(8,128)S(1)} custom-call(f32[8]{0:T(128)S(1)} %stack.100.scalar_ref, bf16[400,768]{1,0:T(8,128)(2,1)S(1)} %copy-done.1, bf16[384,128]{1,0:T(8,128)(2,1)S(1)} %convolution_convert_fusion.1.rows_ref, bf16[400,768]{1,0:T(8,128)(2,1)} %collective-permute-done.8.near_ref, f32[384,768]{1,0:T(8,128)S(1)} %shard_map.106.before_ref), custom_call_target="tpu_custom_call" | custom-call | flops 1760000000 | bytes 4800000 | tf_op jit(solution)/shard_map/pallas_call | solution.py:62
  49.0 3.5 %shard_map.109 = (bf16[384,768]{1,0:T(8,128)(2,1)S(1)}, bf16[384,384]{1,0:T(8,128)(2,1)S(1)}, bf16[384,384]{1,0:T(8,128)(2,1)S(1)}) custom-call(f32[8]{0:T(128)S(1)} %stack.100.scalar_ref, bf16[400,768]{1,0:T(8,128)(2,1)S(1)} %copy-done.1, bf16[384,128]{1,0:T(8,128)(2,1)S(1)} %convolution_convert_fusion.1.rows_ref, ...), custom_call_target="tpu_custom_call" | custom-call | flops 3300000000 | bytes 9000000 | tf_op jit(solution)/shard_map/pallas_call | solution.py:62
  52.6 1.9 %collective-permute-start.9 = (bf16[384,384]{1,0:T(8,128)(2,1)S(1)}, bf16[384,384]{1,0:T(8,128)(2,1)S(1)}, u32[]{:S(2)}, u32[]{:S(2)}) collective-permute-start(bf16[384,384]{1,0:T(8,128)(2,1)S(1)} %get-tuple-element.31), channel_id=1, source_target_pairs={{0,16},{16,0},{32,48},{48,32},{64,80},{80,64},{96,112},{112,96},{1... | collective-permute-start | bytes 884744 | tf_op jit(solution)/shard_map/ppermute | solution.py:44
  54.5 1.5 %shard_map.110 = bf16[384,768]{1,0:T(8,128)(2,1)} custom-call(bf16[384,768]{1,0:T(8,128)(2,1)S(1)} %get-tuple-element.32.dir_ref, bf16[768,768]{1,0:T(8,128)(2,1)S(1)} %copy-done.7), custom_call_target="tpu_custom_call" | custom-call | flops 1650000000 | bytes 4500000 | tf_op jit(solution)/shard_map/pallas_call | solution.py:62
  56.1 2.8 %shard_map.111 = bf16[4,2,96,384]{3,2,1,0:T(8,128)(2,1)} custom-call(bf16[384,384]{1,0:T(8,128)(2,1)S(1)} %get-tuple-element.35.keep_ref, bf16[384,384]{1,0:T(8,128)(2,1)S(1)} %collective-permute-done.9.got_ref, bf16[384,768]{1,0:T(8,128)(2,1)} %fusion.3.feat_ref, bf16[384,768]{1,0:T(8,128)(2,1)} %collective-permute-done.1.feat_near_ref), custom_call_target="tpu_custom_call" | custom-call | flops 1900000000 | bytes 5100000 | tf_op jit(solution)/shard_map/pallas_call | solution.py:210
  58.9 9.4 %all-to-all-start = ((bf16[8,96,384]{2,1,0:T(8,128)(2,1)}), bf16[8,96,384]{2,1,0:T(8,128)(2,1)S(1)}, u32[]{:S(2)}, u32[]{:S(2)}) async-start(bf16[8,96,384]{2,1,0:T(8,128)(2,1)} %bitcast.16), calls=%async_computation | async-start | bytes 1179648 | tf_op jit(solution)/shard_map/all_to_all | solution.py:52
  68.3 1.3 %collective-permute-start.11 = (bf16[400,768]{1,0:T(8,128)(2,1)S(1)}, bf16[400,768]{1,0:T(8,128)(2,1)}, u32[]{:S(2)}, u32[]{:S(2)}) collective-permute-start(bf16[400,768]{1,0:T(8,128)(2,1)S(1)} %copy-done.3), channel_id=1, source_target_pairs={{0,16},{16,0},{32,48},{48,32},{64,80},{80,64},{112,96},{128,144},{... | collective-permute-start | bytes 1843208 | tf_op jit(solution)/shard_map/ppermute | solution.py:44
  69.6 5.1 %collective-permute-start.10 = (bf16[400,768]{1,0:T(8,128)(2,1)}, bf16[400,768]{1,0:T(8,128)(2,1)}, u32[]{:S(2)}, u32[]{:S(2)}) collective-permute-start(bf16[400,768]{1,0:T(8,128)(2,1)} %shard_map.107), channel_id=1, source_target_pairs={{0,496},{32,16},{64,48},{80,464},{96,480},{128,112},{160,144},{192... | collective-permute-start | bytes 1843208 | tf_op jit(solution)/shard_map/ppermute | solution.py:44
  75.1 2.2 %all-to-all-done.parts_ref = bf16[8,96,384]{2,1,0:T(8,128)(2,1)S(1)} async-done(((bf16[8,96,384]{2,1,0:T(8,128)(2,1)}), bf16[8,96,384]{2,1,0:T(8,128)(2,1)S(1)}, u32[]{:S(2)}, u32[]{:S(2)}) %all-to-all-start) | async-done | bytes 589856 | tf_op jit(solution)/shard_map/all_to_all | solution.py:52
  78.1 16.1 %all-to-all-start.1 = ((bf16[32,16,128]{2,1,0:T(8,128)(2,1)}), bf16[32,16,128]{2,1,0:T(8,128)(2,1)S(1)}, u32[]{:S(2)}, u32[]{:S(2)}) async-start(bf16[32,16,128]{2,1,0:T(8,128)(2,1)} %shard_map.112), calls=%async_computation.1 | async-start | bytes 262144 | tf_op jit(solution)/shard_map/all_to_all | solution.py:52
  94.3 4.3 %shard_map.113.before_ref = f32[384,768]{1,0:T(8,128)S(1)} custom-call(f32[8]{0:T(128)S(1)} %stack.113.scalar_ref, bf16[400,768]{1,0:T(8,128)(2,1)} %shard_map.104.other_ref.own_ref, bf16[384,128]{1,0:T(8,128)(2,1)S(1)} %convolution_convert_fusion.rows_ref, bf16[400,768]{1,0:T(8,128)(2,1)S(1)} %copy-done.1, bf16[400,768]{1,0:T(8,128)(2,1)S(1)} %copy-done.5, ...), custom_call_target="tpu_custom_call" | custom-call | flops 5500000256 | bytes 15000000 | tf_op jit(solution)/shard_map/pallas_call | solution.py:62
  98.7 3.6 %shard_map.114 = bf16[384,768]{1,0:T(8,128)(2,1)} custom-call(f32[8]{0:T(128)S(1)} %stack.113.scalar_ref, bf16[400,768]{1,0:T(8,128)(2,1)} %shard_map.104.other_ref.own_ref, bf16[384,128]{1,0:T(8,128)(2,1)S(1)} %convolution_convert_fusion.rows_ref, bf16[400,768]{1,0:T(8,128)(2,1)} %collective-permute-done.10.late_ref, f32[384,768]{1,0:T(8,128)S(1)} %shard_map.113.before_ref, ...), custom_call_target="tpu_custom_call" | custom-call | flops 3300000000 | bytes 9000000 | tf_op jit(solution)/shard_map/pallas_call | solution.py:62
  102.3 4.4 %all-to-all-done.1.parts_ref = bf16[32,16,128]{2,1,0:T(8,128)(2,1)S(1)} async-done(((bf16[32,16,128]{2,1,0:T(8,128)(2,1)}), bf16[32,16,128]{2,1,0:T(8,128)(2,1)S(1)}, u32[]{:S(2)}, u32[]{:S(2)}) %all-to-all-start.1) | async-done | bytes 131104 | tf_op jit(solution)/shard_map/all_to_all | solution.py:52
  (52 shorter events, 5.1 us)
Async XLA Ops:
  0.6 11.0 %copy-start.6 = (bf16[768,768]{1,0:T(8,128)(2,1)S(1)}, bf16[768,768]{1,0:T(8,128)(2,1)}, u32[]{:S(2)}) copy-start(bf16[768,768]{1,0:T(8,128)(2,1)} %head_ref.3) | copy-start | bytes 3538948
  1.4 1.1 copy-start.9
  3.5 24.6 %collective-permute-start = (bf16[400,768]{1,0:T(8,128)(2,1)}, bf16[400,768]{1,0:T(8,128)(2,1)}, u32[]{:S(2)}, u32[]{:S(2)}) collective-permute-start(bf16[400,768]{1,0:T(8,128)(2,1)} %shard_map.104.other_ref.own_ref), channel_id=1, source_target_pairs={{0,32},{16,48},{32,64},{48,80},{64,96},{80,112},{96,128},{112,16},... | collective-permute-start | bytes 1843208 | tf_op jit(solution)/shard_map/ppermute | solution.py:44
  9.5 19.9 %collective-permute-start.3 = (bf16[400,768]{1,0:T(8,128)(2,1)}, bf16[400,768]{1,0:T(8,128)(2,1)}, u32[]{:S(2)}, u32[]{:S(2)}) collective-permute-start(bf16[400,768]{1,0:T(8,128)(2,1)} %shard_map.104.other_ref.own_ref), channel_id=1, source_target_pairs={{0,16},{32,48},{64,80},{80,128},{96,112},{112,32},{128,144},{160,1... | collective-permute-start | bytes 1843208 | tf_op jit(solution)/shard_map/ppermute | solution.py:44
  11.6 1.1 copy-start.8
  13.4 11.3 %copy-start = (bf16[400,768]{1,0:T(8,128)(2,1)}, bf16[400,768]{1,0:T(8,128)(2,1)S(1)}, u32[]{:S(2)}) copy-start(bf16[400,768]{1,0:T(8,128)(2,1)S(1)} %get-tuple-element.23.own_ref.third_ref.same_ref) | copy-start | bytes 1843204
  13.4 26.0 %collective-permute-start.5 = (bf16[400,768]{1,0:T(8,128)(2,1)S(1)}, bf16[400,768]{1,0:T(8,128)(2,1)S(1)}, u32[]{:S(2)}, u32[]{:S(2)}) collective-permute-start(bf16[400,768]{1,0:T(8,128)(2,1)S(1)} %get-tuple-element.23.own_ref.third_ref.same_ref), channel_id=1, source_target_pairs={{0,96},{16,496},{32,0},{48,16},{64,32},{80,48},{96,64},{112,80},{1... | collective-permute-start | bytes 1843208 | tf_op jit(solution)/shard_map/ppermute | solution.py:44
  15.4 24.0 %collective-permute-start.6 = (bf16[400,768]{1,0:T(8,128)(2,1)S(1)}, bf16[400,768]{1,0:T(8,128)(2,1)S(1)}, u32[]{:S(2)}, u32[]{:S(2)}) collective-permute-start(bf16[400,768]{1,0:T(8,128)(2,1)S(1)} %get-tuple-element.23.own_ref.third_ref.same_ref), channel_id=1, source_target_pairs={{0,80},{16,0},{32,496},{48,32},{80,64},{112,96},{128,208},{144,128... | collective-permute-start | bytes 1843208 | tf_op jit(solution)/shard_map/ppermute | solution.py:44
  16.7 6.1 %copy-start.15 = (s32[109]{0:T(128)S(1)}, s32[109]{0:T(128)}, u32[]{:S(2)}) copy-start(s32[109]{0:T(128)} %param.13) | copy-start | bytes 1312
  16.7 6.1 %copy-start.13 = (s32[109,109]{1,0:T(8,128)S(1)}, s32[109,109]{1,0:T(8,128)}, u32[]{:S(2)}) copy-start(s32[109,109]{1,0:T(8,128)} %param.12) | copy-start | bytes 142576
  16.7 6.2 %copy-start.14 = (s32[384]{0:T(512)S(1)}, s32[384]{0:T(512)}, u32[]{:S(2)}) copy-start(s32[384]{0:T(512)} %param.11) | copy-start | bytes 4612
  18.3 9.8 %collective-permute-start.1 = (bf16[384,768]{1,0:T(8,128)(2,1)}, bf16[384,768]{1,0:T(8,128)(2,1)}, u32[]{:S(2)}, u32[]{:S(2)}) collective-permute-start(bf16[384,768]{1,0:T(8,128)(2,1)} %fusion.3.feat_ref), channel_id=1, source_target_pairs={{0,16},{16,0},{32,48},{48,32},{64,80},{80,64},{96,112},{112,96},{1... | collective-permute-start | bytes 1769480 | tf_op jit(solution)/shard_map/ppermute | solution.py:44
  26.8 1.0 copy-start.11
  28.1 18.0 %collective-permute-start.2 = (bf16[400,768]{1,0:T(8,128)(2,1)}, bf16[400,768]{1,0:T(8,128)(2,1)}, u32[]{:S(2)}, u32[]{:S(2)}) collective-permute-start(bf16[400,768]{1,0:T(8,128)(2,1)} %collective-permute-done.far_ref), channel_id=1, source_target_pairs={{16,144},{48,64},{80,96},{144,272},{176,192},{208,224},{272,400},{... | collective-permute-start | bytes 1843208 | tf_op jit(solution)/shard_map/ppermute | solution.py:44
  29.4 16.7 %collective-permute-start.4 = (bf16[400,768]{1,0:T(8,128)(2,1)}, bf16[400,768]{1,0:T(8,128)(2,1)}, u32[]{:S(2)}, u32[]{:S(2)}) collective-permute-start(bf16[400,768]{1,0:T(8,128)(2,1)} %collective-permute-done.3.mix_ref), channel_id=1, source_target_pairs={{32,160},{160,288},{288,416},{416,32},{33,161},{161,289},{289,417}... | collective-permute-start | bytes 1843208 | tf_op jit(solution)/shard_map/ppermute | solution.py:44
  31.0 15.9 %collective-permute-start.8 = (bf16[400,768]{1,0:T(8,128)(2,1)}, bf16[400,768]{1,0:T(8,128)(2,1)}, u32[]{:S(2)}, u32[]{:S(2)}) collective-permute-start(bf16[400,768]{1,0:T(8,128)(2,1)} %collective-permute-done.far_ref), channel_id=1, source_target_pairs={{0,16},{32,48},{48,32},{64,80},{80,64},{96,112},{112,96},{128,144}... | collective-permute-start | bytes 1843208 | tf_op jit(solution)/shard_map/ppermute | solution.py:44
  39.4 0.9 copy-start.2
  39.4 1.1 copy-start.4
  40.5 2.0 %copy-start.1 = (bf16[400,768]{1,0:T(8,128)(2,1)S(1)}, bf16[400,768]{1,0:T(8,128)(2,1)}, u32[]{:S(2)}) copy-start(bf16[400,768]{1,0:T(8,128)(2,1)} %copy-done) | copy-start | bytes 1843204
  42.5 1.3 %copy-start.12 = (f32[384,768]{1,0:T(8,128)S(1)}, f32[384,768]{1,0:T(8,128)}, u32[]{:S(2)}) copy-start(f32[384,768]{1,0:T(8,128)} %copy-done.11) | copy-start | bytes 3538948
  46.1 2.9 %collective-permute-start.7 = (bf16[400,768]{1,0:T(8,128)(2,1)}, bf16[400,768]{1,0:T(8,128)(2,1)S(1)}, u32[]{:S(2)}, u32[]{:S(2)}) collective-permute-start(bf16[400,768]{1,0:T(8,128)(2,1)} %collective-permute-done.2.hop_ref), channel_id=1, source_target_pairs={{16,0},{144,128},{272,256},{400,384},{17,1},{145,129},{273,257},{4... | collective-permute-start | bytes 1843208 | tf_op jit(solution)/shard_map/ppermute | solution.py:44
  49.0 5.5 %copy-start.7 = (bf16[768,768]{1,0:T(8,128)(2,1)S(1)}, bf16[768,768]{1,0:T(8,128)(2,1)}, u32[]{:S(2)}) copy-start(bf16[768,768]{1,0:T(8,128)(2,1)} %head_ref.3) | copy-start | bytes 3538948
  52.6 3.5 %collective-permute-start.9 = (bf16[384,384]{1,0:T(8,128)(2,1)S(1)}, bf16[384,384]{1,0:T(8,128)(2,1)S(1)}, u32[]{:S(2)}, u32[]{:S(2)}) collective-permute-start(bf16[384,384]{1,0:T(8,128)(2,1)S(1)} %get-tuple-element.31), channel_id=1, source_target_pairs={{0,16},{16,0},{32,48},{48,32},{64,80},{80,64},{96,112},{112,96},{1... | collective-permute-start | bytes 884744 | tf_op jit(solution)/shard_map/ppermute | solution.py:44
  58.9 9.4 %copy-start.3 = (bf16[400,768]{1,0:T(8,128)(2,1)S(1)}, bf16[400,768]{1,0:T(8,128)(2,1)}, u32[]{:S(2)}) copy-start(bf16[400,768]{1,0:T(8,128)(2,1)} %copy-done.2) | copy-start | bytes 1843204
  58.9 18.4 %all-to-all-start = ((bf16[8,96,384]{2,1,0:T(8,128)(2,1)}), bf16[8,96,384]{2,1,0:T(8,128)(2,1)S(1)}, u32[]{:S(2)}, u32[]{:S(2)}) async-start(bf16[8,96,384]{2,1,0:T(8,128)(2,1)} %bitcast.16), calls=%async_computation | async-start | bytes 1179648 | tf_op jit(solution)/shard_map/all_to_all | solution.py:52
  68.3 26.0 %collective-permute-start.11 = (bf16[400,768]{1,0:T(8,128)(2,1)S(1)}, bf16[400,768]{1,0:T(8,128)(2,1)}, u32[]{:S(2)}, u32[]{:S(2)}) collective-permute-start(bf16[400,768]{1,0:T(8,128)(2,1)S(1)} %copy-done.3), channel_id=1, source_target_pairs={{0,16},{16,0},{32,48},{48,32},{64,80},{80,64},{112,96},{128,144},{... | collective-permute-start | bytes 1843208 | tf_op jit(solution)/shard_map/ppermute | solution.py:44
  69.6 29.1 %collective-permute-start.10 = (bf16[400,768]{1,0:T(8,128)(2,1)}, bf16[400,768]{1,0:T(8,128)(2,1)}, u32[]{:S(2)}, u32[]{:S(2)}) collective-permute-start(bf16[400,768]{1,0:T(8,128)(2,1)} %shard_map.107), channel_id=1, source_target_pairs={{0,496},{32,16},{64,48},{80,464},{96,480},{128,112},{160,144},{192... | collective-permute-start | bytes 1843208 | tf_op jit(solution)/shard_map/ppermute | solution.py:44
  75.0 19.4 %copy-start.5 = (bf16[400,768]{1,0:T(8,128)(2,1)S(1)}, bf16[400,768]{1,0:T(8,128)(2,1)}, u32[]{:S(2)}) copy-start(bf16[400,768]{1,0:T(8,128)(2,1)} %copy-done.4) | copy-start | bytes 1843204
  78.1 28.6 %all-to-all-start.1 = ((bf16[32,16,128]{2,1,0:T(8,128)(2,1)}), bf16[32,16,128]{2,1,0:T(8,128)(2,1)S(1)}, u32[]{:S(2)}, u32[]{:S(2)}) async-start(bf16[32,16,128]{2,1,0:T(8,128)(2,1)} %shard_map.112), calls=%async_computation.1 | async-start | bytes 262144 | tf_op jit(solution)/shard_map/all_to_all | solution.py:52
  94.3 4.4 %copy-start.10 = (bf16[384,768]{1,0:T(8,128)(2,1)S(1)}, bf16[384,768]{1,0:T(8,128)(2,1)}, u32[]{:S(2)}) copy-start(bf16[384,768]{1,0:T(8,128)(2,1)} %text_ref.3) | copy-start | bytes 1769476

commit v6 on v5

--- a/solution.py
+++ b/solution.py
@@ -89,7 +89,7 @@
 
 
 def put_langs(langs_ref, out_ref):
-    langs = langs_ref[...].astype(jnp.float32)
+    langs = langs_ref[...].reshape(1, ROWS).astype(jnp.float32)
     row = jnp.concatenate([langs, jnp.zeros((1, D - ROWS), jnp.float32)], axis=1)
     out_ref[ROWS:, :] = jnp.broadcast_to(row, (TAIL, D)).astype(jnp.bfloat16)
 
@@ -137,8 +137,8 @@
         )
 
 
-def middle_kernel(scalar_ref, own_ref, rows_ref, mix_ref, far_ref, before_ref, sum_ref):
-    sum_ref[...] = before_ref[...]
+def middle_kernel(scalar_ref, own_ref, rows_ref, same_ref, mix_ref, far_ref, sum_ref):
+    own_kernel(scalar_ref, own_ref, rows_ref, same_ref, sum_ref)
     add_term(scalar_ref, own_ref, rows_ref, mix_ref, scalar_ref[2], sum_ref)
     add_term(scalar_ref, own_ref, rows_ref, far_ref, scalar_ref[3], sum_ref)
 
@@ -176,24 +176,47 @@
     send_ref[...] = turned[HALF:, :]
 
 
+def pair_of_blocks(scalar_ref, own, rows, first_ref, second_ref, keeps, positive, both_ref):
+    both_ref[:ROWS, :] = first_ref[:ROWS, :]
+    both_ref[ROWS:, :] = second_ref[:ROWS, :]
+    langs = [ref[ROWS : ROWS + 1, :ROWS].astype(jnp.int32) for ref in (first_ref, second_ref)]
+    langs = jnp.concatenate(langs, axis=1)
+    hot = lax.broadcasted_iota(jnp.int32, (LABELS, 2 * ROWS), 0) == langs
+    weight = dot(rows, hot.astype(jnp.float32).astype(jnp.bfloat16))
+    column = lax.broadcasted_iota(jnp.int32, (ROWS, 2 * ROWS), 1)
+    weight = weight * jnp.where(column < ROWS, keeps[0], keeps[1])
+    logit = scalar_ref[0] * dot(own, both_ref[...], ((1,), (1,))) + scalar_ref[1]
+    excess = 0.5 + 0.5 * jnp.tanh(0.5 * logit)
+    if positive:
+        row = lax.broadcasted_iota(jnp.int32, (ROWS, 2 * ROWS), 0)
+        excess = jnp.where(row == column, excess - 1.0, excess)
+    return dot((weight * excess).astype(jnp.bfloat16), both_ref[...])
+
+
 def text_middle_kernel(
-    scalar_ref, own_ref, rows_ref, same_ref, mix_ref, far_ref, near_ref, sum_ref
+    scalar_ref, own_ref, rows_ref, same_ref, mix_ref, far_ref, near_ref, sum_ref, both_ref
 ):
-    own_kernel(scalar_ref, own_ref, rows_ref, same_ref, sum_ref)
-    add_term(scalar_ref, own_ref, rows_ref, mix_ref, scalar_ref[2], sum_ref)
-    add_term(scalar_ref, own_ref, rows_ref, far_ref, scalar_ref[3], sum_ref)
-    add_term(scalar_ref, own_ref, rows_ref, near_ref, scalar_ref[4], sum_ref)
+    own, rows = own_ref[:ROWS, :], rows_ref[...]
+    keeps = (1.0, 1.0 - scalar_ref[2])
+    sum_ref[...] = pair_of_blocks(
+        scalar_ref, own, rows, same_ref, mix_ref, keeps, True, both_ref
+    )
+    keeps = (1.0 - scalar_ref[3], 1.0 - scalar_ref[4])
+    sum_ref[...] += pair_of_blocks(
+        scalar_ref, own, rows, far_ref, near_ref, keeps, False, both_ref
+    )
 
 
 def text_last_kernel(
-    scalar_ref, own_ref, rows_ref, late_ref, before_ref, text_ref, out_ref, sum_ref
+    scalar_ref, text_ref, rows_ref, late_ref, before_ref, out_ref, sum_ref, own_ref
 ):
+    text = text_ref[...].astype(jnp.float32)
+    inverse = lax.rsqrt(jnp.sum(text * text, axis=-1, keepdims=True) + EPSILON)
+    unit = text * inverse
+    own_ref[...] = unit.astype(jnp.bfloat16)
     sum_ref[...] = before_ref[...]
     add_term(scalar_ref, own_ref, rows_ref, late_ref, scalar_ref[5], sum_ref)
     grad = scalar_ref[0] * sum_ref[...]
-    text = text_ref[...].astype(jnp.float32)
-    inverse = lax.rsqrt(jnp.sum(text * text, axis=-1, keepdims=True) + EPSILON)
-    unit = text * inverse
     radial = jnp.sum(unit * grad, axis=-1, keepdims=True)
     out_ref[...] = ((grad - unit * radial) * inverse).astype(jnp.bfloat16)
 
@@ -287,12 +310,11 @@
         )
     ]
     image_pick = jnp.where(place == 0, 2, jnp.where(place == 5, 1, 0)).reshape(1)
-    langs = lang_ids.reshape(1, ROWS)
     block = array((ROWS + TAIL, D), jnp.bfloat16)
     total = array((ROWS, D), jnp.float32)
     scratch = [pltpu.VMEM(total.shape, total.dtype)]
 
-    (text_out,) = call(text_kernel, 0.3, [block], (text_emb, langs))
+    (text_out,) = call(text_kernel, 0.3, [block], (text_emb, lang_ids))
     text_far = permute(text_out, lambda i: i + 2 if i % 8 != 7 else i - 6)
     text_mix = permute(
         text_out, lambda i: i + 1 if i % 2 == 0 else {5: i + 3, 7: i - 5}.get(i % 8)
@@ -302,7 +324,7 @@
         image_kernel,
         1.0,
         [block, array((ROWS, 1), jnp.float32)],
-        (image_feat, head_weight, langs),
+        (image_feat, head_weight, lang_ids),
     )
     image_far = permute(image_out, lambda i: i - 2 if i % 8 != 0 else i + 6)
     image_mix = permute(
@@ -315,21 +337,16 @@
     feat_turned = dot(image_feat, order_matrix(row_order()), ((1,), (1,))).astype(jnp.bfloat16)
     feat_near = swap_cores(feat_turned)
     order = order_matrix(column_order(place % 2))
-    (image_sum,) = call(
-        own_kernel, 1.5, [total], (text_scalars, image_out, image_rows, text_out), 1
-    )
-    text_far, feat_near, image_sum, order = lax.optimization_barrier(
-        (text_far, feat_near, image_sum, order)
-    )
+    text_far, feat_near, order = lax.optimization_barrier((text_far, feat_near, order))
 
     text_hop = permute(text_far, lambda i: {1: i + 8, 3: i + 1, 5: i + 1}.get(i % 8))
     text_skip = permute(text_mix, lambda i: {2: i + 8}.get(i % 8))
     text_near = permute(text_far, lambda i: i ^ 1 if i % 8 != 1 else None)
     (image_sum,) = call(
         middle_kernel,
-        2.6,
+        3.6,
         [total],
-        (text_scalars, image_out, image_rows, text_mix, text_far, image_sum),
+        (text_scalars, image_out, image_rows, text_out, text_mix, text_far),
         1,
     )
     image_pass = pick(image_pick, image_far, image_mix, image_out)
@@ -384,14 +401,15 @@
         [total],
         (image_scalars, text_out, text_rows, image_out, image_mix, image_far, image_near),
         1,
+        [pltpu.VMEM((2 * ROWS, D), jnp.bfloat16)],
     )
     (text_back,) = call(
         text_last_kernel,
         3.0,
         [array((ROWS, D), jnp.bfloat16)],
-        (image_scalars, text_out, text_rows, image_late, text_sum, text_emb),
+        (image_scalars, text_emb, text_rows, image_late, text_sum),
         1,
-        scratch,
+        scratch + [pltpu.VMEM((ROWS, D), jnp.bfloat16)],
     )
     return (image_back, text_back, head_grad.T)
 

time: 109 us -> 108 us (level)
  the two profiles are of different devices: /device:TPU:6 before, /device:TPU:8 now
where the time goes in v6:
time: 108 us
  starting transfers between devices  60 us (56%)
  Pallas kernels  25.5 us (24%)
  waiting for transfers between devices  11.8 us (11%)
  local copies, waits for them, and re-layouts  5.29 us (5%)
  between operations  2.46 us (2%)
  matrix products  2.07 us (2%)
    ppermute x12, starting transfers between devices, permute(): lax.ppermute(value, 'blk', [(i, j % N_BLK) for i, j in pairs if j is not...  45.1 us
    pallas_call x10, Pallas kernels, call(): pl.pallas_call(kernel, out_shape=outs, in_specs=[smem] * scalars + [vmem]...  20.8 us
    all_to_all x2, starting transfers between devices, exchange(): lax.all_to_all(value, ('blk', 'lane'), 0, 0, axis_index_groups=groups, ti...  14.9 us
    ppermute x12, waiting for transfers between devices, permute(): lax.ppermute(value, 'blk', [(i, j % N_BLK) for i, j in pairs if j is not...  6.15 us
    all_to_all x2, waiting for transfers between devices, exchange(): lax.all_to_all(value, ('blk', 'lane'), 0, 0, axis_index_groups=groups, ti...  5.65 us
    unnamed x34, local copies, waits for them, and re-layouts  5.12 us
    pallas_call x1, Pallas kernels, head_product(): pl.pallas_call(head_kernel, grid=(2,), out_shape=array((4, 2, 96, HALF),...  2.82 us
  transfers between devices with their start and end apart: 14, of which 4 were waited for; matrix products, arithmetic and copies ran while one was open for 2% of the time, Pallas kernels for 16%

profile of v6, /device:TPU:8, one launch (start us, length us, event | category | flops | bytes accessed | tf_op | source)
XLA Modules:
  0.0 107.5 jit_solution(12317047900434491153)
XLA Ops:
  1.3 1.1 copy-done.11
  2.4 1.1 shard_map.104.same_ref.own_ref
  3.4 3.4 %collective-permute-start = (bf16[400,768]{1,0:T(8,128)(2,1)}, bf16[400,768]{1,0:T(8,128)(2,1)}, u32[]{:S(2)}, u32[]{:S(2)}) collective-permute-start(bf16[400,768]{1,0:T(8,128)(2,1)} %shard_map.104.same_ref.own_ref), channel_id=1, source_target_pairs={{0,32},{16,48},{32,64},{48,80},{64,96},{80,112},{96,128},{112,16},... | collective-permute-start | bytes 1843208 | tf_op jit(solution)/shard_map/ppermute | solution.py:44
  6.8 1.9 %collective-permute-start.3 = (bf16[400,768]{1,0:T(8,128)(2,1)}, bf16[400,768]{1,0:T(8,128)(2,1)}, u32[]{:S(2)}, u32[]{:S(2)}) collective-permute-start(bf16[400,768]{1,0:T(8,128)(2,1)} %shard_map.104.same_ref.own_ref), channel_id=1, source_target_pairs={{0,16},{32,48},{64,80},{80,128},{96,112},{112,32},{128,144},{160,1... | collective-permute-start | bytes 1843208 | tf_op jit(solution)/shard_map/ppermute | solution.py:44
  8.8 1.6 %fusion.3.feat_ref = bf16[384,768]{1,0:T(8,128)(2,1)} fusion(bf16[384,768]{1,0:T(8,128)(2,1)S(1)} %copy-done.10, s32[768]{0:T(1024)S(1)} %fusion.24), kind=kOutput, calls=%fused_computation.5 | convolution fusion | flops 453869568 | bytes 1182720 | tf_op jit(solution)/shard_map/dot_general | solution.py:56
  10.4 2.0 %collective-permute-start.1 = (bf16[384,768]{1,0:T(8,128)(2,1)}, bf16[384,768]{1,0:T(8,128)(2,1)}, u32[]{:S(2)}, u32[]{:S(2)}) collective-permute-start(bf16[384,768]{1,0:T(8,128)(2,1)} %fusion.3.feat_ref), channel_id=1, source_target_pairs={{0,16},{16,0},{32,48},{48,32},{64,80},{80,64},{96,112},{112,96},{1... | collective-permute-start | bytes 1769480 | tf_op jit(solution)/shard_map/ppermute | solution.py:44
  12.5 0.7 shard_map.103
  13.2 7.6 %collective-permute-start.5 = (bf16[400,768]{1,0:T(8,128)(2,1)S(1)}, bf16[400,768]{1,0:T(8,128)(2,1)S(1)}, u32[]{:S(2)}, u32[]{:S(2)}) collective-permute-start(bf16[400,768]{1,0:T(8,128)(2,1)S(1)} %get-tuple-element.22.own_ref.third_ref.same_ref), channel_id=1, source_target_pairs={{0,96},{16,496},{32,0},{48,16},{64,32},{80,48},{96,64},{112,80},{1... | collective-permute-start | bytes 1843208 | tf_op jit(solution)/shard_map/ppermute | solution.py:44
  20.9 3.2 %collective-permute-start.6 = (bf16[400,768]{1,0:T(8,128)(2,1)S(1)}, bf16[400,768]{1,0:T(8,128)(2,1)S(1)}, u32[]{:S(2)}, u32[]{:S(2)}) collective-permute-start(bf16[400,768]{1,0:T(8,128)(2,1)S(1)} %get-tuple-element.22.own_ref.third_ref.same_ref), channel_id=1, source_target_pairs={{0,80},{16,0},{32,496},{48,32},{80,64},{112,96},{128,208},{144,128... | collective-permute-start | bytes 1843208 | tf_op jit(solution)/shard_map/ppermute | solution.py:44
  24.4 5.1 %collective-permute-done.far_ref = bf16[400,768]{1,0:T(8,128)(2,1)} collective-permute-done((bf16[400,768]{1,0:T(8,128)(2,1)}, bf16[400,768]{1,0:T(8,128)(2,1)}, u32[]{:S(2)}, u32[]{:S(2)}) %collective-permute-start) | collective-permute-done | bytes 614432 | tf_op jit(solution)/shard_map/ppermute | solution.py:44
  29.6 1.5 %collective-permute-start.2 = (bf16[400,768]{1,0:T(8,128)(2,1)}, bf16[400,768]{1,0:T(8,128)(2,1)}, u32[]{:S(2)}, u32[]{:S(2)}) collective-permute-start(bf16[400,768]{1,0:T(8,128)(2,1)} %collective-permute-done.far_ref), channel_id=1, source_target_pairs={{16,144},{48,64},{80,96},{144,272},{176,192},{208,224},{272,400},{... | collective-permute-start | bytes 1843208 | tf_op jit(solution)/shard_map/ppermute | solution.py:44
  31.7 1.5 %collective-permute-start.4 = (bf16[400,768]{1,0:T(8,128)(2,1)}, bf16[400,768]{1,0:T(8,128)(2,1)}, u32[]{:S(2)}, u32[]{:S(2)}) collective-permute-start(bf16[400,768]{1,0:T(8,128)(2,1)} %collective-permute-done.3.mix_ref), channel_id=1, source_target_pairs={{32,160},{160,288},{288,416},{416,32},{33,161},{161,289},{289,417}... | collective-permute-start | bytes 1843208 | tf_op jit(solution)/shard_map/ppermute | solution.py:44
  35.0 5.7 %collective-permute-start.8 = (bf16[400,768]{1,0:T(8,128)(2,1)}, bf16[400,768]{1,0:T(8,128)(2,1)}, u32[]{:S(2)}, u32[]{:S(2)}) collective-permute-start(bf16[400,768]{1,0:T(8,128)(2,1)} %collective-permute-done.far_ref), channel_id=1, source_target_pairs={{0,16},{32,48},{48,32},{64,80},{80,64},{96,112},{112,96},{128,144}... | collective-permute-start | bytes 1843208 | tf_op jit(solution)/shard_map/ppermute | solution.py:44
  40.7 4.5 %shard_map.105.before_ref = f32[384,768]{1,0:T(8,128)S(1)} custom-call(f32[8]{0:T(128)S(1)} %stack.100.scalar_ref, bf16[400,768]{1,0:T(8,128)(2,1)S(1)} %get-tuple-element.22.own_ref.third_ref.same_ref, bf16[384,128]{1,0:T(8,128)(2,1)S(1)} %convolution_convert_fusion.1.rows_ref, bf16[400,768]{1,0:T(8,128)(2,1)} %shard_map.104.same_ref.own_ref, ...), custom_call_target="tpu_custom_call" | custom-call | flops 3960000000 | bytes 10800000 | tf_op jit(solution)/shard_map/pallas_call | solution.py:62
  45.2 1.0 copy-done.13
  46.2 0.8 copy-done.2
  47.3 2.0 %shard_map.106 = bf16[400,768]{1,0:T(8,128)(2,1)} custom-call(s32[1]{0:T(128)} %bitcast.9.pick_ref, bf16[400,768]{1,0:T(8,128)(2,1)} %copy-done.2, bf16[400,768]{1,0:T(8,128)(2,1)} %copy-done.4, bf16[400,768]{1,0:T(8,128)(2,1)} %copy-done), custom_call_target="tpu_custom_call" | custom-call | bytes 3000000 | tf_op jit(solution)/shard_map/pallas_call | solution.py:77
  49.3 1.3 %collective-permute-start.7 = (bf16[400,768]{1,0:T(8,128)(2,1)}, bf16[400,768]{1,0:T(8,128)(2,1)S(1)}, u32[]{:S(2)}, u32[]{:S(2)}) collective-permute-start(bf16[400,768]{1,0:T(8,128)(2,1)} %collective-permute-done.2.hop_ref), channel_id=1, source_target_pairs={{16,0},{144,128},{272,256},{400,384},{17,1},{145,129},{273,257},{4... | collective-permute-start | bytes 1843208 | tf_op jit(solution)/shard_map/ppermute | solution.py:44
  50.6 1.3 %copy-done.14 = f32[384,768]{1,0:T(8,128)S(1)} copy-done((f32[384,768]{1,0:T(8,128)S(1)}, f32[384,768]{1,0:T(8,128)}, u32[]{:S(2)}) %copy-start.14) | copy-done | bytes 1179672
  51.8 1.2 %shard_map.107.before_ref = f32[384,768]{1,0:T(8,128)S(1)} custom-call(f32[8]{0:T(128)S(1)} %stack.100.scalar_ref, bf16[400,768]{1,0:T(8,128)(2,1)S(1)} %copy-done.1, bf16[384,128]{1,0:T(8,128)(2,1)S(1)} %convolution_convert_fusion.1.rows_ref, bf16[400,768]{1,0:T(8,128)(2,1)} %collective-permute-done.8.near_ref, f32[384,768]{1,0:T(8,128)S(1)} %copy-done.14), custom_call_target="tpu_custom_call" | custom-call | flops 1760000000 | bytes 4800000 | tf_op jit(solution)/shard_map/pallas_call | solution.py:62
  53.4 3.5 %shard_map.108 = (bf16[384,768]{1,0:T(8,128)(2,1)S(1)}, bf16[384,384]{1,0:T(8,128)(2,1)S(1)}, bf16[384,384]{1,0:T(8,128)(2,1)S(1)}) custom-call(f32[8]{0:T(128)S(1)} %stack.100.scalar_ref, bf16[400,768]{1,0:T(8,128)(2,1)S(1)} %copy-done.1, bf16[384,128]{1,0:T(8,128)(2,1)S(1)} %convolution_convert_fusion.1.rows_ref, ...), custom_call_target="tpu_custom_call" | custom-call | flops 3300000000 | bytes 9000000 | tf_op jit(solution)/shard_map/pallas_call | solution.py:62
  56.9 3.7 %collective-permute-start.9 = (bf16[384,384]{1,0:T(8,128)(2,1)S(1)}, bf16[384,384]{1,0:T(8,128)(2,1)S(1)}, u32[]{:S(2)}, u32[]{:S(2)}) collective-permute-start(bf16[384,384]{1,0:T(8,128)(2,1)S(1)} %get-tuple-element.29), channel_id=1, source_target_pairs={{0,16},{16,0},{32,48},{48,32},{64,80},{80,64},{96,112},{112,96},{1... | collective-permute-start | bytes 884744 | tf_op jit(solution)/shard_map/ppermute | solution.py:44
  60.7 1.5 %shard_map.109 = bf16[384,768]{1,0:T(8,128)(2,1)} custom-call(bf16[384,768]{1,0:T(8,128)(2,1)S(1)} %get-tuple-element.30.dir_ref, bf16[768,768]{1,0:T(8,128)(2,1)S(1)} %copy-done.9), custom_call_target="tpu_custom_call" | custom-call | flops 1650000000 | bytes 4500000 | tf_op jit(solution)/shard_map/pallas_call | solution.py:62
  62.1 2.8 %shard_map.110 = bf16[4,2,96,384]{3,2,1,0:T(8,128)(2,1)} custom-call(bf16[384,384]{1,0:T(8,128)(2,1)S(1)} %get-tuple-element.33.keep_ref, bf16[384,384]{1,0:T(8,128)(2,1)S(1)} %collective-permute-done.9.got_ref, bf16[384,768]{1,0:T(8,128)(2,1)} %fusion.3.feat_ref, bf16[384,768]{1,0:T(8,128)(2,1)} %collective-permute-done.1.feat_near_ref), custom_call_target="tpu_custom_call" | custom-call | flops 1900000000 | bytes 5100000 | tf_op jit(solution)/shard_map/pallas_call | solution.py:233
  65.0 4.0 %all-to-all-start = ((bf16[8,96,384]{2,1,0:T(8,128)(2,1)}), bf16[8,96,384]{2,1,0:T(8,128)(2,1)S(1)}, u32[]{:S(2)}, u32[]{:S(2)}) async-start(bf16[8,96,384]{2,1,0:T(8,128)(2,1)} %bitcast.16), calls=%async_computation | async-start | bytes 1179648 | tf_op jit(solution)/shard_map/all_to_all | solution.py:52
  69.0 1.9 %collective-permute-start.11 = (bf16[400,768]{1,0:T(8,128)(2,1)S(1)}, bf16[400,768]{1,0:T(8,128)(2,1)}, u32[]{:S(2)}, u32[]{:S(2)}) collective-permute-start(bf16[400,768]{1,0:T(8,128)(2,1)S(1)} %copy-done.3), channel_id=1, source_target_pairs={{0,16},{16,0},{32,48},{48,32},{64,80},{80,64},{112,96},{128,144},{... | collective-permute-start | bytes 1843208 | tf_op jit(solution)/shard_map/ppermute | solution.py:44
  70.9 11.3 %collective-permute-start.10 = (bf16[400,768]{1,0:T(8,128)(2,1)}, bf16[400,768]{1,0:T(8,128)(2,1)}, u32[]{:S(2)}, u32[]{:S(2)}) collective-permute-start(bf16[400,768]{1,0:T(8,128)(2,1)} %shard_map.106), channel_id=1, source_target_pairs={{0,496},{32,16},{64,48},{80,464},{96,480},{128,112},{160,144},{192... | collective-permute-start | bytes 1843208 | tf_op jit(solution)/shard_map/ppermute | solution.py:44
  82.6 0.8 shard_map.111
  83.5 10.8 %all-to-all-start.1 = ((bf16[32,16,128]{2,1,0:T(8,128)(2,1)}), bf16[32,16,128]{2,1,0:T(8,128)(2,1)S(1)}, u32[]{:S(2)}, u32[]{:S(2)}) async-start(bf16[32,16,128]{2,1,0:T(8,128)(2,1)} %shard_map.111), calls=%async_computation.1 | async-start | bytes 262144 | tf_op jit(solution)/shard_map/all_to_all | solution.py:52
  94.3 4.3 %shard_map.112.before_ref = f32[384,768]{1,0:T(8,128)S(1)} custom-call(f32[8]{0:T(128)S(1)} %stack.113.scalar_ref, bf16[400,768]{1,0:T(8,128)(2,1)} %shard_map.104.same_ref.own_ref, bf16[384,128]{1,0:T(8,128)(2,1)S(1)} %convolution_convert_fusion.rows_ref, bf16[400,768]{1,0:T(8,128)(2,1)S(1)} %copy-done.1, bf16[400,768]{1,0:T(8,128)(2,1)S(1)} %copy-done.5, ...), custom_call_target="tpu_custom_call" | custom-call | flops 5500000256 | bytes 15000000 | tf_op jit(solution)/shard_map/pallas_call | solution.py:62
  98.7 2.5 %shard_map.113 = bf16[384,768]{1,0:T(8,128)(2,1)} custom-call(f32[8]{0:T(128)S(1)} %stack.113.scalar_ref, bf16[384,768]{1,0:T(8,128)(2,1)S(1)} %copy-done.12, bf16[384,128]{1,0:T(8,128)(2,1)S(1)} %convolution_convert_fusion.rows_ref, bf16[400,768]{1,0:T(8,128)(2,1)} %collective-permute-done.10.late_ref, f32[384,768]{1,0:T(8,128)S(1)} %shard_map.112.before_ref), custom_call_target="tpu_custom_call" | custom-call | flops 3300000000 | bytes 9000000 | tf_op jit(solution)/shard_map/pallas_call | solution.py:62
  101.2 5.6 %all-to-all-done.1.parts_ref = bf16[32,16,128]{2,1,0:T(8,128)(2,1)S(1)} async-done(((bf16[32,16,128]{2,1,0:T(8,128)(2,1)}), bf16[32,16,128]{2,1,0:T(8,128)(2,1)S(1)}, u32[]{:S(2)}, u32[]{:S(2)}) %all-to-all-start.1) | async-done | bytes 131104 | tf_op jit(solution)/shard_map/all_to_all | solution.py:52
  (52 shorter events, 3.7 us)
Async XLA Ops:
  0.6 0.7 copy-start.6
  1.3 1.1 copy-start.11
  2.4 6.4 %copy-start.10 = (bf16[384,768]{1,0:T(8,128)(2,1)S(1)}, bf16[384,768]{1,0:T(8,128)(2,1)}, u32[]{:S(2)}) copy-start(bf16[384,768]{1,0:T(8,128)(2,1)} %feat_ref.1) | copy-start | bytes 1769476
  3.4 26.1 %collective-permute-start = (bf16[400,768]{1,0:T(8,128)(2,1)}, bf16[400,768]{1,0:T(8,128)(2,1)}, u32[]{:S(2)}, u32[]{:S(2)}) collective-permute-start(bf16[400,768]{1,0:T(8,128)(2,1)} %shard_map.104.same_ref.own_ref), channel_id=1, source_target_pairs={{0,32},{16,48},{32,64},{48,80},{64,96},{80,112},{96,128},{112,16},... | collective-permute-start | bytes 1843208 | tf_op jit(solution)/shard_map/ppermute | solution.py:44
  6.8 24.8 %collective-permute-start.3 = (bf16[400,768]{1,0:T(8,128)(2,1)}, bf16[400,768]{1,0:T(8,128)(2,1)}, u32[]{:S(2)}, u32[]{:S(2)}) collective-permute-start(bf16[400,768]{1,0:T(8,128)(2,1)} %shard_map.104.same_ref.own_ref), channel_id=1, source_target_pairs={{0,16},{32,48},{64,80},{80,128},{96,112},{112,32},{128,144},{160,1... | collective-permute-start | bytes 1843208 | tf_op jit(solution)/shard_map/ppermute | solution.py:44
  8.8 3.7 %copy-start.7 = (s32[384]{0:T(512)S(1)}, s32[384]{0:T(512)}, u32[]{:S(2)}) copy-start(s32[384]{0:T(512)} %langs_ref.3) | copy-start | bytes 4612
  8.8 3.7 %copy-start.8 = (bf16[768,768]{1,0:T(8,128)(2,1)S(1)}, bf16[768,768]{1,0:T(8,128)(2,1)}, u32[]{:S(2)}) copy-start(bf16[768,768]{1,0:T(8,128)(2,1)} %head_ref.3) | copy-start | bytes 3538948
  10.4 13.7 %copy-start.16 = (s32[109]{0:T(128)S(1)}, s32[109]{0:T(128)}, u32[]{:S(2)}) copy-start(s32[109]{0:T(128)} %param.13) | copy-start | bytes 1312
  10.4 14.0 %collective-permute-start.1 = (bf16[384,768]{1,0:T(8,128)(2,1)}, bf16[384,768]{1,0:T(8,128)(2,1)}, u32[]{:S(2)}, u32[]{:S(2)}) collective-permute-start(bf16[384,768]{1,0:T(8,128)(2,1)} %fusion.3.feat_ref), channel_id=1, source_target_pairs={{0,16},{16,0},{32,48},{48,32},{64,80},{80,64},{96,112},{112,96},{1... | collective-permute-start | bytes 1769480 | tf_op jit(solution)/shard_map/ppermute | solution.py:44
  13.2 31.9 %copy-start = (bf16[400,768]{1,0:T(8,128)(2,1)}, bf16[400,768]{1,0:T(8,128)(2,1)S(1)}, u32[]{:S(2)}) copy-start(bf16[400,768]{1,0:T(8,128)(2,1)S(1)} %get-tuple-element.22.own_ref.third_ref.same_ref) | copy-start | bytes 1843204
  13.2 19.9 %copy-start.15 = (s32[109,109]{1,0:T(8,128)S(1)}, s32[109,109]{1,0:T(8,128)}, u32[]{:S(2)}) copy-start(s32[109,109]{1,0:T(8,128)} %param.12) | copy-start | bytes 142576
  13.2 33.0 %collective-permute-start.5 = (bf16[400,768]{1,0:T(8,128)(2,1)S(1)}, bf16[400,768]{1,0:T(8,128)(2,1)S(1)}, u32[]{:S(2)}, u32[]{:S(2)}) collective-permute-start(bf16[400,768]{1,0:T(8,128)(2,1)S(1)} %get-tuple-element.22.own_ref.third_ref.same_ref), channel_id=1, source_target_pairs={{0,96},{16,496},{32,0},{48,16},{64,32},{80,48},{96,64},{112,80},{1... | collective-permute-start | bytes 1843208 | tf_op jit(solution)/shard_map/ppermute | solution.py:44
  20.9 25.4 %collective-permute-start.6 = (bf16[400,768]{1,0:T(8,128)(2,1)S(1)}, bf16[400,768]{1,0:T(8,128)(2,1)S(1)}, u32[]{:S(2)}, u32[]{:S(2)}) collective-permute-start(bf16[400,768]{1,0:T(8,128)(2,1)S(1)} %get-tuple-element.22.own_ref.third_ref.same_ref), channel_id=1, source_target_pairs={{0,80},{16,0},{32,496},{48,32},{80,64},{112,96},{128,208},{144,128... | collective-permute-start | bytes 1843208 | tf_op jit(solution)/shard_map/ppermute | solution.py:44
  29.6 19.7 %collective-permute-start.2 = (bf16[400,768]{1,0:T(8,128)(2,1)}, bf16[400,768]{1,0:T(8,128)(2,1)}, u32[]{:S(2)}, u32[]{:S(2)}) collective-permute-start(bf16[400,768]{1,0:T(8,128)(2,1)} %collective-permute-done.far_ref), channel_id=1, source_target_pairs={{16,144},{48,64},{80,96},{144,272},{176,192},{208,224},{272,400},{... | collective-permute-start | bytes 1843208 | tf_op jit(solution)/shard_map/ppermute | solution.py:44
  31.7 17.6 %collective-permute-start.4 = (bf16[400,768]{1,0:T(8,128)(2,1)}, bf16[400,768]{1,0:T(8,128)(2,1)}, u32[]{:S(2)}, u32[]{:S(2)}) collective-permute-start(bf16[400,768]{1,0:T(8,128)(2,1)} %collective-permute-done.3.mix_ref), channel_id=1, source_target_pairs={{32,160},{160,288},{288,416},{416,32},{33,161},{161,289},{289,417}... | collective-permute-start | bytes 1843208 | tf_op jit(solution)/shard_map/ppermute | solution.py:44
  35.0 15.6 %collective-permute-start.8 = (bf16[400,768]{1,0:T(8,128)(2,1)}, bf16[400,768]{1,0:T(8,128)(2,1)}, u32[]{:S(2)}, u32[]{:S(2)}) collective-permute-start(bf16[400,768]{1,0:T(8,128)(2,1)} %collective-permute-done.far_ref), channel_id=1, source_target_pairs={{0,16},{32,48},{48,32},{64,80},{80,64},{96,112},{112,96},{128,144}... | collective-permute-start | bytes 1843208 | tf_op jit(solution)/shard_map/ppermute | solution.py:44
  45.2 1.0 copy-start.13
  46.2 0.8 copy-start.2
  46.2 1.0 copy-start.4
  47.3 3.3 %copy-start.1 = (bf16[400,768]{1,0:T(8,128)(2,1)S(1)}, bf16[400,768]{1,0:T(8,128)(2,1)}, u32[]{:S(2)}) copy-start(bf16[400,768]{1,0:T(8,128)(2,1)} %copy-done) | copy-start | bytes 1843204
  49.3 4.1 %collective-permute-start.7 = (bf16[400,768]{1,0:T(8,128)(2,1)}, bf16[400,768]{1,0:T(8,128)(2,1)S(1)}, u32[]{:S(2)}, u32[]{:S(2)}) collective-permute-start(bf16[400,768]{1,0:T(8,128)(2,1)} %collective-permute-done.2.hop_ref), channel_id=1, source_target_pairs={{16,0},{144,128},{272,256},{400,384},{17,1},{145,129},{273,257},{4... | collective-permute-start | bytes 1843208 | tf_op jit(solution)/shard_map/ppermute | solution.py:44
  50.6 1.3 %copy-start.14 = (f32[384,768]{1,0:T(8,128)S(1)}, f32[384,768]{1,0:T(8,128)}, u32[]{:S(2)}) copy-start(f32[384,768]{1,0:T(8,128)} %copy-done.13) | copy-start | bytes 3538948
  53.4 7.3 %copy-start.9 = (bf16[768,768]{1,0:T(8,128)(2,1)S(1)}, bf16[768,768]{1,0:T(8,128)(2,1)}, u32[]{:S(2)}) copy-start(bf16[768,768]{1,0:T(8,128)(2,1)} %head_ref.3) | copy-start | bytes 3538948
  56.9 5.2 %collective-permute-start.9 = (bf16[384,384]{1,0:T(8,128)(2,1)S(1)}, bf16[384,384]{1,0:T(8,128)(2,1)S(1)}, u32[]{:S(2)}, u32[]{:S(2)}) collective-permute-start(bf16[384,384]{1,0:T(8,128)(2,1)S(1)} %get-tuple-element.29), channel_id=1, source_target_pairs={{0,16},{16,0},{32,48},{48,32},{64,80},{80,64},{96,112},{112,96},{1... | collective-permute-start | bytes 884744 | tf_op jit(solution)/shard_map/ppermute | solution.py:44
  65.0 4.0 %copy-start.3 = (bf16[400,768]{1,0:T(8,128)(2,1)S(1)}, bf16[400,768]{1,0:T(8,128)(2,1)}, u32[]{:S(2)}) copy-start(bf16[400,768]{1,0:T(8,128)(2,1)} %copy-done.2) | copy-start | bytes 1843204
  65.0 17.7 %all-to-all-start = ((bf16[8,96,384]{2,1,0:T(8,128)(2,1)}), bf16[8,96,384]{2,1,0:T(8,128)(2,1)S(1)}, u32[]{:S(2)}, u32[]{:S(2)}) async-start(bf16[8,96,384]{2,1,0:T(8,128)(2,1)} %bitcast.16), calls=%async_computation | async-start | bytes 1179648 | tf_op jit(solution)/shard_map/all_to_all | solution.py:52
  69.0 25.3 %collective-permute-start.11 = (bf16[400,768]{1,0:T(8,128)(2,1)S(1)}, bf16[400,768]{1,0:T(8,128)(2,1)}, u32[]{:S(2)}, u32[]{:S(2)}) collective-permute-start(bf16[400,768]{1,0:T(8,128)(2,1)S(1)} %copy-done.3), channel_id=1, source_target_pairs={{0,16},{16,0},{32,48},{48,32},{64,80},{80,64},{112,96},{128,144},{... | collective-permute-start | bytes 1843208 | tf_op jit(solution)/shard_map/ppermute | solution.py:44
  70.9 27.7 %collective-permute-start.10 = (bf16[400,768]{1,0:T(8,128)(2,1)}, bf16[400,768]{1,0:T(8,128)(2,1)}, u32[]{:S(2)}, u32[]{:S(2)}) collective-permute-start(bf16[400,768]{1,0:T(8,128)(2,1)} %shard_map.106), channel_id=1, source_target_pairs={{0,496},{32,16},{64,48},{80,464},{96,480},{128,112},{160,144},{192... | collective-permute-start | bytes 1843208 | tf_op jit(solution)/shard_map/ppermute | solution.py:44
  82.5 11.8 %copy-start.5 = (bf16[400,768]{1,0:T(8,128)(2,1)S(1)}, bf16[400,768]{1,0:T(8,128)(2,1)}, u32[]{:S(2)}) copy-start(bf16[400,768]{1,0:T(8,128)(2,1)} %copy-done.4) | copy-start | bytes 1843204
  83.5 23.4 %all-to-all-start.1 = ((bf16[32,16,128]{2,1,0:T(8,128)(2,1)}), bf16[32,16,128]{2,1,0:T(8,128)(2,1)S(1)}, u32[]{:S(2)}, u32[]{:S(2)}) async-start(bf16[32,16,128]{2,1,0:T(8,128)(2,1)} %shard_map.111), calls=%async_computation.1 | async-start | bytes 262144 | tf_op jit(solution)/shard_map/all_to_all | solution.py:52
  94.3 4.4 %copy-start.12 = (bf16[384,768]{1,0:T(8,128)(2,1)S(1)}, bf16[384,768]{1,0:T(8,128)(2,1)}, u32[]{:S(2)}) copy-start(bf16[384,768]{1,0:T(8,128)(2,1)} %text_ref.3) | copy-start | bytes 1769476

commit v7 on v6

--- a/solution.py
+++ b/solution.py
@@ -143,11 +143,6 @@
     add_term(scalar_ref, own_ref, rows_ref, far_ref, scalar_ref[3], sum_ref)
 
 
-def near_kernel(scalar_ref, own_ref, rows_ref, near_ref, before_ref, sum_ref):
-    sum_ref[...] = before_ref[...]
-    add_term(scalar_ref, own_ref, rows_ref, near_ref, scalar_ref[4], sum_ref)
-
-
 def pick_kernel(pick_ref, first_ref, second_ref, third_ref, out_ref, sem_ref):
     for index, ref in enumerate((first_ref, second_ref, third_ref)):
 
@@ -159,10 +154,11 @@
 
 
 def image_last_kernel(
-    scalar_ref, own_ref, rows_ref, hop_ref, skip_ref, corner_ref, before_ref, inv_ref, order_ref,
-    dir_ref, keep_ref, send_ref, sum_ref,
+    scalar_ref, own_ref, rows_ref, hop_ref, skip_ref, corner_ref, near_ref, before_ref, inv_ref,
+    order_ref, dir_ref, keep_ref, send_ref, sum_ref,
 ):
     sum_ref[...] = before_ref[...]
+    add_term(scalar_ref, own_ref, rows_ref, near_ref, scalar_ref[4], sum_ref)
     add_term(scalar_ref, own_ref, rows_ref, hop_ref, scalar_ref[6], sum_ref)
     add_term(scalar_ref, own_ref, rows_ref, skip_ref, scalar_ref[7], sum_ref)
     add_term(scalar_ref, own_ref, rows_ref, corner_ref, 1.0 - scalar_ref[4], sum_ref)
@@ -354,21 +350,14 @@
         (text_hop, text_skip, image_sum, image_pass)
     )
     text_corner = permute(text_hop, lambda i: {1: i - 1}.get(i % 8))
-    (image_sum,) = call(
-        near_kernel,
-        1.6,
-        [total],
-        (text_scalars, image_out, image_rows, text_near, image_sum),
-        1,
-    )
     half = array((HALF, ROWS), jnp.bfloat16)
     image_dir, keep, send = call(
         image_last_kernel,
         3.0,
         [array((ROWS, D), jnp.bfloat16), half, half],
         (
-            text_scalars, image_out, image_rows, text_hop, text_skip, text_corner, image_sum,
-            image_inv, order,
+            text_scalars, image_out, image_rows, text_hop, text_skip, text_corner, text_near,
+            image_sum, image_inv, order,
         ),
         1,
         scratch,

time: 108 us -> 109 us (level)
  waiting for transfers between devices: 11.8 us -> 15.3 us
  local copies, waits for them, and re-layouts: 5.29 us -> 4.1 us
  Pallas kernels: 25.5 us -> 24.4 us
    ppermute x12, waiting for transfers between devices: 6.15 us -> 10.4 us  [permute(): lax.ppermute(value, 'blk', [(i, j % N_BLK) for i, j in pairs if j is not...]
    all_to_all x2, starting transfers between devices: 14.9 us -> 13.3 us  [exchange(): lax.all_to_all(value, ('blk', 'lane'), 0, 0, axis_index_groups=groups, ti...]
    unnamed x34 -> x32, local copies, waits for them, and re-layouts: 5.12 us -> 3.92 us
    ppermute x12, starting transfers between devices: 45.1 us -> 46.3 us  [permute(): lax.ppermute(value, 'blk', [(i, j % N_BLK) for i, j in pairs if j is not...]
    pallas_call x10 -> x9, Pallas kernels: 20.8 us -> 19.7 us  [call(): pl.pallas_call(kernel, out_shape=outs, in_specs=[smem] * scalars + [vmem]...]
  transfers between devices with their start and end apart: 14 -> 14, of which waited for: 4 -> 6; matrix products, arithmetic and copies ran while one was open for 2% -> 2% of each run, Pallas kernels for 16% -> 15%
where the time goes in v7:
time: 109 us; the launch traced here: 108 us
  starting transfers between devices  59.6 us (55%)
  Pallas kernels  24.4 us (22%)
  waiting for transfers between devices  15.3 us (14%)
  local copies, waits for them, and re-layouts  4.1 us (4%)
  between operations  2.42 us (2%)
  matrix products  2.07 us (2%)
    ppermute x12, starting transfers between devices, permute(): lax.ppermute(value, 'blk', [(i, j % N_BLK) for i, j in pairs if j is not...  46.3 us
    pallas_call x9, Pallas kernels, call(): pl.pallas_call(kernel, out_shape=outs, in_specs=[smem] * scalars + [vmem]...  19.7 us
    all_to_all x2, starting transfers between devices, exchange(): lax.all_to_all(value, ('blk', 'lane'), 0, 0, axis_index_groups=groups, ti...  13.3 us
    ppermute x12, waiting for transfers between devices, permute(): lax.ppermute(value, 'blk', [(i, j % N_BLK) for i, j in pairs if j is not...  10.4 us
    all_to_all x2, waiting for transfers between devices, exchange(): lax.all_to_all(value, ('blk', 'lane'), 0, 0, axis_index_groups=groups, ti...  4.84 us
    unnamed x32, local copies, waits for them, and re-layouts  3.92 us
    pallas_call x1, Pallas kernels, head_product(): pl.pallas_call(head_kernel, grid=(2,), out_shape=array((4, 2, 96, HALF),...  2.82 us
  transfers between devices with their start and end apart: 14, of which 6 were waited for; matrix products, arithmetic and copies ran while one was open for 2% of the time, Pallas kernels for 15%

profile of v7, /device:TPU:8, one launch (start us, length us, event | category | flops | bytes accessed | tf_op | source)
XLA Modules:
  0.0 108.3 jit_solution(16031069626108417031)
XLA Ops:
  1.3 1.1 copy-done.12
  2.4 1.0 shard_map.104.same_ref.own_ref
  3.4 3.4 %collective-permute-start = (bf16[400,768]{1,0:T(8,128)(2,1)}, bf16[400,768]{1,0:T(8,128)(2,1)}, u32[]{:S(2)}, u32[]{:S(2)}) collective-permute-start(bf16[400,768]{1,0:T(8,128)(2,1)} %shard_map.104.same_ref.own_ref), channel_id=1, source_target_pairs={{0,32},{16,48},{32,64},{48,80},{64,96},{80,112},{96,128},{112,16},... | collective-permute-start | bytes 1843208 | tf_op jit(solution)/shard_map/ppermute | solution.py:44
  6.8 1.9 %collective-permute-start.3 = (bf16[400,768]{1,0:T(8,128)(2,1)}, bf16[400,768]{1,0:T(8,128)(2,1)}, u32[]{:S(2)}, u32[]{:S(2)}) collective-permute-start(bf16[400,768]{1,0:T(8,128)(2,1)} %shard_map.104.same_ref.own_ref), channel_id=1, source_target_pairs={{0,16},{32,48},{64,80},{80,128},{96,112},{112,32},{128,144},{160,1... | collective-permute-start | bytes 1843208 | tf_op jit(solution)/shard_map/ppermute | solution.py:44
  8.8 1.6 %fusion.3.feat_ref = bf16[384,768]{1,0:T(8,128)(2,1)} fusion(bf16[384,768]{1,0:T(8,128)(2,1)S(1)} %copy-done.11, s32[768]{0:T(1024)S(1)} %fusion.24), kind=kOutput, calls=%fused_computation.5 | convolution fusion | flops 453869568 | bytes 1182720 | tf_op jit(solution)/shard_map/dot_general | solution.py:56
  10.4 2.0 %collective-permute-start.1 = (bf16[384,768]{1,0:T(8,128)(2,1)}, bf16[384,768]{1,0:T(8,128)(2,1)}, u32[]{:S(2)}, u32[]{:S(2)}) collective-permute-start(bf16[384,768]{1,0:T(8,128)(2,1)} %fusion.3.feat_ref), channel_id=1, source_target_pairs={{0,16},{16,0},{32,48},{48,32},{64,80},{80,64},{96,112},{112,96},{1... | collective-permute-start | bytes 1769480 | tf_op jit(solution)/shard_map/ppermute | solution.py:44
  13.2 7.6 %collective-permute-start.5 = (bf16[400,768]{1,0:T(8,128)(2,1)S(1)}, bf16[400,768]{1,0:T(8,128)(2,1)S(1)}, u32[]{:S(2)}, u32[]{:S(2)}) collective-permute-start(bf16[400,768]{1,0:T(8,128)(2,1)S(1)} %get-tuple-element.22.own_ref.third_ref.same_ref), channel_id=1, source_target_pairs={{0,96},{16,496},{32,0},{48,16},{64,32},{80,48},{96,64},{112,80},{1... | collective-permute-start | bytes 1843208 | tf_op jit(solution)/shard_map/ppermute | solution.py:44
  20.8 3.2 %collective-permute-start.6 = (bf16[400,768]{1,0:T(8,128)(2,1)S(1)}, bf16[400,768]{1,0:T(8,128)(2,1)S(1)}, u32[]{:S(2)}, u32[]{:S(2)}) collective-permute-start(bf16[400,768]{1,0:T(8,128)(2,1)S(1)} %get-tuple-element.22.own_ref.third_ref.same_ref), channel_id=1, source_target_pairs={{0,80},{16,0},{32,496},{48,32},{80,64},{112,96},{128,208},{144,128... | collective-permute-start | bytes 1843208 | tf_op jit(solution)/shard_map/ppermute | solution.py:44
  24.4 5.1 %collective-permute-done.far_ref = bf16[400,768]{1,0:T(8,128)(2,1)} collective-permute-done((bf16[400,768]{1,0:T(8,128)(2,1)}, bf16[400,768]{1,0:T(8,128)(2,1)}, u32[]{:S(2)}, u32[]{:S(2)}) %collective-permute-start) | collective-permute-done | bytes 614432 | tf_op jit(solution)/shard_map/ppermute | solution.py:44
  29.5 1.5 %collective-permute-start.2 = (bf16[400,768]{1,0:T(8,128)(2,1)}, bf16[400,768]{1,0:T(8,128)(2,1)}, u32[]{:S(2)}, u32[]{:S(2)}) collective-permute-start(bf16[400,768]{1,0:T(8,128)(2,1)} %collective-permute-done.far_ref), channel_id=1, source_target_pairs={{16,144},{48,64},{80,96},{144,272},{176,192},{208,224},{272,400},{... | collective-permute-start | bytes 1843208 | tf_op jit(solution)/shard_map/ppermute | solution.py:44
  31.6 1.5 %collective-permute-start.4 = (bf16[400,768]{1,0:T(8,128)(2,1)}, bf16[400,768]{1,0:T(8,128)(2,1)}, u32[]{:S(2)}, u32[]{:S(2)}) collective-permute-start(bf16[400,768]{1,0:T(8,128)(2,1)} %collective-permute-done.3.mix_ref), channel_id=1, source_target_pairs={{32,160},{160,288},{288,416},{416,32},{33,161},{161,289},{289,417}... | collective-permute-start | bytes 1843208 | tf_op jit(solution)/shard_map/ppermute | solution.py:44
  34.9 5.7 %collective-permute-start.8 = (bf16[400,768]{1,0:T(8,128)(2,1)}, bf16[400,768]{1,0:T(8,128)(2,1)}, u32[]{:S(2)}, u32[]{:S(2)}) collective-permute-start(bf16[400,768]{1,0:T(8,128)(2,1)} %collective-permute-done.far_ref), channel_id=1, source_target_pairs={{0,16},{32,48},{48,32},{64,80},{80,64},{96,112},{112,96},{128,144}... | collective-permute-start | bytes 1843208 | tf_op jit(solution)/shard_map/ppermute | solution.py:44
  40.7 1.0 collective-permute-done.5.first_ref.far_ref
  41.7 0.8 copy-done.3
  42.7 1.9 %shard_map.106 = bf16[400,768]{1,0:T(8,128)(2,1)} custom-call(s32[1]{0:T(128)} %bitcast.9.pick_ref, bf16[400,768]{1,0:T(8,128)(2,1)} %copy-done.3, bf16[400,768]{1,0:T(8,128)(2,1)} %copy-done.5, bf16[400,768]{1,0:T(8,128)(2,1)} %copy-done), custom_call_target="tpu_custom_call" | custom-call | bytes 3000000 | tf_op jit(solution)/shard_map/pallas_call | solution.py:77
  44.7 1.1 copy-done.1
  45.7 4.5 %shard_map.105.before_ref = f32[384,768]{1,0:T(8,128)S(1)} custom-call(f32[8]{0:T(128)S(1)} %stack.100.scalar_ref, bf16[400,768]{1,0:T(8,128)(2,1)S(1)} %copy-done.1, bf16[384,128]{1,0:T(8,128)(2,1)S(1)} %convolution_convert_fusion.1.rows_ref, bf16[400,768]{1,0:T(8,128)(2,1)} %shard_map.104.same_ref.own_ref, ...), custom_call_target="tpu_custom_call" | custom-call | flops 3960000000 | bytes 10800000 | tf_op jit(solution)/shard_map/pallas_call | solution.py:62
  50.2 1.3 %collective-permute-start.7 = (bf16[400,768]{1,0:T(8,128)(2,1)}, bf16[400,768]{1,0:T(8,128)(2,1)S(1)}, u32[]{:S(2)}, u32[]{:S(2)}) collective-permute-start(bf16[400,768]{1,0:T(8,128)(2,1)} %collective-permute-done.2.hop_ref), channel_id=1, source_target_pairs={{16,0},{144,128},{272,256},{400,384},{17,1},{145,129},{273,257},{4... | collective-permute-start | bytes 1843208 | tf_op jit(solution)/shard_map/ppermute | solution.py:44
  51.5 2.8 %collective-permute-done.7.corner_ref = bf16[400,768]{1,0:T(8,128)(2,1)S(1)} collective-permute-done((bf16[400,768]{1,0:T(8,128)(2,1)}, bf16[400,768]{1,0:T(8,128)(2,1)S(1)}, u32[]{:S(2)}, u32[]{:S(2)}) %collective-permute-start.7) | collective-permute-done | bytes 614432 | tf_op jit(solution)/shard_map/ppermute | solution.py:44
  54.4 3.7 %shard_map.107 = (bf16[384,768]{1,0:T(8,128)(2,1)S(1)}, bf16[384,384]{1,0:T(8,128)(2,1)S(1)}, bf16[384,384]{1,0:T(8,128)(2,1)S(1)}) custom-call(f32[8]{0:T(128)S(1)} %stack.100.scalar_ref, bf16[400,768]{1,0:T(8,128)(2,1)S(1)} %copy-done.1, bf16[384,128]{1,0:T(8,128)(2,1)S(1)} %convolution_convert_fusion.1.rows_ref, ...), custom_call_target="tpu_custom_call" | custom-call | flops 3300000000 | bytes 9000000 | tf_op jit(solution)/shard_map/pallas_call | solution.py:62
  58.1 3.0 %collective-permute-start.9 = (bf16[384,384]{1,0:T(8,128)(2,1)S(1)}, bf16[384,384]{1,0:T(8,128)(2,1)S(1)}, u32[]{:S(2)}, u32[]{:S(2)}) collective-permute-start(bf16[384,384]{1,0:T(8,128)(2,1)S(1)} %get-tuple-element.29), channel_id=1, source_target_pairs={{0,16},{16,0},{32,48},{48,32},{64,80},{80,64},{96,112},{112,96},{1... | collective-permute-start | bytes 884744 | tf_op jit(solution)/shard_map/ppermute | solution.py:44
  61.2 1.5 %shard_map.108 = bf16[384,768]{1,0:T(8,128)(2,1)} custom-call(bf16[384,768]{1,0:T(8,128)(2,1)S(1)} %get-tuple-element.30.dir_ref, bf16[768,768]{1,0:T(8,128)(2,1)S(1)} %copy-done.10), custom_call_target="tpu_custom_call" | custom-call | flops 1650000000 | bytes 4500000 | tf_op jit(solution)/shard_map/pallas_call | solution.py:62
  62.6 2.8 %shard_map.109 = bf16[4,2,96,384]{3,2,1,0:T(8,128)(2,1)} custom-call(bf16[384,384]{1,0:T(8,128)(2,1)S(1)} %get-tuple-element.33.keep_ref, bf16[384,384]{1,0:T(8,128)(2,1)S(1)} %collective-permute-done.9.got_ref, bf16[384,768]{1,0:T(8,128)(2,1)} %fusion.3.feat_ref, bf16[384,768]{1,0:T(8,128)(2,1)} %collective-permute-done.1.feat_near_ref), custom_call_target="tpu_custom_call" | custom-call | flops 1900000000 | bytes 5100000 | tf_op jit(solution)/shard_map/pallas_call | solution.py:229
  65.5 4.3 %all-to-all-start = ((bf16[8,96,384]{2,1,0:T(8,128)(2,1)}), bf16[8,96,384]{2,1,0:T(8,128)(2,1)S(1)}, u32[]{:S(2)}, u32[]{:S(2)}) async-start(bf16[8,96,384]{2,1,0:T(8,128)(2,1)} %bitcast.16), calls=%async_computation | async-start | bytes 1179648 | tf_op jit(solution)/shard_map/all_to_all | solution.py:52
  69.8 1.9 %collective-permute-start.11 = (bf16[400,768]{1,0:T(8,128)(2,1)S(1)}, bf16[400,768]{1,0:T(8,128)(2,1)}, u32[]{:S(2)}, u32[]{:S(2)}) collective-permute-start(bf16[400,768]{1,0:T(8,128)(2,1)S(1)} %copy-done.4), channel_id=1, source_target_pairs={{0,16},{16,0},{32,48},{48,32},{64,80},{80,64},{112,96},{128,144},{... | collective-permute-start | bytes 1843208 | tf_op jit(solution)/shard_map/ppermute | solution.py:44
  71.7 13.2 %collective-permute-start.10 = (bf16[400,768]{1,0:T(8,128)(2,1)}, bf16[400,768]{1,0:T(8,128)(2,1)}, u32[]{:S(2)}, u32[]{:S(2)}) collective-permute-start(bf16[400,768]{1,0:T(8,128)(2,1)} %shard_map.106), channel_id=1, source_target_pairs={{0,496},{32,16},{64,48},{80,464},{96,480},{128,112},{160,144},{192... | collective-permute-start | bytes 1843208 | tf_op jit(solution)/shard_map/ppermute | solution.py:44
  85.3 0.8 shard_map.110
  86.1 9.0 %all-to-all-start.1 = ((bf16[32,16,128]{2,1,0:T(8,128)(2,1)}), bf16[32,16,128]{2,1,0:T(8,128)(2,1)S(1)}, u32[]{:S(2)}, u32[]{:S(2)}) async-start(bf16[32,16,128]{2,1,0:T(8,128)(2,1)} %shard_map.110), calls=%async_computation.1 | async-start | bytes 262144 | tf_op jit(solution)/shard_map/all_to_all | solution.py:52
  95.1 4.3 %shard_map.111.before_ref = f32[384,768]{1,0:T(8,128)S(1)} custom-call(f32[8]{0:T(128)S(1)} %stack.113.scalar_ref, bf16[400,768]{1,0:T(8,128)(2,1)} %shard_map.104.same_ref.own_ref, bf16[384,128]{1,0:T(8,128)(2,1)S(1)} %convolution_convert_fusion.rows_ref, bf16[400,768]{1,0:T(8,128)(2,1)S(1)} %copy-done.2, bf16[400,768]{1,0:T(8,128)(2,1)S(1)} %copy-done.6, ...), custom_call_target="tpu_custom_call" | custom-call | flops 5500000256 | bytes 15000000 | tf_op jit(solution)/shard_map/pallas_call | solution.py:62
  99.4 0.8 collective-permute-done.10.late_ref
  100.3 2.5 %shard_map.112 = bf16[384,768]{1,0:T(8,128)(2,1)} custom-call(f32[8]{0:T(128)S(1)} %stack.113.scalar_ref, bf16[384,768]{1,0:T(8,128)(2,1)S(1)} %copy-done.13, bf16[384,128]{1,0:T(8,128)(2,1)S(1)} %convolution_convert_fusion.rows_ref, bf16[400,768]{1,0:T(8,128)(2,1)} %collective-permute-done.10.late_ref, f32[384,768]{1,0:T(8,128)S(1)} %shard_map.111.before_ref), custom_call_target="tpu_custom_call" | custom-call | flops 3300000000 | bytes 9000000 | tf_op jit(solution)/shard_map/pallas_call | solution.py:62
  102.8 4.8 %all-to-all-done.1.parts_ref = bf16[32,16,128]{2,1,0:T(8,128)(2,1)S(1)} async-done(((bf16[32,16,128]{2,1,0:T(8,128)(2,1)}), bf16[32,16,128]{2,1,0:T(8,128)(2,1)S(1)}, u32[]{:S(2)}, u32[]{:S(2)}) %all-to-all-start.1) | async-done | bytes 131104 | tf_op jit(solution)/shard_map/all_to_all | solution.py:52
  (49 shorter events, 4.0 us)
Async XLA Ops:
  0.6 0.7 copy-start.7
  1.3 1.1 copy-start.12
  2.4 6.4 %copy-start.11 = (bf16[384,768]{1,0:T(8,128)(2,1)S(1)}, bf16[384,768]{1,0:T(8,128)(2,1)}, u32[]{:S(2)}) copy-start(bf16[384,768]{1,0:T(8,128)(2,1)} %feat_ref.1) | copy-start | bytes 1769476
  3.4 26.1 %collective-permute-start = (bf16[400,768]{1,0:T(8,128)(2,1)}, bf16[400,768]{1,0:T(8,128)(2,1)}, u32[]{:S(2)}, u32[]{:S(2)}) collective-permute-start(bf16[400,768]{1,0:T(8,128)(2,1)} %shard_map.104.same_ref.own_ref), channel_id=1, source_target_pairs={{0,32},{16,48},{32,64},{48,80},{64,96},{80,112},{96,128},{112,16},... | collective-permute-start | bytes 1843208 | tf_op jit(solution)/shard_map/ppermute | solution.py:44
  6.8 24.8 %collective-permute-start.3 = (bf16[400,768]{1,0:T(8,128)(2,1)}, bf16[400,768]{1,0:T(8,128)(2,1)}, u32[]{:S(2)}, u32[]{:S(2)}) collective-permute-start(bf16[400,768]{1,0:T(8,128)(2,1)} %shard_map.104.same_ref.own_ref), channel_id=1, source_target_pairs={{0,16},{32,48},{64,80},{80,128},{96,112},{112,32},{128,144},{160,1... | collective-permute-start | bytes 1843208 | tf_op jit(solution)/shard_map/ppermute | solution.py:44
  8.8 3.7 %copy-start.8 = (s32[384]{0:T(512)S(1)}, s32[384]{0:T(512)}, u32[]{:S(2)}) copy-start(s32[384]{0:T(512)} %langs_ref.3) | copy-start | bytes 4612
  8.8 3.7 %copy-start.9 = (bf16[768,768]{1,0:T(8,128)(2,1)S(1)}, bf16[768,768]{1,0:T(8,128)(2,1)}, u32[]{:S(2)}) copy-start(bf16[768,768]{1,0:T(8,128)(2,1)} %head_ref.3) | copy-start | bytes 3538948
  10.4 13.7 %copy-start.15 = (s32[109]{0:T(128)S(1)}, s32[109]{0:T(128)}, u32[]{:S(2)}) copy-start(s32[109]{0:T(128)} %param.13) | copy-start | bytes 1312
  10.4 14.0 %collective-permute-start.1 = (bf16[384,768]{1,0:T(8,128)(2,1)}, bf16[384,768]{1,0:T(8,128)(2,1)}, u32[]{:S(2)}, u32[]{:S(2)}) collective-permute-start(bf16[384,768]{1,0:T(8,128)(2,1)} %fusion.3.feat_ref), channel_id=1, source_target_pairs={{0,16},{16,0},{32,48},{48,32},{64,80},{80,64},{96,112},{112,96},{1... | collective-permute-start | bytes 1769480 | tf_op jit(solution)/shard_map/ppermute | solution.py:44
  13.2 28.5 %copy-start = (bf16[400,768]{1,0:T(8,128)(2,1)}, bf16[400,768]{1,0:T(8,128)(2,1)S(1)}, u32[]{:S(2)}) copy-start(bf16[400,768]{1,0:T(8,128)(2,1)S(1)} %get-tuple-element.22.own_ref.third_ref.same_ref) | copy-start | bytes 1843204
  13.2 19.9 %copy-start.14 = (s32[109,109]{1,0:T(8,128)S(1)}, s32[109,109]{1,0:T(8,128)}, u32[]{:S(2)}) copy-start(s32[109,109]{1,0:T(8,128)} %param.12) | copy-start | bytes 142576
  13.2 28.5 %collective-permute-start.5 = (bf16[400,768]{1,0:T(8,128)(2,1)S(1)}, bf16[400,768]{1,0:T(8,128)(2,1)S(1)}, u32[]{:S(2)}, u32[]{:S(2)}) collective-permute-start(bf16[400,768]{1,0:T(8,128)(2,1)S(1)} %get-tuple-element.22.own_ref.third_ref.same_ref), channel_id=1, source_target_pairs={{0,96},{16,496},{32,0},{48,16},{64,32},{80,48},{96,64},{112,80},{1... | collective-permute-start | bytes 1843208 | tf_op jit(solution)/shard_map/ppermute | solution.py:44
  20.8 20.8 %collective-permute-start.6 = (bf16[400,768]{1,0:T(8,128)(2,1)S(1)}, bf16[400,768]{1,0:T(8,128)(2,1)S(1)}, u32[]{:S(2)}, u32[]{:S(2)}) collective-permute-start(bf16[400,768]{1,0:T(8,128)(2,1)S(1)} %get-tuple-element.22.own_ref.third_ref.same_ref), channel_id=1, source_target_pairs={{0,80},{16,0},{32,496},{48,32},{80,64},{112,96},{128,208},{144,128... | collective-permute-start | bytes 1843208 | tf_op jit(solution)/shard_map/ppermute | solution.py:44
  29.5 20.7 %collective-permute-start.2 = (bf16[400,768]{1,0:T(8,128)(2,1)}, bf16[400,768]{1,0:T(8,128)(2,1)}, u32[]{:S(2)}, u32[]{:S(2)}) collective-permute-start(bf16[400,768]{1,0:T(8,128)(2,1)} %collective-permute-done.far_ref), channel_id=1, source_target_pairs={{16,144},{48,64},{80,96},{144,272},{176,192},{208,224},{272,400},{... | collective-permute-start | bytes 1843208 | tf_op jit(solution)/shard_map/ppermute | solution.py:44
  31.6 18.6 %collective-permute-start.4 = (bf16[400,768]{1,0:T(8,128)(2,1)}, bf16[400,768]{1,0:T(8,128)(2,1)}, u32[]{:S(2)}, u32[]{:S(2)}) collective-permute-start(bf16[400,768]{1,0:T(8,128)(2,1)} %collective-permute-done.3.mix_ref), channel_id=1, source_target_pairs={{32,160},{160,288},{288,416},{416,32},{33,161},{161,289},{289,417}... | collective-permute-start | bytes 1843208 | tf_op jit(solution)/shard_map/ppermute | solution.py:44
  34.9 16.6 %collective-permute-start.8 = (bf16[400,768]{1,0:T(8,128)(2,1)}, bf16[400,768]{1,0:T(8,128)(2,1)}, u32[]{:S(2)}, u32[]{:S(2)}) collective-permute-start(bf16[400,768]{1,0:T(8,128)(2,1)} %collective-permute-done.far_ref), channel_id=1, source_target_pairs={{0,16},{32,48},{48,32},{64,80},{80,64},{96,112},{112,96},{128,144}... | collective-permute-start | bytes 1843208 | tf_op jit(solution)/shard_map/ppermute | solution.py:44
  41.7 0.9 copy-start.3
  41.7 1.1 copy-start.5
  44.7 1.1 copy-start.1
  50.2 4.1 %collective-permute-start.7 = (bf16[400,768]{1,0:T(8,128)(2,1)}, bf16[400,768]{1,0:T(8,128)(2,1)S(1)}, u32[]{:S(2)}, u32[]{:S(2)}) collective-permute-start(bf16[400,768]{1,0:T(8,128)(2,1)} %collective-permute-done.2.hop_ref), channel_id=1, source_target_pairs={{16,0},{144,128},{272,256},{400,384},{17,1},{145,129},{273,257},{4... | collective-permute-start | bytes 1843208 | tf_op jit(solution)/shard_map/ppermute | solution.py:44
  54.4 6.8 %copy-start.10 = (bf16[768,768]{1,0:T(8,128)(2,1)S(1)}, bf16[768,768]{1,0:T(8,128)(2,1)}, u32[]{:S(2)}) copy-start(bf16[768,768]{1,0:T(8,128)(2,1)} %head_ref.3) | copy-start | bytes 3538948
  58.1 4.5 %collective-permute-start.9 = (bf16[384,384]{1,0:T(8,128)(2,1)S(1)}, bf16[384,384]{1,0:T(8,128)(2,1)S(1)}, u32[]{:S(2)}, u32[]{:S(2)}) collective-permute-start(bf16[384,384]{1,0:T(8,128)(2,1)S(1)} %get-tuple-element.29), channel_id=1, source_target_pairs={{0,16},{16,0},{32,48},{48,32},{64,80},{80,64},{96,112},{112,96},{1... | collective-permute-start | bytes 884744 | tf_op jit(solution)/shard_map/ppermute | solution.py:44
  65.4 4.4 %copy-start.4 = (bf16[400,768]{1,0:T(8,128)(2,1)S(1)}, bf16[400,768]{1,0:T(8,128)(2,1)}, u32[]{:S(2)}) copy-start(bf16[400,768]{1,0:T(8,128)(2,1)} %copy-done.3) | copy-start | bytes 1843204
  65.5 19.8 %all-to-all-start = ((bf16[8,96,384]{2,1,0:T(8,128)(2,1)}), bf16[8,96,384]{2,1,0:T(8,128)(2,1)S(1)}, u32[]{:S(2)}, u32[]{:S(2)}) async-start(bf16[8,96,384]{2,1,0:T(8,128)(2,1)} %bitcast.16), calls=%async_computation | async-start | bytes 1179648 | tf_op jit(solution)/shard_map/all_to_all | solution.py:52
  69.8 25.3 %collective-permute-start.11 = (bf16[400,768]{1,0:T(8,128)(2,1)S(1)}, bf16[400,768]{1,0:T(8,128)(2,1)}, u32[]{:S(2)}, u32[]{:S(2)}) collective-permute-start(bf16[400,768]{1,0:T(8,128)(2,1)S(1)} %copy-done.4), channel_id=1, source_target_pairs={{0,16},{16,0},{32,48},{48,32},{64,80},{80,64},{112,96},{128,144},{... | collective-permute-start | bytes 1843208 | tf_op jit(solution)/shard_map/ppermute | solution.py:44
  71.7 28.5 %collective-permute-start.10 = (bf16[400,768]{1,0:T(8,128)(2,1)}, bf16[400,768]{1,0:T(8,128)(2,1)}, u32[]{:S(2)}, u32[]{:S(2)}) collective-permute-start(bf16[400,768]{1,0:T(8,128)(2,1)} %shard_map.106), channel_id=1, source_target_pairs={{0,496},{32,16},{64,48},{80,464},{96,480},{128,112},{160,144},{192... | collective-permute-start | bytes 1843208 | tf_op jit(solution)/shard_map/ppermute | solution.py:44
  85.1 10.0 %copy-start.2 = (bf16[400,768]{1,0:T(8,128)(2,1)S(1)}, bf16[400,768]{1,0:T(8,128)(2,1)}, u32[]{:S(2)}) copy-start(bf16[400,768]{1,0:T(8,128)(2,1)} %copy-done) | copy-start | bytes 1843204
  85.1 10.0 %copy-start.6 = (bf16[400,768]{1,0:T(8,128)(2,1)S(1)}, bf16[400,768]{1,0:T(8,128)(2,1)}, u32[]{:S(2)}) copy-start(bf16[400,768]{1,0:T(8,128)(2,1)} %copy-done.5) | copy-start | bytes 1843204
  86.1 21.5 %all-to-all-start.1 = ((bf16[32,16,128]{2,1,0:T(8,128)(2,1)}), bf16[32,16,128]{2,1,0:T(8,128)(2,1)S(1)}, u32[]{:S(2)}, u32[]{:S(2)}) async-start(bf16[32,16,128]{2,1,0:T(8,128)(2,1)} %shard_map.110), calls=%async_computation.1 | async-start | bytes 262144 | tf_op jit(solution)/shard_map/all_to_all | solution.py:52
  95.1 5.2 %copy-start.13 = (bf16[384,768]{1,0:T(8,128)(2,1)S(1)}, bf16[384,768]{1,0:T(8,128)(2,1)}, u32[]{:S(2)}) copy-start(bf16[384,768]{1,0:T(8,128)(2,1)} %text_ref.3) | copy-start | bytes 1769476
